TPU v7x, 32 devices: a whole 2x2x4 slice. The times are simulated.
32 devices in a mesh: rep: 4 (over x, core), dom: 4 (over z), tp: 2 (over y).
Axes of the slice: x: 2, y: 2, z: 4, core: 2. Of those that a mesh axis runs over, the one named last changes fastest.
Arguments:
- features: bfloat16 [8, 1024, 256], P('rep', ('dom', 'tp')), may hold values from -6 to 6
- radial: bfloat16 [8, 32, 1024], P('rep', None, ('dom', 'tp')), may hold values from 0.019897461 to 0.125
- neighbours: int32 [8, 32, 1024], P('rep', None, ('dom', 'tp')), may hold values from -1 to 191, as said below
- halo_lists: int32 [8, 2, 256], P('rep', None, ('dom', 'tp')), may hold values from 0 to 127, as said below
- slab_counts: int32 [8, 8], P('rep', ('dom', 'tp')), may hold values from 64 to 128, as said below
- frame_labels: int32 [8], P('rep'), may hold values from 0 to 1, as said below
- w_a: bfloat16 [2, 256, 256], replicated, may hold values from -0.375 to 0.375
- w_c: bfloat16 [2, 256, 256], replicated, may hold values from -0.375 to 0.375
- w_b: bfloat16 [2, 256, 256], replicated, may hold values from -0.375 to 0.375
- readout: float32 [256], replicated, may hold values from -0.375 to 0.375
Outputs:
- grad_wa: float32 [2, 256, 256], replicated
- grad_wc: float32 [2, 256, 256], replicated
- grad_wb: float32 [2, 256, 256], replicated
- grad_readout: float32 [256], replicated
- bead_energy: float32 [8, 1024], P('rep', ('dom', 'tp'))
Inputs may be any that keep to these rules, and one draw needn't show every extreme that they name: `neighbours`: an entry of a live bead names a live row of its own slab, or a halo row at 128 or above; empty slots are -1 and come after the filled ones; beads beyond the count have only empty slots. `halo_lists`: each entry names a live row of the sending slab. `slab_counts`: every frame has a full slab. `frame_labels`: exactly 4 frames carry each label.
All inputs are finite; a program needn't handle non-finite values.
Results may differ from a plain program's by a relative error of at most 0.008.
Values may be sent and summed in bfloat16 or wider, within the bound.
No kernel may reach another device: no remote copies, remote signals or barrier semaphores. Data moves between devices by JAX's collectives and lax.ppermute only.
A program may use at most 64 MiB of HBM per device.

v0:
```python
import math

import jax
import jax.numpy as jnp
from jax import lax
from jax.sharding import PartitionSpec as P


def shifted(value, axis, steps):
    count = lax.axis_size(axis)
    pairs = [(source, (source + steps) % count) for source in range(count)]
    return lax.ppermute(value, axis, pairs)


def slope_of(argument):
    sigmoid_value = jax.nn.sigmoid(argument)
    return sigmoid_value * (1.0 + argument * (1.0 - sigmoid_value))


def selector_of(indices, count):
    return (indices[..., None] == jnp.arange(count, dtype=jnp.int32)).astype(jnp.bfloat16)


def build_table(projected, send_select):
    down_rows = jnp.einsum(
        "fhs,fsc->fhc", send_select[:, 0], projected, preferred_element_type=jnp.float32
    ).astype(jnp.bfloat16)
    up_rows = jnp.einsum(
        "fhs,fsc->fhc", send_select[:, 1], projected, preferred_element_type=jnp.float32
    ).astype(jnp.bfloat16)
    from_lower = shifted(up_rows, ("dom", "tp"), 1)
    from_upper = shifted(down_rows, ("dom", "tp"), -1)
    return jnp.concatenate([projected, from_lower, from_upper], axis=1)


def local(
    features, radial, neighbours, halo_lists, slab_counts, frame_labels, w_a, w_c, w_b, readout
):
    frame_count, slab_rows, channels = features.shape
    hidden_cols = w_a.shape[2]
    halo_rows = halo_lists.shape[2]
    layer_total = w_a.shape[0]
    table_rows = slab_rows + 2 * halo_rows
    total_frames = frame_count * lax.axis_size("rep")
    norm_scale = 1.0 / math.sqrt(slab_rows * lax.axis_size(("dom", "tp")))
    edge_select = selector_of(neighbours, table_rows)
    send_select = selector_of(halo_lists, slab_rows)
    edge_weight = radial.astype(jnp.float32) * (neighbours >= 0).astype(jnp.float32)
    live_mask = (jnp.arange(slab_rows)[None, :] < slab_counts).astype(jnp.float32)
    frame_coef = (
        jnp.where(frame_labels == 0, 2.0 / total_frames, -2.0 / total_frames).astype(jnp.float32)
        * norm_scale
    )
    state_now = features
    saved = []
    for layer_num in range(layer_total):
        flat_rows = state_now.reshape(-1, channels)
        projected = (
            jnp.dot(flat_rows, w_a[layer_num], preferred_element_type=jnp.float32)
            .astype(jnp.bfloat16)
            .reshape(frame_count, slab_rows, hidden_cols)
        )
        crossed = jnp.dot(flat_rows, w_c[layer_num], preferred_element_type=jnp.float32).reshape(
            frame_count, slab_rows, hidden_cols
        )
        lookup_table = build_table(projected, send_select)
        picked = jnp.einsum(
            "fksr,frh->fksh", edge_select, lookup_table, preferred_element_type=jnp.float32
        )
        edge_sum = picked + crossed[:, None]
        gathered = jnp.sum(jax.nn.silu(edge_sum) * edge_weight[..., None], axis=1).astype(
            jnp.bfloat16
        )
        saved.append((state_now, edge_sum, gathered))
        update = jnp.dot(
            gathered.reshape(-1, hidden_cols), w_b[layer_num], preferred_element_type=jnp.float32
        )
        state_now = (state_now.astype(jnp.float32) + update.reshape(state_now.shape)).astype(
            jnp.bfloat16
        )
    final_state = state_now.astype(jnp.float32)
    activated = jax.nn.silu(final_state)
    bead_energy = live_mask * jnp.sum(activated * readout, axis=-1)
    grad_readout = jnp.sum((frame_coef[:, None] * live_mask)[..., None] * activated, axis=(0, 1))
    cotangent = (frame_coef[:, None] * live_mask)[..., None] * readout * slope_of(final_state)
    edge_select_wide = edge_select.astype(jnp.float32)
    send_select_wide = send_select.astype(jnp.float32)
    grads_a = [None] * layer_total
    grads_c = [None] * layer_total
    grads_b = [None] * layer_total
    for layer_num in reversed(range(layer_total)):
        state_in, edge_sum, gathered = saved[layer_num]
        cot_low = cotangent.astype(jnp.bfloat16).reshape(-1, channels)
        grads_b[layer_num] = jnp.dot(
            cot_low.T, gathered.reshape(-1, hidden_cols), preferred_element_type=jnp.float32
        )
        cot_gathered = jnp.dot(
            cot_low, w_b[layer_num].T, preferred_element_type=jnp.float32
        ).reshape(frame_count, slab_rows, hidden_cols)
        cot_edge = cot_gathered[:, None] * edge_weight[..., None] * slope_of(edge_sum)
        cot_cross = jnp.sum(cot_edge, axis=1)
        cot_table = jnp.einsum(
            "fksr,fksh->frh", edge_select_wide, cot_edge, precision=lax.Precision.HIGHEST
        )
        back_up = shifted(
            cot_table[:, slab_rows : slab_rows + halo_rows].astype(jnp.bfloat16), ("dom", "tp"), -1
        ).astype(jnp.float32)
        back_down = shifted(
            cot_table[:, slab_rows + halo_rows :].astype(jnp.bfloat16), ("dom", "tp"), 1
        ).astype(jnp.float32)
        cot_pre = cot_table[:, :slab_rows]
        cot_pre = cot_pre + jnp.einsum(
            "fhs,fhc->fsc", send_select_wide[:, 1], back_up, precision=lax.Precision.HIGHEST
        )
        cot_pre = cot_pre + jnp.einsum(
            "fhs,fhc->fsc", send_select_wide[:, 0], back_down, precision=lax.Precision.HIGHEST
        )
        pre_low = cot_pre.astype(jnp.bfloat16).reshape(-1, hidden_cols)
        cross_low = cot_cross.astype(jnp.bfloat16).reshape(-1, hidden_cols)
        flat_rows = state_in.reshape(-1, channels)
        grads_a[layer_num] = jnp.dot(flat_rows.T, pre_low, preferred_element_type=jnp.float32)
        grads_c[layer_num] = jnp.dot(flat_rows.T, cross_low, preferred_element_type=jnp.float32)
        if layer_num > 0:
            partial_value = jnp.dot(pre_low, w_a[layer_num].T, preferred_element_type=jnp.float32)
            partial_value = partial_value + jnp.dot(
                cross_low, w_c[layer_num].T, preferred_element_type=jnp.float32
            )
            cotangent = cotangent + partial_value.reshape(cotangent.shape)
    stacked = jnp.stack(grads_a + grads_c + grads_b)
    stacked, grad_readout = lax.psum((stacked, grad_readout), ("rep", "dom", "tp"))
    grad_wa = stacked[:layer_total]
    grad_wc = stacked[layer_total : 2 * layer_total]
    grad_wb = jnp.transpose(stacked[2 * layer_total :], (0, 2, 1))
    return (grad_wa, grad_wc, grad_wb, grad_readout, bead_energy)


def solution(mesh):
    placed = (
        P("rep", ("dom", "tp"), None),
        P("rep", None, ("dom", "tp")),
        P("rep", None, ("dom", "tp")),
        P("rep", None, ("dom", "tp")),
        P("rep", ("dom", "tp")),
        P("rep"),
        P(),
        P(),
        P(),
        P(),
    )
    return jax.shard_map(
        local,
        mesh=mesh,
        in_specs=placed,
        out_specs=(P(), P(), P(), P(), P("rep", ("dom", "tp"))),
        check_vma=False,
    )
```

profile of v0, /device:TPU:0, one launch (start us, length us, event | category | flops | bytes accessed | tf_op | source)
XLA Modules:
  0.0 215.7 jit_solution(14171810843981474578)
XLA Ops:
  8.0 1.1 convolution_convert_fusion.1
  9.3 3.0 %collective-permute-start = (bf16[2,32,256]{2,1,0:T(8,128)(2,1)S(1)}, bf16[2,32,256]{2,1,0:T(8,128)(2,1)S(1)}, u32[]{:S(2)}, u32[]{:S(2)}) collective-permute-start(bf16[2,32,256]{2,1,0:T(8,128)(2,1)S(1)} %convolution_convert_fusion.5), channel_id=1, source_target_pairs={{0,1},{1,2},{2,3},{3,4},{4,5},{5,6},{6,7},{7,0},{8,9},{9,10},{10,1... | collective-permute-start | bytes 98312 | tf_op jit(solution)/shard_map/ppermute | solution.py:12
  12.4 3.1 %collective-permute-start.1 = (bf16[2,32,256]{2,1,0:T(8,128)(2,1)S(1)}, bf16[2,32,256]{2,1,0:T(8,128)(2,1)S(1)}, u32[]{:S(2)}, u32[]{:S(2)}) collective-permute-start(bf16[2,32,256]{2,1,0:T(8,128)(2,1)S(1)} %convolution_convert_fusion.4), channel_id=1, source_target_pairs={{0,7},{1,0},{2,1},{3,2},{4,3},{5,4},{6,5},{7,6},{8,15},{9,8},{10,9... | collective-permute-start | bytes 98312 | tf_op jit(solution)/shard_map/ppermute | solution.py:12
  16.2 1.1 fusion.44
  17.4 0.8 convert_select_fusion
  18.1 0.7 fusion.67
  18.9 5.4 %multiply_reduce_fusion.1 = (bf16[2,128,256]{2,1,0:T(8,128)(2,1)S(1)}, f32[2,32,128,256]{3,2,1,0:T(8,128)S(1)}) fusion(f32[2,32,128]{2,1,0:T(8,128)S(1)} %convert_select_fusion, f32[2,128,256]{2,1,0:T(8,128)S(1)} %fusion.44, bf16[2,32,256]{2,1,0:T(8,128)(2,1)S(1)} %collective-permute-done.1, bf16[2,32,256]{2,1,0:T(8,128)(2,1)S(1)} %collective-permute-done, ...), kind=kOutput, calls=%fused_computation.4 | convolution fusion | flops 822083584 | bytes 9043968 | tf_op jit(solution)/shard_map/fksr,frh->fksh/dot_general | solution.py:67
  25.1 4.7 %collective-permute-start.3 = (bf16[2,32,256]{2,1,0:T(8,128)(2,1)S(1)}, bf16[2,32,256]{2,1,0:T(8,128)(2,1)S(1)}, u32[]{:S(2)}, u32[]{:S(2)}) collective-permute-start(bf16[2,32,256]{2,1,0:T(8,128)(2,1)S(1)} %convolution_convert_fusion.2), channel_id=1, source_target_pairs={{0,7},{1,0},{2,1},{3,2},{4,3},{5,4},{6,5},{7,6},{8,15},{9,8},{10,9... | collective-permute-start | bytes 98312 | tf_op jit(solution)/shard_map/ppermute | solution.py:12
  30.0 1.7 collective-permute-done.2
  31.7 4.7 %multiply_reduce_fusion = (bf16[2,128,256]{2,1,0:T(8,128)(2,1)S(1)}, f32[2,32,128,256]{3,2,1,0:T(8,128)S(1)}) fusion(f32[2,128,256]{2,1,0:T(8,128)S(1)} %fusion.35, f32[2,32,128]{2,1,0:T(8,128)S(1)} %convert_select_fusion, bf16[2,32,256]{2,1,0:T(8,128)(2,1)S(1)} %collective-permute-done.3, bf16[2,32,256]{2,1,0:T(8,128)(2,1)S(1)} %collective-permute-done.2, ...), kind=kOutput, calls=%fused_computation.2 | convolution fusion | flops 822083584 | bytes 9043968 | tf_op jit(solution)/shard_map/fksr,frh->fksh/dot_general | solution.py:67
  36.9 3.6 %fusion.72 = (bf16[2,128,256]{2,1,0:T(8,128)(2,1)S(1)}, f32[2,32,128,256]{3,2,1,0:T(8,128)S(1)}) fusion(f32[2,32,128,256]{3,2,1,0:T(8,128)S(1)} %get-tuple-element.32, f32[2,128,256]{2,1,0:T(8,128)S(1)} %fusion.35, f32[2,32,128]{2,1,0:T(8,128)S(1)} %convert_select_fusion, f32[2,128,256]{2,1,0:T(8,128)S(1)} %fusion.32), kind=kLoop, calls=%fused_computation.110 | loop fusion | flops 23003136 | bytes 17465344 | tf_op jit(solution)/shard_map/reduce_sum | solution.py:101
  40.5 4.4 %fusion.75 = (bf16[2,192,256]{2,1,0:T(8,128)(2,1)S(1)}, f32[2,192,256]{2,1,0:T(8,128)S(1)}) fusion(f32[2,32,128,256]{3,2,1,0:T(8,128)S(1)} %get-tuple-element.20, s32[2,32,128]{2,1,0:T(8,128)S(1)} %copy-done.5), kind=kOutput, calls=%fused_computation.113 | convolution fusion | flops 4833509376 | bytes 9011200 | tf_op jit(solution)/shard_map/fksr,fksh->frh/dot_general | solution.py:102
  45.0 5.0 %collective-permute-start.4 = (bf16[2,32,256]{2,1,0:T(8,128)(2,1)S(1)}, bf16[2,32,256]{2,1,0:T(8,128)(2,1)S(1)}, u32[]{:S(2)}, u32[]{:S(2)}) collective-permute-start(bf16[2,32,256]{2,1,0:T(8,128)(2,1)S(1)} %get-tuple-element.27), channel_id=1, source_target_pairs={{0,7},{1,0},{2,1},{3,2},{4,3},{5,4},{6,5},{7,6},{8,15},{9,8},{10,9... | collective-permute-start | bytes 98312 | tf_op jit(solution)/shard_map/ppermute | solution.py:12
  49.9 1.6 collective-permute-done.5
  53.0 3.5 %fusion.71 = (bf16[2,128,256]{2,1,0:T(8,128)(2,1)S(1)}, f32[2,32,128,256]{3,2,1,0:T(8,128)S(1)}) fusion(f32[2,32,128,256]{3,2,1,0:T(8,128)S(1)} %get-tuple-element.30, f32[2,128,256]{2,1,0:T(8,128)S(1)} %fusion.44, f32[2,32,128]{2,1,0:T(8,128)S(1)} %convert_select_fusion, f32[2,128,256]{2,1,0:T(8,128)S(1)} %fusion.41), kind=kLoop, calls=%fused_computation.109 | loop fusion | flops 23003136 | bytes 17465344 | tf_op jit(solution)/shard_map/reduce_sum | solution.py:101
  56.5 4.4 %fusion.76 = (bf16[2,192,256]{2,1,0:T(8,128)(2,1)S(1)}, f32[2,192,256]{2,1,0:T(8,128)S(1)}) fusion(f32[2,32,128,256]{3,2,1,0:T(8,128)S(1)} %get-tuple-element.18, s32[2,32,128]{2,1,0:T(8,128)S(1)} %copy-done.5), kind=kOutput, calls=%fused_computation.114 | convolution fusion | flops 4833509376 | bytes 9011200 | tf_op jit(solution)/shard_map/fksr,fksh->frh/dot_general | solution.py:102
  61.1 4.8 %collective-permute-start.6 = (bf16[2,32,256]{2,1,0:T(8,128)(2,1)S(1)}, bf16[2,32,256]{2,1,0:T(8,128)(2,1)S(1)}, u32[]{:S(2)}, u32[]{:S(2)}) collective-permute-start(bf16[2,32,256]{2,1,0:T(8,128)(2,1)S(1)} %get-tuple-element.25), channel_id=1, source_target_pairs={{0,7},{1,0},{2,1},{3,2},{4,3},{5,4},{6,5},{7,6},{8,15},{9,8},{10,9... | collective-permute-start | bytes 98312 | tf_op jit(solution)/shard_map/ppermute | solution.py:12
  65.8 1.8 collective-permute-done.7
  69.6 1.1 copy-done.1
  70.7 40.2 %psum.15 = f32[256]{0:T(256)} all-reduce(f32[256]{0:T(256)S(1)} %get-tuple-element.16), channel_id=1, replica_groups=mesh['rep'=4,'dom'=4,'tp'=2] {'rep','dom','tp'}, use_global_device_ids=true, to_apply=%region_6.7 | all-reduce | flops 256 | bytes 2048 | tf_op jit(solution)/shard_map/psum | solution.py:130
  111.6 92.9 %all-reduce.2.cloned.1.call-done = f32[6,256,256]{1,2,0:T(8,128)} async-done(((f32[6,256,256]{1,2,0:T(8,128)}), f32[6,256,256]{1,2,0:T(8,128)}) %all-reduce.2.cloned.1.call-update) | async-done | bytes 1572880 | tf_op jit(solution)/shard_map/psum | solution.py:130
  204.5 2.3 %slice_bitcast_fusion = (f32[2,256,256]{2,1,0:T(8,128)}, f32[2,256,256]{1,2,0:T(8,128)S(1)}, f32[2,256,256]{1,2,0:T(8,128)S(1)}) fusion(f32[6,256,256]{1,2,0:T(8,128)} %all-reduce.2.cloned.1.call-done), kind=kLoop, calls=%fused_computation.47 | loop fusion | bytes 3145728 | tf_op jit(solution)/shard_map/transpose | solution.py:133
  206.8 1.0 copy.39
  207.8 1.0 copy.38
  (54 shorter events, 7.1 us)
Async XLA Ops:
  7.2 197.4 %all-reduce.2.cloned.1.call-start = ((), (), s32[]{:S(2)}) async-start(), calls=%async_computation | async-start | bytes 3145728 | tf_op jit(solution)/shard_map/psum | solution.py:130
  9.3 9.6 %collective-permute-start = (bf16[2,32,256]{2,1,0:T(8,128)(2,1)S(1)}, bf16[2,32,256]{2,1,0:T(8,128)(2,1)S(1)}, u32[]{:S(2)}, u32[]{:S(2)}) collective-permute-start(bf16[2,32,256]{2,1,0:T(8,128)(2,1)S(1)} %convolution_convert_fusion.5), channel_id=1, source_target_pairs={{0,1},{1,2},{2,3},{3,4},{4,5},{5,6},{6,7},{7,0},{8,9},{9,10},{10,1... | collective-permute-start | bytes 98312 | tf_op jit(solution)/shard_map/ppermute | solution.py:12
  12.4 6.5 %collective-permute-start.1 = (bf16[2,32,256]{2,1,0:T(8,128)(2,1)S(1)}, bf16[2,32,256]{2,1,0:T(8,128)(2,1)S(1)}, u32[]{:S(2)}, u32[]{:S(2)}) collective-permute-start(bf16[2,32,256]{2,1,0:T(8,128)(2,1)S(1)} %convolution_convert_fusion.4), channel_id=1, source_target_pairs={{0,7},{1,0},{2,1},{3,2},{4,3},{5,4},{6,5},{7,6},{8,15},{9,8},{10,9... | collective-permute-start | bytes 98312 | tf_op jit(solution)/shard_map/ppermute | solution.py:12
  18.9 5.5 %copy-start = (bf16[2,128,256]{2,1,0:T(8,128)(2,1)S(1)}, bf16[2,128,256]{2,1,0:T(8,128)(2,1)}, u32[]{:S(2)}) copy-start(bf16[2,128,256]{2,1,0:T(8,128)(2,1)} %param.10) | copy-start | bytes 393220
  18.9 5.5 %copy-start.3 = (bf16[2,256,256]{2,1,0:T(8,128)(2,1)S(1)}, bf16[2,256,256]{2,1,0:T(8,128)(2,1)}, u32[]{:S(2)}) copy-start(bf16[2,256,256]{2,1,0:T(8,128)(2,1)} %param.18) | copy-start | bytes 786436
  18.9 5.7 %copy-start.2 = (bf16[2,256,256]{2,1,0:T(8,128)(2,1)S(1)}, bf16[2,256,256]{2,1,0:T(8,128)(2,1)}, u32[]{:S(2)}) copy-start(bf16[2,256,256]{2,1,0:T(8,128)(2,1)} %param.16) | copy-start | bytes 786436
  18.9 10.9 %copy-start.4 = (bf16[2,256,256]{2,1,0:T(8,128)(2,1)S(1)}, bf16[2,256,256]{2,1,0:T(8,128)(2,1)}, u32[]{:S(2)}) copy-start(bf16[2,256,256]{2,1,0:T(8,128)(2,1)} %param.17) | copy-start | bytes 786436
  18.9 12.8 %copy-start.5 = (s32[2,32,128]{2,1,0:T(8,128)S(1)}, s32[2,32,128]{2,1,0:T(8,128)}, u32[]{:S(2)}) copy-start(s32[2,32,128]{2,1,0:T(8,128)} %param.12) | copy-start | bytes 98308
  25.0 6.7 %collective-permute-start.2 = (bf16[2,32,256]{2,1,0:T(8,128)(2,1)S(1)}, bf16[2,32,256]{2,1,0:T(8,128)(2,1)S(1)}, u32[]{:S(2)}, u32[]{:S(2)}) collective-permute-start(bf16[2,32,256]{2,1,0:T(8,128)(2,1)S(1)} %convolution_convert_fusion.3), channel_id=1, source_target_pairs={{0,1},{1,2},{2,3},{3,4},{4,5},{5,6},{6,7},{7,0},{8,9},{9,10},{10,1... | collective-permute-start | bytes 98312 | tf_op jit(solution)/shard_map/ppermute | solution.py:12
  25.1 6.6 %collective-permute-start.3 = (bf16[2,32,256]{2,1,0:T(8,128)(2,1)S(1)}, bf16[2,32,256]{2,1,0:T(8,128)(2,1)S(1)}, u32[]{:S(2)}, u32[]{:S(2)}) collective-permute-start(bf16[2,32,256]{2,1,0:T(8,128)(2,1)S(1)} %convolution_convert_fusion.2), channel_id=1, source_target_pairs={{0,7},{1,0},{2,1},{3,2},{4,3},{5,4},{6,5},{7,6},{8,15},{9,8},{10,9... | collective-permute-start | bytes 98312 | tf_op jit(solution)/shard_map/ppermute | solution.py:12
  30.0 6.7 %copy-start.7 = (f32[256]{0:T(256)S(1)}, f32[256]{0:T(256)}, u32[]{:S(2)}) copy-start(f32[256]{0:T(256)} %param.19) | copy-start | bytes 3076
  44.9 6.7 %collective-permute-start.5 = (bf16[2,32,256]{2,1,0:T(8,128)(2,1)S(1)}, bf16[2,32,256]{2,1,0:T(8,128)(2,1)S(1)}, u32[]{:S(2)}, u32[]{:S(2)}) collective-permute-start(bf16[2,32,256]{2,1,0:T(8,128)(2,1)S(1)} %get-tuple-element.28), channel_id=1, source_target_pairs={{0,1},{1,2},{2,3},{3,4},{4,5},{5,6},{6,7},{7,0},{8,9},{9,10},{10,1... | collective-permute-start | bytes 98312 | tf_op jit(solution)/shard_map/ppermute | solution.py:12
  45.0 6.8 %collective-permute-start.4 = (bf16[2,32,256]{2,1,0:T(8,128)(2,1)S(1)}, bf16[2,32,256]{2,1,0:T(8,128)(2,1)S(1)}, u32[]{:S(2)}, u32[]{:S(2)}) collective-permute-start(bf16[2,32,256]{2,1,0:T(8,128)(2,1)S(1)} %get-tuple-element.27), channel_id=1, source_target_pairs={{0,7},{1,0},{2,1},{3,2},{4,3},{5,4},{6,5},{7,6},{8,15},{9,8},{10,9... | collective-permute-start | bytes 98312 | tf_op jit(solution)/shard_map/ppermute | solution.py:12
  56.5 54.4 %copy-start.6 = (s32[2,1]{0,1:T(1,128)S(1)}, s32[2,1]{0,1:T(1,128)}, u32[]{:S(2)}) copy-start(s32[2,1]{0,1:T(1,128)} %param.14) | copy-start | bytes 28
  61.0 6.7 %collective-permute-start.7 = (bf16[2,32,256]{2,1,0:T(8,128)(2,1)S(1)}, bf16[2,32,256]{2,1,0:T(8,128)(2,1)S(1)}, u32[]{:S(2)}, u32[]{:S(2)}) collective-permute-start(bf16[2,32,256]{2,1,0:T(8,128)(2,1)S(1)} %get-tuple-element.26), channel_id=1, source_target_pairs={{0,1},{1,2},{2,3},{3,4},{4,5},{5,6},{6,7},{7,0},{8,9},{9,10},{10,1... | collective-permute-start | bytes 98312 | tf_op jit(solution)/shard_map/ppermute | solution.py:12
  61.1 6.8 %collective-permute-start.6 = (bf16[2,32,256]{2,1,0:T(8,128)(2,1)S(1)}, bf16[2,32,256]{2,1,0:T(8,128)(2,1)S(1)}, u32[]{:S(2)}, u32[]{:S(2)}) collective-permute-start(bf16[2,32,256]{2,1,0:T(8,128)(2,1)S(1)} %get-tuple-element.25), channel_id=1, source_target_pairs={{0,7},{1,0},{2,1},{3,2},{4,3},{5,4},{6,5},{7,6},{8,15},{9,8},{10,9... | collective-permute-start | bytes 98312 | tf_op jit(solution)/shard_map/ppermute | solution.py:12
  69.6 1.1 copy-start.1
Sparse Core Ops, SparseCore 0:
  70.9 133.6 all-reduce.1
where the time goes:
time: 216 us
  waiting for transfers between devices  98.1 us (45%)
  blocking collectives  40.2 us (19%)
  matrix products  25.8 us (12%)
  starting transfers between devices  20.8 us (10%)
  between operations  14.4 us (7%)
  other arithmetic  10.2 us (5%)
  local copies, waits for them, and re-layouts  6.14 us (3%)
    psum x1, waiting for transfers between devices, local(): lax.psum((stacked, grad_readout), ('rep', 'dom', 'tp'))  92.9 us
    psum x1, blocking collectives, local(): lax.psum((stacked, grad_readout), ('rep', 'dom', 'tp'))  40.2 us
    ppermute x8, starting transfers between devices, shifted(): return lax.ppermute(value, axis, pairs)  20.7 us
    dot_general x2, matrix products, local(): jnp.einsum('fksr,frh->fksh', edge_select, lookup_table, preferred_element...  10.2 us
    dot_general x2, matrix products, local(): jnp.einsum('fksr,fksh->frh', edge_select_wide, cot_edge, precision=lax.Pr...  8.85 us
    reduce_sum x2, other arithmetic, local(): cot_cross = jnp.sum(cot_edge, axis=1)  7.1 us
    ppermute x8, waiting for transfers between devices, shifted(): return lax.ppermute(value, axis, pairs)  5.18 us
  transfers between devices with their start and end apart: 9, of which 4 were waited for; matrix products, arithmetic and copies ran while one was open for 2% of the time, Pallas kernels for 0%

commit v1 on v0

v1 whole, which is shorter than its diff:
```python
import functools
import math

import jax
import jax.numpy as jnp
from jax import lax
from jax.experimental import pallas as pl
from jax.experimental.pallas import tpu as pltpu
from jax.sharding import PartitionSpec as P

BF16, F32 = jnp.bfloat16, jnp.float32
MEBI = 1024 * 1024
SUB = 16
RING = ("dom", "tp")
EVERY = ("rep", "dom", "tp")


def mul(a, b):
    return jnp.dot(a, b, preferred_element_type=F32)


def mul_nt(a, b):
    return lax.dot_general(a, b, (((1,), (1,)), ((), ())), preferred_element_type=F32)


def mul_tn(a, b):
    return lax.dot_general(a, b, (((0,), (0,)), ((), ())), preferred_element_type=F32)


def packed_halves(both):
    rows, lanes = both.shape[0] // 2, both.shape[1] // 2
    low, high = both[:rows], both[rows:]
    first = jnp.concatenate([low[:, :lanes], high[:, :lanes]], axis=1)
    second = jnp.concatenate([low[:, lanes:], high[:, lanes:]], axis=1)
    return first, second


def unpacked_halves(first, second):
    lanes = first.shape[1] // 2
    low = jnp.concatenate([first[:, :lanes], second[:, :lanes]], axis=1)
    high = jnp.concatenate([first[:, lanes:], second[:, lanes:]], axis=1)
    return jnp.concatenate([low, high], axis=0)


def send_lanes(even, list_ref, beads):
    parts = []
    for side in range(2):
        for frame in range(list_ref.shape[0]):
            down, up = list_ref[frame, 0:1, :], list_ref[frame, 1:2, :]
            parts.append((jnp.where(even, down, up) if side else jnp.where(even, up, down)) + frame * beads)
    return jnp.concatenate(parts, axis=1)


def write_halo(first_ref, second_ref, both):
    first, second = packed_halves(both)
    first_ref[...] = first.astype(BF16)
    second_ref[...] = second.astype(BF16)


def read_halo(first_ref, second_ref):
    return unpacked_halves(first_ref[...].astype(F32), second_ref[...].astype(F32)).astype(BF16)


def copies_of(pairs, sems):
    copies = [pltpu.make_async_copy(source, target, sems.at[n]) for n, (source, target) in enumerate(pairs)]
    for copy in copies:
        copy.start()
    return copies


def select_kernel(
    where_ref, feat_hbm, list_hbm, state_ref, select_ref, first_ref, second_ref, feat_ref, list_ref, sems
):
    list_copy, feat_copy = copies_of([(list_hbm, list_ref), (feat_hbm, feat_ref)], sems)
    list_copy.wait()
    frames, beads, channels = feat_ref.shape
    lanes = frames * beads
    sent = send_lanes(where_ref[1] == 0, list_ref, beads)
    row = lax.broadcasted_iota(jnp.int32, (lanes, sent.shape[1]), 0)
    select = jnp.where(row == sent, 1.0, 0.0).astype(BF16)
    feat_copy.wait()
    state = feat_ref[...].reshape(lanes, channels).astype(F32).T.astype(BF16)
    write_halo(first_ref, second_ref, mul(state, select))
    state_ref[...] = state
    select_ref[...] = select


def write_onehot(onehot_ref, slots_ref):
    frames, degree, beads = slots_ref.shape
    row = lax.broadcasted_iota(jnp.int32, (onehot_ref.shape[1], beads), 0)
    for frame in range(frames):
        for slot in range(degree):
            hit = row == slots_ref[frame, slot : slot + 1, :]
            onehot_ref[frame, :, slot * beads : (slot + 1) * beads] = jnp.where(hit, 1.0, 0.0).astype(BF16)


def prepare_kernel(
    halo, where_ref, count_ref, label_ref, neigh_hbm, radial_hbm, wa_hbm, wc_hbm, wb_hbm, readout_hbm, state_ref,
    onehot_ref, edge_ref, wa_ref, wc_ref, wb_ref, wta_ref, wtc_ref, wtb_ref, own_ref, cross_ref, live_ref, sign_ref, wide_ref,
    neigh_ref, radial_ref, readout_ref, slots_ref, sems,
):
    frames, degree, beads = neigh_ref.shape
    pairs = [(neigh_hbm, neigh_ref), (radial_hbm, radial_ref), (wa_hbm, wa_ref), (wc_hbm, wc_ref), (wb_hbm, wb_ref)]
    pairs.append((readout_hbm, readout_ref))
    copies = copies_of(pairs, sems)
    copies[0].wait()
    copies[1].wait()
    odd = where_ref[1] != 0
    bead = lax.broadcasted_iota(jnp.int32, (1, beads), 1)
    for frame in range(frames):
        live = jnp.where(bead < count_ref[frame, 0], 1.0, 0.0)
        lanes = slice(frame * beads, (frame + 1) * beads)
        live_ref[:, lanes] = live
        sign_ref[:, lanes] = jnp.where(label_ref[frame] == 0, live, -live)
        neigh = neigh_ref[frame]
        weight = jnp.where(neigh >= 0, radial_ref[frame].astype(F32), 0.0)
        entry = neigh - beads
        upper = entry >= halo
        entry = jnp.where(upper, entry - halo, entry) + (beads + frame * halo)
        upper = jnp.where(upper, 1, 0)
        side = jnp.where(odd, upper, 1 - upper)
        slots_ref[frame] = jnp.where(neigh < beads, neigh, entry + side * (frames * halo))
        for slot in range(degree):
            edge_ref[frame, slot] = jnp.broadcast_to(weight[slot : slot + 1, :], (SUB, beads)).astype(BF16)
    write_onehot(onehot_ref, slots_ref)
    for copy in copies[2:]:
        copy.wait()
    for layer in range(wa_ref.shape[0]):
        wta_ref[layer] = wa_ref[layer].astype(F32).T.astype(BF16)
        wtc_ref[layer] = wc_ref[layer].astype(F32).T.astype(BF16)
        wtb_ref[layer] = wb_ref[layer].astype(F32).T.astype(BF16)
    own_ref[...] = mul(wta_ref[0], state_ref[...]).astype(BF16)
    cross_ref[...] = mul(wtc_ref[0], state_ref[...])
    wide = readout_ref[...].reshape(1, -1)
    wide_ref[...] = jnp.broadcast_to(wide, (wide_ref.shape[1], wide.shape[1])).T


def edges(onehot_ref, edge_ref, own, halo, cross, slope_ref, total_ref, slope_total_ref, group=4):
    frames, degree, _, beads = edge_ref.shape
    hidden = own.shape[0]
    blocks = hidden // SUB
    for frame in range(frames):
        lanes = slice(frame * beads, (frame + 1) * beads)
        table = jnp.concatenate([own[:, lanes], halo], axis=1) * jnp.asarray(0.5, BF16)
        half_cross = cross[:, lanes] * 0.5
        wide_cross = jnp.concatenate([half_cross] * group, axis=1)
        total_ref[:, lanes] = jnp.zeros((hidden, beads), F32)
        slope_total_ref[:, lanes] = jnp.zeros((hidden, beads), F32)

        def step(index, carry):
            at = slice(index * group * beads, (index + 1) * group * beads)
            half = (mul(table, onehot_ref[frame, :, at]) + wide_cross).astype(BF16)
            turn = jnp.tanh(half)
            act = half + half * turn
            slope = (1 + turn) + half * (1 - turn * turn)
            act_sum, slope_sum = None, None
            kept = []
            for part in range(group):
                here = slice(part * beads, (part + 1) * beads)
                weight = edge_ref[frame, index * group + part]
                a = (act[:, here].reshape(blocks, SUB, beads) * weight[None]).reshape(hidden, beads)
                s = (slope[:, here].reshape(blocks, SUB, beads) * (weight * jnp.asarray(0.5, BF16))[None]).reshape(hidden, beads)
                kept.append(s)
                act_sum = a if act_sum is None else act_sum + a
                slope_sum = s if slope_sum is None else slope_sum + s
            slope_ref[frame, :, at] = jnp.concatenate(kept, axis=1)
            total_ref[:, lanes] += act_sum.astype(F32)
            slope_total_ref[:, lanes] += slope_sum.astype(F32)
            return carry

        for index in range(degree // group):
            step(index, 0)


def scatter(onehot_ref, slope_ref, cot_gathered, frame, beads, group=8):
    count = slope_ref.shape[2] // beads
    lanes = slice(frame * beads, (frame + 1) * beads)
    wide = jnp.concatenate([cot_gathered[:, lanes]] * group, axis=1)
    total = None
    for index in range(count // group):
        at = slice(index * group * beads, (index + 1) * group * beads)
        part = mul_nt(slope_ref[frame, :, at] * wide, onehot_ref[frame, :, at])
        total = part if total is None else total + part
    return total


def first_kernel(
    hf_ref, hs_ref, onehot_ref, edge_ref, wta_ref, wtb_ref, own_ref, cross_ref, state_ref, select_ref,
    next_ref, first_ref, second_ref, halo_ref, gathered_ref, slope_ref, slope_total_ref,
    total_ref,
):
    halo = read_halo(hf_ref, hs_ref)
    halo_ref[...] = halo
    halo_rows = mul(wta_ref[0], halo).astype(BF16)
    edges(onehot_ref, edge_ref, own_ref[...], halo_rows, cross_ref[...], slope_ref, total_ref, slope_total_ref)
    gathered = total_ref[...].astype(BF16)
    gathered_ref[...] = gathered
    state = (state_ref[...].astype(F32) + mul(wtb_ref[0], gathered)).astype(BF16)
    next_ref[...] = state
    write_halo(first_ref, second_ref, mul(state, select_ref[...]))


def middle_kernel(
    scale,
    hf_ref, hs_ref, onehot_ref, edge_ref, wta_ref, wtc_ref, wtb_ref, wb_ref, state_ref, live_ref, sign_ref, readout_ref,
    energy_ref, grad_readout_ref, cot_ref, first_ref, second_ref, cot_own_ref, cot_halo_ref, cot_cross_ref,
    halo_ref, gathered_ref, cot_low_ref,
    slope_ref, slope_total_ref, total_ref,
):
    last = wta_ref.shape[0] - 1
    beads = edge_ref.shape[3]
    frames = edge_ref.shape[0]
    halo = read_halo(hf_ref, hs_ref)
    halo_ref[...] = halo
    state = state_ref[...]
    own = mul(wta_ref[last], state).astype(BF16)
    cross = mul(wtc_ref[last], state)
    halo_rows = mul(wta_ref[last], halo).astype(BF16)
    edges(onehot_ref, edge_ref, own, halo_rows, cross, slope_ref, total_ref, slope_total_ref)
    gathered = total_ref[...].astype(BF16)
    gathered_ref[...] = gathered
    final = (state.astype(F32) + mul(wtb_ref[last], gathered)).astype(BF16).astype(F32)
    sigmoid = jax.nn.sigmoid(final)
    activated = final * sigmoid
    readout = jnp.concatenate([readout_ref[...]] * frames, axis=1)
    live = live_ref[...]
    sign = sign_ref[...]
    energy = live * jnp.sum(activated * readout, axis=0, keepdims=True)
    for frame in range(frames):
        energy_ref[frame : frame + 1, :] = energy[:, frame * beads : (frame + 1) * beads]
    signs = jnp.broadcast_to(sign, (SUB, sign.shape[1])).astype(BF16)
    grad_readout_ref[...] = mul_nt(signs, activated.astype(BF16)) * scale
    cot = (sign * scale) * readout * (sigmoid * (1.0 + final * (1.0 - sigmoid)))
    cot_ref[...] = cot
    cot_low = cot.astype(BF16)
    cot_low_ref[...] = cot_low
    cot_gathered = mul(wb_ref[last], cot_low)
    cot_cross_ref[...] = (cot_gathered * slope_total_ref[...]).astype(BF16)
    cot_gathered = cot_gathered.astype(BF16)
    cot_halo = None
    for frame in range(frames):
        part = scatter(onehot_ref, slope_ref, cot_gathered, frame, beads)
        cot_own_ref[:, frame * beads : (frame + 1) * beads] = part[:, :beads]
        cot_halo = part[:, beads:] if cot_halo is None else cot_halo + part[:, beads:]
    write_halo(first_ref, second_ref, cot_halo)
    cot_halo_ref[...] = cot_halo.astype(BF16)


def put_slots(slots_ref, me, grads, base=0):
    slots = slots_ref.shape[0]
    rows = grads[0].shape[0] // slots
    for chunk in range(slots):
        slot = jnp.bitwise_xor(me, chunk)
        for number, grad in enumerate(grads):
            slots_ref[slot, base + number * rows : base + (number + 1) * rows, :] = grad[chunk * rows : (chunk + 1) * rows]


def upper_grads_kernel(
    me_ref, state_ref, halo_ref, gathered_ref, cot_low_ref, cot_own_ref, cot_halo_ref, cot_cross_ref, grad_readout_ref, slots_ref
):
    me = me_ref[0]
    state = state_ref[...]
    grad_a = mul_nt(state, cot_own_ref[...].astype(BF16)) + mul_nt(halo_ref[...], cot_halo_ref[...])
    grad_c = mul_nt(state, cot_cross_ref[...])
    grad_b = mul_nt(gathered_ref[...], cot_low_ref[...])
    put_slots(slots_ref, me, [grad_a, grad_c, grad_b], SUB)
    row = lax.broadcasted_iota(jnp.int32, (SUB, slots_ref.shape[2]), 0)
    only = jnp.where(row == 0, grad_readout_ref[...], 0.0)
    for slot in range(slots_ref.shape[0]):
        slots_ref[slot, :SUB, :] = only


def lower_kernel(
    me_ref, bf_ref, bs_ref, select_ref, cot_own_ref, cot_cross_ref, cot_ref, wa_ref, wc_ref, wb_ref,
    onehot_ref, slope_ref, slope_total_ref, state_ref, halo_ref, gathered_ref,
    slots_ref,
):
    me = me_ref[0]
    frames = onehot_ref.shape[0]
    beads = cot_ref.shape[1] // frames
    back = read_halo(bf_ref, bs_ref)
    cot_own = (cot_own_ref[...] + mul_nt(back, select_ref[...])).astype(BF16)
    cot = cot_ref[...] + mul(wa_ref[1], cot_own) + mul(wc_ref[1], cot_cross_ref[...])
    cot_low = cot.astype(BF16)
    state = state_ref[...]
    grad_b = mul_nt(gathered_ref[...], cot_low)
    cot_gathered = mul(wb_ref[0], cot_low)
    grad_c = mul_nt(state, (cot_gathered * slope_total_ref[...]).astype(BF16))
    cot_gathered = cot_gathered.astype(BF16)
    cot_halo, grad_a = None, None
    for frame in range(frames):
        lanes = slice(frame * beads, (frame + 1) * beads)
        part = scatter(onehot_ref, slope_ref, cot_gathered, frame, beads)
        here = mul_nt(state[:, lanes], part[:, :beads].astype(BF16))
        grad_a = here if grad_a is None else grad_a + here
        cot_halo = part[:, beads:] if cot_halo is None else cot_halo + part[:, beads:]
    grad_a = grad_a + mul_nt(halo_ref[...], cot_halo.astype(BF16))
    put_slots(slots_ref, me, [grad_a, grad_c, grad_b])


def finish_kernel(me_ref, *refs):
    near, far = refs[:4], refs[4]
    wa_ref, wc_ref, wb_ref, readout_ref = refs[5:]
    me = me_ref[0]
    rows = (far.shape[1] - SUB) // 6
    for slot in range(8):
        source = near[slot] if slot < 4 else far.at[slot - 4]
        chunk = jnp.bitwise_xor(me, slot)
        place = pl.ds(pl.multiple_of(chunk * rows, rows), rows)
        for layer, base in ((1, SUB), (0, SUB + 3 * rows)):
            for number, ref in enumerate((wa_ref, wc_ref, wb_ref)):
                ref[layer, place, :] = source[base + number * rows : base + (number + 1) * rows, :].astype(F32)
        if slot == 0:
            head = source[:SUB, :].astype(F32)
            readout_ref[...] = head[0] + head[1]


def kernel_call(body, outs, args, scratch=(), flops=0, smem=0, far=0, limit=24):
    spaces = [pltpu.SMEM] * smem + [pltpu.HBM] * far + [pltpu.VMEM] * (len(args) - smem - far)
    args = [pltpu.with_memory_space_constraint(a, pltpu.HBM) if s is pltpu.HBM else a for a, s in zip(args, spaces)]
    return pl.pallas_call(
        body,
        out_shape=outs,
        in_specs=[pl.BlockSpec(memory_space=space) for space in spaces],
        out_specs=jax.tree.map(
            lambda out: pl.BlockSpec(memory_space=pltpu.HBM if getattr(out, "memory_space", None) is pltpu.HBM else pltpu.VMEM), outs
        ),
        scratch_shapes=list(scratch),
        compiler_params=pltpu.CompilerParams(vmem_limit_bytes=limit * MEBI),
        cost_estimate=pl.CostEstimate(flops=flops, bytes_accessed=0, transcendentals=0),
    )(*args)


def near(shape, dtype=BF16):
    return pltpu.VMEM(shape, dtype)


def swapped(value, kind):
    count = lax.axis_size(RING)
    if kind == 0:
        pairs = [(s, s ^ 1) for s in range(count)]
    else:
        pairs = [(s, (s + 1) % count if s % 2 else (s - 1) % count) for s in range(count)]
    return lax.ppermute(value, RING, pairs)


def partner(value, axis, bits):
    return lax.ppermute(value, axis, [(s, s ^ bits) for s in range(lax.axis_size(axis))])


def summed(*terms):
    total = terms[0].astype(F32)
    for term in terms[1:]:
        total = total + term.astype(F32)
    whole = total[..., 0:1, :] + total[..., 1:2, :]
    upper = lax.reduce_precision(whole, 8, 7)
    row = lax.broadcasted_iota(jnp.int32, total.shape, total.ndim - 2)
    return jnp.where(row == 0, upper, jnp.where(row == 1, whole - upper, total)).astype(BF16)


def plane(value, x, y):
    rep, dom, tp = (lax.axis_size(a) for a in EVERY)
    flip = (2 * dom * tp if x else 0) + (1 if y else 0)
    return lax.ppermute(value, EVERY, [(s, s ^ flip) for s in range(rep * dom * tp)])


def along_dom(mine):
    count, bit = lax.axis_size("dom"), 1
    while bit < count:
        flips = [bit] if 2 * bit >= count else [bit, 2 * bit, 3 * bit]
        mine = summed(mine, *[partner(mine, "dom", flip) for flip in flips])
        bit *= 4
    return mine


def reduce_slots(slots):
    part = slots[:4] + partner(slots[4:], "rep", 1)
    mine = summed(part[0], plane(part[1], 0, 1), plane(part[2], 1, 0), plane(part[3], 1, 1))
    mine = along_dom(mine)
    close = [mine, plane(mine, 0, 1), plane(mine, 1, 0), plane(mine, 1, 1)]
    return close, partner(jnp.stack(close), "rep", 1)


def local(features, radial, neighbours, halo_lists, slab_counts, frame_labels, w_a, w_c, w_b, readout):
    frames, beads, channels = features.shape
    hidden, layers = w_a.shape[2], w_a.shape[0]
    degree, halo = radial.shape[1], halo_lists.shape[2]
    lanes, halo_lanes = frames * beads, 2 * frames * halo
    rows = beads + halo_lanes
    scale = (2.0 / (frames * lax.axis_size("rep"))) / math.sqrt(beads * lax.axis_size(RING))
    rep = lax.axis_index("rep")
    me = (lax.rem(rep, 2) * 4 + (rep // 2) * 2 + lax.axis_index("tp")).astype(jnp.int32)
    where = jnp.stack([me, lax.rem(lax.axis_index(RING), 2).astype(jnp.int32)])

    half = (channels // 2, halo_lanes)
    state, select, first, second = kernel_call(
        select_kernel,
        (near((channels, lanes)), near((lanes, halo_lanes)), near(half), near(half)),
        (where, features, halo_lists),
        scratch=[
            pltpu.VMEM(features.shape, BF16),
            pltpu.VMEM(halo_lists.shape, jnp.int32),
            pltpu.SemaphoreType.DMA((2,)),
        ],
        smem=1,
        far=2,
    )
    second, first = swapped(second, 1), swapped(first, 0)
    weights = [near((layers, channels, hidden)), near((layers, channels, hidden)), near((layers, hidden, channels))]
    turned = [near((layers, hidden, channels)), near((layers, hidden, channels)), near((layers, channels, hidden))]
    onehot_type = near((frames, rows, degree * beads))
    onehot, edge, wa, wc, wb, wta, wtc, wtb, own, cross, live, sign, wide = kernel_call(
        functools.partial(prepare_kernel, halo),
        (
            onehot_type,
            near((frames, degree, SUB, beads)),
            *weights,
            *turned,
            near((hidden, lanes)),
            near((hidden, lanes), F32),
            near((1, lanes), F32),
            near((1, lanes), F32),
            near((channels, beads), F32),
        ),
        (where, slab_counts, frame_labels, neighbours, radial, w_a, w_c, w_b, readout, state),
        scratch=[
            pltpu.VMEM(neighbours.shape, jnp.int32),
            pltpu.VMEM(radial.shape, BF16),
            pltpu.VMEM(readout.shape, F32),
            pltpu.VMEM(neighbours.shape, jnp.int32),
            pltpu.SemaphoreType.DMA((6,)),
        ],
        smem=3,
        far=6,
        flops=2 * 10**9,
    )
    totals = (hidden, lanes)
    edge_slopes = (frames, hidden, degree * beads)
    state1, first, second, halo0, gathered0, slope0, slope_total0 = kernel_call(
        first_kernel,
        (
            near((channels, lanes)),
            near(half),
            near(half),
            near((channels, halo_lanes)),
            near(totals),
            near(edge_slopes),
            near(totals, F32),
        ),
        (first, second, onehot, edge, wta, wtb, own, cross, state, select),
        scratch=[pltpu.VMEM(totals, F32)],
        flops=4 * 10**9,
    )
    second, first = swapped(second, 1), swapped(first, 0)
    energy, grad_readout, cot, first, second, cot_own, cot_halo, cot_cross, halo1, gathered1, cot_low1 = kernel_call(
        functools.partial(middle_kernel, scale),
        (
            jax.ShapeDtypeStruct((frames, beads), F32),
            near((SUB, channels), F32),
            near((channels, lanes), F32),
            near(half),
            near(half),
            near(totals, F32),
            near((hidden, halo_lanes)),
            near(totals),
            near((channels, halo_lanes)),
            near(totals),
            near((channels, lanes)),
        ),
        (first, second, onehot, edge, wta, wtc, wtb, wb, state1, live, sign, wide),
        scratch=[pltpu.VMEM(edge_slopes, BF16), pltpu.VMEM(totals, F32), pltpu.VMEM(totals, F32)],
        flops=6 * 10**9,
    )
    second, first = swapped(second, 1), swapped(first, 0)
    chunk = hidden // 8
    upper_slots = kernel_call(
        upper_grads_kernel,
        near((8, SUB + 3 * chunk, channels), F32),
        (where, state1, halo1, gathered1, cot_low1, cot_own, cot_halo, cot_cross, grad_readout),
        smem=1,
        flops=10**9,
    )
    lower_slots = kernel_call(
        lower_kernel,
        near((8, 3 * chunk, channels), F32),
        (
            where, first, second, select, cot_own, cot_cross, cot, wa, wc, wb,
            onehot, slope0, slope_total0, state, halo0, gathered0,
        ),
        smem=1,
        flops=4 * 10**9,
    )
    close, far = reduce_slots(jnp.concatenate([upper_slots, lower_slots], axis=1))
    grad = jax.ShapeDtypeStruct((layers, channels, hidden), F32)
    grad_wa, grad_wc, grad_wb, grad_readout = kernel_call(
        finish_kernel,
        (grad, grad, grad, jax.ShapeDtypeStruct((channels,), F32)),
        (where, *close, far),
        smem=1,
    )
    return grad_wa, grad_wc, grad_wb, grad_readout, energy


def solution(mesh):
    placed = (
        P("rep", RING, None),
        P("rep", None, RING),
        P("rep", None, RING),
        P("rep", None, RING),
        P("rep", RING),
        P("rep"),
        P(),
        P(),
        P(),
        P(),
    )
    return jax.shard_map(
        local,
        mesh=mesh,
        in_specs=placed,
        out_specs=(P(), P(), P(), P(), P("rep", RING)),
        check_vma=False,
    )
```

time: 216 us -> 78.9 us (0.37)
  waiting for transfers between devices: 98.1 us -> 32.8 us
  blocking collectives: 40.2 us -> 0 us
  matrix products: 25.8 us -> 0 us
  Pallas kernels: 0 us -> 20.7 us
  between operations: 14.4 us -> 0.82 us
  other arithmetic: 10.2 us -> 0.89 us
  local copies, waits for them, and re-layouts: 6.14 us -> 1.44 us
    psum x1 -> x0, waiting for transfers between devices: 92.9 us -> none  [local(): lax.psum((stacked, grad_readout), ('rep', 'dom', 'tp'))]
    psum x1 -> x0, blocking collectives: 40.2 us -> none  [local(): lax.psum((stacked, grad_readout), ('rep', 'dom', 'tp'))]
    ppermute x8 -> x17, waiting for transfers between devices: 5.18 us -> 32.8 us  [the longest x6 13.7 us: plane(): lax.ppermute(value, EVERY, [(s, s ^ flip) for s in range(rep * dom * tp)])]
    dot_general x28 -> x0, matrix products: 25.8 us -> none  [the longest x2 10.2 us: local(): jnp.einsum('fksr,frh->fksh', edge_select, lookup_table, preferred_element...]
    pallas_call x0 -> x7, Pallas kernels: none -> 20.7 us  [kernel_call(): pl.pallas_call(body, out_shape=outs, in_specs=[pl.BlockSpec(memory_space=...]
    reduce_sum x3 -> x0, other arithmetic: 7.32 us -> none  [the longest x2 7.1 us: local(): cot_cross = jnp.sum(cot_edge, axis=1)]
    mul x4 -> x0, other arithmetic: 2.8 us -> none  [the longest x1 0.78 us: local(): radial.astype(jnp.float32) * (neighbours >= 0).astype(jnp.float32)]
    unnamed x19 -> x3, local copies, waits for them, and re-layouts: 3.85 us -> 1.4 us
  transfers between devices with their start and end apart: 9 -> 17, of which waited for: 4 -> 14; matrix products, arithmetic and copies ran while one was open for 2% -> 1% of each run, Pallas kernels for 0% -> 6%
where the time goes in v1:
time: 78.9 us; the launch traced here: 78.7 us
  waiting for transfers between devices  32.8 us (42%)
  starting transfers between devices  22.1 us (28%)
  Pallas kernels  20.7 us (26%)
  local copies, waits for them, and re-layouts  1.44 us (2%)
  other arithmetic  0.89 us (1%)
  between operations  0.82 us (1%)
    pallas_call x7, Pallas kernels, kernel_call(): pl.pallas_call(body, out_shape=outs, in_specs=[pl.BlockSpec(memory_space=...  20.7 us
    ppermute x6, waiting for transfers between devices, plane(): lax.ppermute(value, EVERY, [(s, s ^ flip) for s in range(rep * dom * tp)])  13.7 us
    ppermute x6, starting transfers between devices, swapped(): return lax.ppermute(value, RING, pairs)  10.4 us
    ppermute x5, waiting for transfers between devices, partner(): lax.ppermute(value, axis, [(s, s ^ bits) for s in range(lax.axis_size(axi...  10.3 us
    ppermute x6, waiting for transfers between devices, swapped(): return lax.ppermute(value, RING, pairs)  8.84 us
    ppermute x6, starting transfers between devices, plane(): lax.ppermute(value, EVERY, [(s, s ^ flip) for s in range(rep * dom * tp)])  7.11 us
    ppermute x5, starting transfers between devices, partner(): lax.ppermute(value, axis, [(s, s ^ bits) for s in range(lax.axis_size(axi...  4.59 us
  transfers between devices with their start and end apart: 17, of which 14 were waited for; matrix products, arithmetic and copies ran while one was open for 1% of the time, Pallas kernels for 6%

profile of v1, /device:TPU:0, one launch (start us, length us, event | category | flops | bytes accessed | tf_op | source)
XLA Modules:
  0.0 78.7 jit_solution(17570474519939246314)
XLA Ops:
  0.7 1.8 %shard_map.137 = (bf16[256,256]{1,0:T(8,128)(2,1)S(1)}, bf16[256,128]{1,0:T(8,128)(2,1)S(1)}, bf16[128,128]{1,0:T(8,128)(2,1)S(1)}, bf16[128,128]{1,0:T(8,128)(2,1)S(1)}) custom-call(s32[2]{0:T(128)S(1)} %pad_add_fusion.where_ref.me_ref, bf16[2,128,256]{2,1,0:T(8,128)(2,1)} %feat_hbm.1, s32[2,2,32]{2,1,0:T(2,128)} %list_hbm.1), custom_call_target="tpu_custom_call" | custom-call | tf_op jit(solution)/shard_map/pallas_call | solution.py:321
  2.5 3.0 %collective-permute-start = (bf16[128,128]{1,0:T(8,128)(2,1)S(1)}, bf16[128,128]{1,0:T(8,128)(2,1)S(1)}, u32[]{:S(2)}, u32[]{:S(2)}) collective-permute-start(bf16[128,128]{1,0:T(8,128)(2,1)S(1)} %get-tuple-element.44), channel_id=1, source_target_pairs={{0,1},{1,0},{2,3},{3,2},{4,5},{5,4},{6,7},{7,6},{8,9},{9,8},{10,11... | collective-permute-start | bytes 98312 | tf_op jit(solution)/shard_map/ppermute | solution.py:344
  5.6 3.5 %collective-permute-start.1 = (bf16[128,128]{1,0:T(8,128)(2,1)S(1)}, bf16[128,128]{1,0:T(8,128)(2,1)S(1)}, u32[]{:S(2)}, u32[]{:S(2)}) collective-permute-start(bf16[128,128]{1,0:T(8,128)(2,1)S(1)} %get-tuple-element.45), channel_id=1, source_target_pairs={{0,7},{1,2},{2,1},{3,4},{4,3},{5,6},{6,5},{7,0},{8,15},{9,10},{10,... | collective-permute-start | bytes 98312 | tf_op jit(solution)/shard_map/ppermute | solution.py:344
  10.5 3.5 %shard_map.138 = (bf16[2,256,4096]{2,1,0:T(8,128)(2,1)S(1)}, bf16[2,32,16,128]{3,2,1,0:T(8,128)(2,1)S(1)}, bf16[2,256,256]{2,1,0:T(8,128)(2,1)S(1)}, bf16[2,256,...) custom-call(s32[2]{0:T(128)S(1)} %pad_add_fusion.where_ref.me_ref, ...), custom_call_target="tpu_custom_call" | custom-call | flops 2000000000 | tf_op jit(solution)/shard_map/pallas_call | solution.py:321
  14.1 4.0 %shard_map.139 = (bf16[256,256]{1,0:T(8,128)(2,1)S(1)}, bf16[128,128]{1,0:T(8,128)(2,1)S(1)}, bf16[128,128]{1,0:T(8,128)(2,1)S(1)}, bf16[256,128]{1,0:T(8,128)(2...) custom-call(bf16[128,128]{1,0:T(8,128)(2,1)S(1)} %collective-permute-done.hf_ref, ...), custom_call_target="tpu_custom_call" | custom-call | flops 4000000000 | tf_op jit(solution)/shard_map/pallas_call | solution.py:321
  18.2 1.9 %collective-permute-start.3 = (bf16[128,128]{1,0:T(8,128)(2,1)S(1)}, bf16[128,128]{1,0:T(8,128)(2,1)S(1)}, u32[]{:S(2)}, u32[]{:S(2)}) collective-permute-start(bf16[128,128]{1,0:T(8,128)(2,1)S(1)} %get-tuple-element.56), channel_id=1, source_target_pairs={{0,7},{1,2},{2,1},{3,4},{4,3},{5,6},{6,5},{7,0},{8,15},{9,10},{10,... | collective-permute-start | bytes 98312 | tf_op jit(solution)/shard_map/ppermute | solution.py:344
  20.1 2.0 %collective-permute-done.2.hf_ref = bf16[128,128]{1,0:T(8,128)(2,1)S(1)} collective-permute-done((bf16[128,128]{1,0:T(8,128)(2,1)S(1)}, bf16[128,128]{1,0:T(8,128)(2,1)S(1)}, u32[]{:S(2)}, u32[]{:S(2)}) %collective-permute-start.2) | collective-permute-done | bytes 32800 | tf_op jit(solution)/shard_map/ppermute | solution.py:344
  22.1 2.8 %collective-permute-done.3.hs_ref = bf16[128,128]{1,0:T(8,128)(2,1)S(1)} collective-permute-done((bf16[128,128]{1,0:T(8,128)(2,1)S(1)}, bf16[128,128]{1,0:T(8,128)(2,1)S(1)}, u32[]{:S(2)}, u32[]{:S(2)}) %collective-permute-start.3) | collective-permute-done | bytes 32800 | tf_op jit(solution)/shard_map/ppermute | solution.py:344
  24.9 5.8 %shard_map.140 = (f32[2,128]{1,0:T(2,128)}, f32[16,256]{1,0:T(8,128)S(1)}, f32[256,256]{1,0:T(8,128)S(1)}, bf16[128,128]{1,0:T(8,128)(2,1)S(1)}, bf16[128,128]{1...) custom-call(bf16[128,128]{1,0:T(8,128)(2,1)S(1)} %collective-permute, ...), custom_call_target="tpu_custom_call" | custom-call | flops 6000000000 | tf_op jit(solution)/shard_map/pallas_call | solution.py:321
  30.8 1.7 %collective-permute-start.5 = (bf16[128,128]{1,0:T(8,128)(2,1)S(1)}, bf16[128,128]{1,0:T(8,128)(2,1)S(1)}, u32[]{:S(2)}, u32[]{:S(2)}) collective-permute-start(bf16[128,128]{1,0:T(8,128)(2,1)S(1)} %get-tuple-element.70), channel_id=1, source_target_pairs={{0,7},{1,2},{2,1},{3,4},{4,3},{5,6},{6,5},{7,0},{8,15},{9,10},{10,... | collective-permute-start | bytes 98312 | tf_op jit(solution)/shard_map/ppermute | solution.py:344
  33.4 1.4 %collective-permute-done.4.bf_ref = bf16[128,128]{1,0:T(8,128)(2,1)S(1)} collective-permute-done((bf16[128,128]{1,0:T(8,128)(2,1)S(1)}, bf16[128,128]{1,0:T(8,128)(2,1)S(1)}, u32[]{:S(2)}, u32[]{:S(2)}) %collective-permute-start.4) | collective-permute-done | bytes 32800 | tf_op jit(solution)/shard_map/ppermute | solution.py:344
  34.8 2.7 %collective-permute-done.5.bs_ref = bf16[128,128]{1,0:T(8,128)(2,1)S(1)} collective-permute-done((bf16[128,128]{1,0:T(8,128)(2,1)S(1)}, bf16[128,128]{1,0:T(8,128)(2,1)S(1)}, u32[]{:S(2)}, u32[]{:S(2)}) %collective-permute-start.5) | collective-permute-done | bytes 32800 | tf_op jit(solution)/shard_map/ppermute | solution.py:344
  37.4 2.9 %shard_map.142 = f32[8,96,256]{2,1,0:T(8,128)S(1)} custom-call(s32[2]{0:T(128)S(1)} %pad_add_fusion.where_ref.me_ref, bf16[128,128]{1,0:T(8,128)(2,1)S(1)} %collective-permute-done.4.bf_ref, bf16[128,128]{1,0:T(8,128)(2,1)S(1)} %collective-permute-done.5.bs_ref, bf16[256,128]{1,0:T(8,128)(2,1)S(1)} %get-tuple-element.53.select_ref, ...), custom_call_target="tpu_custom_call" | custom-call | flops 4000000000 | tf_op jit(solution)/shard_map/pallas_call | solution.py:321
  40.4 2.4 %collective-permute-done.6 = f32[4,208,256]{2,1,0:T(8,128)S(1)} collective-permute-done((f32[4,208,256]{2,1,0:T(8,128)S(1)}, f32[4,208,256]{2,1,0:T(8,128)S(1)}, u32[]{:S(2)}, u32[]{:S(2)}) %collective-permute-start.6) | collective-permute-done | bytes 852000 | tf_op jit(solution)/shard_map/ppermute | solution.py:348
  43.1 1.5 %collective-permute-start.8 = (f32[208,256]{1,0:T(8,128)S(1)}, f32[208,256]{1,0:T(8,128)S(1)}, u32[]{:S(2)}, u32[]{:S(2)}) collective-permute-start(f32[208,256]{1,0:T(8,128)S(1)} %get-tuple-element.85), channel_id=1, source_target_pairs={{0,16},{1,17},{2,18},{3,19},{4,20},{5,21},{6,22},{7,23},{8,24},{9,... | collective-permute-start | bytes 638984 | tf_op jit(solution)/shard_map/ppermute | solution.py:364
  44.6 1.9 %collective-permute-start.9 = (f32[208,256]{1,0:T(8,128)S(1)}, f32[208,256]{1,0:T(8,128)S(1)}, u32[]{:S(2)}, u32[]{:S(2)}) collective-permute-start(f32[208,256]{1,0:T(8,128)S(1)} %get-tuple-element.84), channel_id=1, source_target_pairs={{0,17},{1,16},{2,19},{3,18},{4,21},{5,20},{6,23},{7,22},{8,25},{9,... | collective-permute-start | bytes 638984 | tf_op jit(solution)/shard_map/ppermute | solution.py:364
  46.5 3.8 %collective-permute-done.7 = f32[208,256]{1,0:T(8,128)S(1)} collective-permute-done((f32[208,256]{1,0:T(8,128)S(1)}, f32[208,256]{1,0:T(8,128)S(1)}, u32[]{:S(2)}, u32[]{:S(2)}) %collective-permute-start.7) | collective-permute-done | bytes 213024 | tf_op jit(solution)/shard_map/ppermute | solution.py:364
  51.2 4.9 %collective-permute-done.9 = f32[208,256]{1,0:T(8,128)S(1)} collective-permute-done((f32[208,256]{1,0:T(8,128)S(1)}, f32[208,256]{1,0:T(8,128)S(1)}, u32[]{:S(2)}, u32[]{:S(2)}) %collective-permute-start.9) | collective-permute-done | bytes 213024 | tf_op jit(solution)/shard_map/ppermute | solution.py:364
  57.5 3.3 %collective-permute-start.12 = (bf16[208,256]{1,0:T(8,128)(2,1)S(1)}, bf16[208,256]{1,0:T(8,128)(2,1)S(1)}, u32[]{:S(2)}, u32[]{:S(2)}) collective-permute-start(bf16[208,256]{1,0:T(8,128)(2,1)S(1)} %select_convert_fusion.1), channel_id=1, source_target_pairs={{0,6},{2,4},{4,2},{6,0},{1,7},{3,5},{5,3},{7,1},{8,14},{10,12},{12... | collective-permute-start | bytes 319496 | tf_op jit(solution)/shard_map/ppermute | solution.py:348
  61.4 5.6 %collective-permute-done.11 = bf16[208,256]{1,0:T(8,128)(2,1)S(1)} collective-permute-done((bf16[208,256]{1,0:T(8,128)(2,1)S(1)}, bf16[208,256]{1,0:T(8,128)(2,1)S(1)}, u32[]{:S(2)}, u32[]{:S(2)}) %collective-permute-start.11) | collective-permute-done | bytes 106528 | tf_op jit(solution)/shard_map/ppermute | solution.py:348
  68.0 1.5 %collective-permute-start.14 = (bf16[208,256]{1,0:T(8,128)(2,1)S(1)}, bf16[208,256]{1,0:T(8,128)(2,1)S(1)}, u32[]{:S(2)}, u32[]{:S(2)}) collective-permute-start(bf16[208,256]{1,0:T(8,128)(2,1)S(1)} %select_convert_fusion.refs_0_), channel_id=1, source_target_pairs={{0,16},{1,17},{2,18},{3,19},{4,20},{5,21},{6,22},{7,23},{8,24},{9,... | collective-permute-start | bytes 319496 | tf_op jit(solution)/shard_map/ppermute | solution.py:364
  72.7 2.4 %collective-permute-done.15.refs_3_ = bf16[208,256]{1,0:T(8,128)(2,1)S(1)} collective-permute-done((bf16[208,256]{1,0:T(8,128)(2,1)S(1)}, bf16[208,256]{1,0:T(8,128)(2,1)S(1)}, u32[]{:S(2)}, u32[]{:S(2)}) %collective-permute-start.15) | collective-permute-done | bytes 106528 | tf_op jit(solution)/shard_map/ppermute | solution.py:364
  75.2 1.8 %collective-permute-done.16.refs_4_ = bf16[4,208,256]{2,1,0:T(8,128)(2,1)S(1)} collective-permute-done((bf16[4,208,256]{2,1,0:T(8,128)(2,1)S(1)}, bf16[4,208,256]{2,1,0:T(8,128)(2,1)S(1)}, u32[]{:S(2)}, u32[]{:S(2)}) %collective-permute-start.16) | collective-permute-done | bytes 426016 | tf_op jit(solution)/shard_map/ppermute | solution.py:348
  76.9 1.8 %shard_map.143 = (f32[2,256,256]{2,1,0:T(8,128)}, f32[2,256,256]{2,1,0:T(8,128)}, f32[2,256,256]{2,1,0:T(8,128)}, f32[256]{0:T(256)}) custom-call(s32[2]{0:T(128)S(1)} %pad_add_fusion.where_ref.me_ref, bf16[208,256]{1,0:T(8,128)(2,1)S(1)} %select_convert_fusion.refs_0_, bf16[208,256]{1,0:T(8,128)(2,1)S(1)} %collective-permute-done.13.refs_1_, ...), custom_call_target="tpu_custom_call" | custom-call | tf_op jit(solution)/shard_map/pallas_call | solution.py:321
  (33 shorter events, 10.3 us)
Async XLA Ops:
  2.5 11.5 %collective-permute-start = (bf16[128,128]{1,0:T(8,128)(2,1)S(1)}, bf16[128,128]{1,0:T(8,128)(2,1)S(1)}, u32[]{:S(2)}, u32[]{:S(2)}) collective-permute-start(bf16[128,128]{1,0:T(8,128)(2,1)S(1)} %get-tuple-element.44), channel_id=1, source_target_pairs={{0,1},{1,0},{2,3},{3,2},{4,5},{5,4},{6,7},{7,6},{8,9},{9,8},{10,11... | collective-permute-start | bytes 98312 | tf_op jit(solution)/shard_map/ppermute | solution.py:344
  5.6 8.5 %collective-permute-start.1 = (bf16[128,128]{1,0:T(8,128)(2,1)S(1)}, bf16[128,128]{1,0:T(8,128)(2,1)S(1)}, u32[]{:S(2)}, u32[]{:S(2)}) collective-permute-start(bf16[128,128]{1,0:T(8,128)(2,1)S(1)} %get-tuple-element.45), channel_id=1, source_target_pairs={{0,7},{1,2},{2,1},{3,4},{4,3},{5,6},{6,5},{7,0},{8,15},{9,10},{10,... | collective-permute-start | bytes 98312 | tf_op jit(solution)/shard_map/ppermute | solution.py:344
  9.8 0.7 copy-start
  18.1 4.0 %collective-permute-start.2 = (bf16[128,128]{1,0:T(8,128)(2,1)S(1)}, bf16[128,128]{1,0:T(8,128)(2,1)S(1)}, u32[]{:S(2)}, u32[]{:S(2)}) collective-permute-start(bf16[128,128]{1,0:T(8,128)(2,1)S(1)} %get-tuple-element.55), channel_id=1, source_target_pairs={{0,1},{1,0},{2,3},{3,2},{4,5},{5,4},{6,7},{7,6},{8,9},{9,8},{10,11... | collective-permute-start | bytes 98312 | tf_op jit(solution)/shard_map/ppermute | solution.py:344
  18.2 6.7 %collective-permute-start.3 = (bf16[128,128]{1,0:T(8,128)(2,1)S(1)}, bf16[128,128]{1,0:T(8,128)(2,1)S(1)}, u32[]{:S(2)}, u32[]{:S(2)}) collective-permute-start(bf16[128,128]{1,0:T(8,128)(2,1)S(1)} %get-tuple-element.56), channel_id=1, source_target_pairs={{0,7},{1,2},{2,1},{3,4},{4,3},{5,6},{6,5},{7,0},{8,15},{9,10},{10,... | collective-permute-start | bytes 98312 | tf_op jit(solution)/shard_map/ppermute | solution.py:344
  30.6 4.1 %collective-permute-start.4 = (bf16[128,128]{1,0:T(8,128)(2,1)S(1)}, bf16[128,128]{1,0:T(8,128)(2,1)S(1)}, u32[]{:S(2)}, u32[]{:S(2)}) collective-permute-start(bf16[128,128]{1,0:T(8,128)(2,1)S(1)} %get-tuple-element.69), channel_id=1, source_target_pairs={{0,1},{1,0},{2,3},{3,2},{4,5},{5,4},{6,7},{7,6},{8,9},{9,8},{10,11... | collective-permute-start | bytes 98312 | tf_op jit(solution)/shard_map/ppermute | solution.py:344
  30.8 6.6 %collective-permute-start.5 = (bf16[128,128]{1,0:T(8,128)(2,1)S(1)}, bf16[128,128]{1,0:T(8,128)(2,1)S(1)}, u32[]{:S(2)}, u32[]{:S(2)}) collective-permute-start(bf16[128,128]{1,0:T(8,128)(2,1)S(1)} %get-tuple-element.70), channel_id=1, source_target_pairs={{0,7},{1,2},{2,1},{3,4},{4,3},{5,6},{6,5},{7,0},{8,15},{9,10},{10,... | collective-permute-start | bytes 98312 | tf_op jit(solution)/shard_map/ppermute | solution.py:344
  40.4 2.4 %collective-permute-start.6 = (f32[4,208,256]{2,1,0:T(8,128)S(1)}, f32[4,208,256]{2,1,0:T(8,128)S(1)}, u32[]{:S(2)}, u32[]{:S(2)}) collective-permute-start(f32[4,208,256]{2,1,0:T(8,128)S(1)} %pad_maximum_fusion), channel_id=1, source_target_pairs={{0,8},{8,0},{16,24},{24,16},{1,9},{9,1},{17,25},{25,17},{2,10},{10... | collective-permute-start | bytes 2555912 | tf_op jit(solution)/shard_map/ppermute | solution.py:348
  43.0 7.4 %collective-permute-start.7 = (f32[208,256]{1,0:T(8,128)S(1)}, f32[208,256]{1,0:T(8,128)S(1)}, u32[]{:S(2)}, u32[]{:S(2)}) collective-permute-start(f32[208,256]{1,0:T(8,128)S(1)} %get-tuple-element.83), channel_id=1, source_target_pairs={{0,1},{1,0},{2,3},{3,2},{4,5},{5,4},{6,7},{7,6},{8,9},{9,8},{10,11... | collective-permute-start | bytes 638984 | tf_op jit(solution)/shard_map/ppermute | solution.py:364
  43.1 8.1 %collective-permute-start.8 = (f32[208,256]{1,0:T(8,128)S(1)}, f32[208,256]{1,0:T(8,128)S(1)}, u32[]{:S(2)}, u32[]{:S(2)}) collective-permute-start(f32[208,256]{1,0:T(8,128)S(1)} %get-tuple-element.85), channel_id=1, source_target_pairs={{0,16},{1,17},{2,18},{3,19},{4,20},{5,21},{6,22},{7,23},{8,24},{9,... | collective-permute-start | bytes 638984 | tf_op jit(solution)/shard_map/ppermute | solution.py:364
  44.6 11.5 %collective-permute-start.9 = (f32[208,256]{1,0:T(8,128)S(1)}, f32[208,256]{1,0:T(8,128)S(1)}, u32[]{:S(2)}, u32[]{:S(2)}) collective-permute-start(f32[208,256]{1,0:T(8,128)S(1)} %get-tuple-element.84), channel_id=1, source_target_pairs={{0,17},{1,16},{2,19},{3,18},{4,21},{5,20},{6,23},{7,22},{8,25},{9,... | collective-permute-start | bytes 638984 | tf_op jit(solution)/shard_map/ppermute | solution.py:364
  56.3 5.1 %collective-permute-start.10 = (bf16[208,256]{1,0:T(8,128)(2,1)S(1)}, bf16[208,256]{1,0:T(8,128)(2,1)S(1)}, u32[]{:S(2)}, u32[]{:S(2)}) collective-permute-start(bf16[208,256]{1,0:T(8,128)(2,1)S(1)} %select_convert_fusion.1), channel_id=1, source_target_pairs={{0,2},{2,0},{4,6},{6,4},{1,3},{3,1},{5,7},{7,5},{8,10},{10,8},{12,... | collective-permute-start | bytes 319496 | tf_op jit(solution)/shard_map/ppermute | solution.py:348
  56.4 10.6 %collective-permute-start.11 = (bf16[208,256]{1,0:T(8,128)(2,1)S(1)}, bf16[208,256]{1,0:T(8,128)(2,1)S(1)}, u32[]{:S(2)}, u32[]{:S(2)}) collective-permute-start(bf16[208,256]{1,0:T(8,128)(2,1)S(1)} %select_convert_fusion.1), channel_id=1, source_target_pairs={{0,4},{2,6},{4,0},{6,2},{1,5},{3,7},{5,1},{7,3},{8,12},{10,14},{12... | collective-permute-start | bytes 319496 | tf_op jit(solution)/shard_map/ppermute | solution.py:348
  57.5 9.5 %collective-permute-start.12 = (bf16[208,256]{1,0:T(8,128)(2,1)S(1)}, bf16[208,256]{1,0:T(8,128)(2,1)S(1)}, u32[]{:S(2)}, u32[]{:S(2)}) collective-permute-start(bf16[208,256]{1,0:T(8,128)(2,1)S(1)} %select_convert_fusion.1), channel_id=1, source_target_pairs={{0,6},{2,4},{4,2},{6,0},{1,7},{3,5},{5,3},{7,1},{8,14},{10,12},{12... | collective-permute-start | bytes 319496 | tf_op jit(solution)/shard_map/ppermute | solution.py:348
  67.2 4.8 %collective-permute-start.13 = (bf16[208,256]{1,0:T(8,128)(2,1)S(1)}, bf16[208,256]{1,0:T(8,128)(2,1)S(1)}, u32[]{:S(2)}, u32[]{:S(2)}) collective-permute-start(bf16[208,256]{1,0:T(8,128)(2,1)S(1)} %select_convert_fusion.refs_0_), channel_id=1, source_target_pairs={{0,1},{1,0},{2,3},{3,2},{4,5},{5,4},{6,7},{7,6},{8,9},{9,8},{10,11... | collective-permute-start | bytes 319496 | tf_op jit(solution)/shard_map/ppermute | solution.py:364
  68.0 4.7 %collective-permute-start.14 = (bf16[208,256]{1,0:T(8,128)(2,1)S(1)}, bf16[208,256]{1,0:T(8,128)(2,1)S(1)}, u32[]{:S(2)}, u32[]{:S(2)}) collective-permute-start(bf16[208,256]{1,0:T(8,128)(2,1)S(1)} %select_convert_fusion.refs_0_), channel_id=1, source_target_pairs={{0,16},{1,17},{2,18},{3,19},{4,20},{5,21},{6,22},{7,23},{8,24},{9,... | collective-permute-start | bytes 319496 | tf_op jit(solution)/shard_map/ppermute | solution.py:364
  69.4 5.6 %collective-permute-start.15 = (bf16[208,256]{1,0:T(8,128)(2,1)S(1)}, bf16[208,256]{1,0:T(8,128)(2,1)S(1)}, u32[]{:S(2)}, u32[]{:S(2)}) collective-permute-start(bf16[208,256]{1,0:T(8,128)(2,1)S(1)} %select_convert_fusion.refs_0_), channel_id=1, source_target_pairs={{0,17},{1,16},{2,19},{3,18},{4,21},{5,20},{6,23},{7,22},{8,25},{9,... | collective-permute-start | bytes 319496 | tf_op jit(solution)/shard_map/ppermute | solution.py:364
  75.1 1.8 %collective-permute-start.16 = (bf16[4,208,256]{2,1,0:T(8,128)(2,1)S(1)}, bf16[4,208,256]{2,1,0:T(8,128)(2,1)S(1)}, u32[]{:S(2)}, u32[]{:S(2)}) collective-permute-start(bf16[4,208,256]{2,1,0:T(8,128)(2,1)S(1)} %pad_maximum_fusion.1), channel_id=1, source_target_pairs={{0,8},{8,0},{16,24},{24,16},{1,9},{9,1},{17,25},{25,17},{2,10},{10... | collective-permute-start | bytes 1277960 | tf_op jit(solution)/shard_map/ppermute | solution.py:348

commit v2 on v1

--- a/solution.py
+++ b/solution.py
@@ -8,7 +8,7 @@
 from jax.experimental.pallas import tpu as pltpu
 from jax.sharding import PartitionSpec as P
 
-BF16, F32 = jnp.bfloat16, jnp.float32
+BF16, F16, F32 = jnp.bfloat16, jnp.float16, jnp.float32
 MEBI = 1024 * 1024
 SUB = 16
 RING = ("dom", "tp")
@@ -69,9 +69,12 @@
 
 
 def select_kernel(
-    where_ref, feat_hbm, list_hbm, state_ref, select_ref, first_ref, second_ref, feat_ref, list_ref, sems
-):
-    list_copy, feat_copy = copies_of([(list_hbm, list_ref), (feat_hbm, feat_ref)], sems)
+    where_ref, feat_hbm, list_hbm, neigh_hbm, radial_hbm,
+    state_ref, select_ref, first_ref, second_ref, neigh_ref, radial_ref,
+    feat_ref, list_ref, sems,
+):
+    pairs = [(list_hbm, list_ref), (feat_hbm, feat_ref), (neigh_hbm, neigh_ref), (radial_hbm, radial_ref)]
+    list_copy, feat_copy, *others = copies_of(pairs, sems)
     list_copy.wait()
     frames, beads, channels = feat_ref.shape
     lanes = frames * beads
@@ -83,6 +86,8 @@
     write_halo(first_ref, second_ref, mul(state, select))
     state_ref[...] = state
     select_ref[...] = select
+    for copy in others:
+        copy.wait()
 
 
 def write_onehot(onehot_ref, slots_ref):
@@ -95,23 +100,15 @@
 
 
 def prepare_kernel(
-    halo, where_ref, count_ref, label_ref, neigh_hbm, radial_hbm, wa_hbm, wc_hbm, wb_hbm, readout_hbm, state_ref,
-    onehot_ref, edge_ref, wa_ref, wc_ref, wb_ref, wta_ref, wtc_ref, wtb_ref, own_ref, cross_ref, live_ref, sign_ref, wide_ref,
-    neigh_ref, radial_ref, readout_ref, slots_ref, sems,
+    halo, where_ref, wa_hbm, wc_hbm, wb_hbm, readout_hbm, state_ref, neigh_ref, radial_ref,
+    onehot_ref, edge_ref, wa_ref, wc_ref, wb_ref, readout_ref, wta_ref, wtb_ref, own_ref, cross_ref,
+    slots_ref, sems,
 ):
     frames, degree, beads = neigh_ref.shape
-    pairs = [(neigh_hbm, neigh_ref), (radial_hbm, radial_ref), (wa_hbm, wa_ref), (wc_hbm, wc_ref), (wb_hbm, wb_ref)]
-    pairs.append((readout_hbm, readout_ref))
+    pairs = [(wa_hbm, wa_ref), (wc_hbm, wc_ref), (wb_hbm, wb_ref), (readout_hbm, readout_ref)]
     copies = copies_of(pairs, sems)
-    copies[0].wait()
-    copies[1].wait()
     odd = where_ref[1] != 0
-    bead = lax.broadcasted_iota(jnp.int32, (1, beads), 1)
-    for frame in range(frames):
-        live = jnp.where(bead < count_ref[frame, 0], 1.0, 0.0)
-        lanes = slice(frame * beads, (frame + 1) * beads)
-        live_ref[:, lanes] = live
-        sign_ref[:, lanes] = jnp.where(label_ref[frame] == 0, live, -live)
+    for frame in range(frames):
         neigh = neigh_ref[frame]
         weight = jnp.where(neigh >= 0, radial_ref[frame].astype(F32), 0.0)
         entry = neigh - beads
@@ -123,16 +120,30 @@
         for slot in range(degree):
             edge_ref[frame, slot] = jnp.broadcast_to(weight[slot : slot + 1, :], (SUB, beads)).astype(BF16)
     write_onehot(onehot_ref, slots_ref)
-    for copy in copies[2:]:
+    for copy in copies:
         copy.wait()
-    for layer in range(wa_ref.shape[0]):
-        wta_ref[layer] = wa_ref[layer].astype(F32).T.astype(BF16)
-        wtc_ref[layer] = wc_ref[layer].astype(F32).T.astype(BF16)
-        wtb_ref[layer] = wb_ref[layer].astype(F32).T.astype(BF16)
-    own_ref[...] = mul(wta_ref[0], state_ref[...]).astype(BF16)
-    cross_ref[...] = mul(wtc_ref[0], state_ref[...])
+    turned = wa_ref[0].astype(F32).T.astype(BF16)
+    wta_ref[...] = turned
+    wtb_ref[...] = wb_ref[0].astype(F32).T.astype(BF16)
+    own_ref[...] = mul(turned, state_ref[...]).astype(BF16)
+    cross_ref[...] = mul(wc_ref[0].astype(F32).T.astype(BF16), state_ref[...])
+
+
+def later_kernel(
+    frame_ref, _after, wa_ref, wc_ref, wb_ref, readout_ref, wta_ref, wtc_ref, wtb_ref, wide_ref, live_ref, sign_ref
+):
+    for source, target in ((wa_ref, wta_ref), (wc_ref, wtc_ref), (wb_ref, wtb_ref)):
+        target[...] = source[source.shape[0] - 1].astype(F32).T.astype(BF16)
     wide = readout_ref[...].reshape(1, -1)
-    wide_ref[...] = jnp.broadcast_to(wide, (wide_ref.shape[1], wide.shape[1])).T
+    beads = wide_ref.shape[1]
+    wide_ref[...] = jnp.broadcast_to(wide, (beads, wide.shape[1])).T
+    frames = live_ref.shape[1] // beads
+    bead = lax.broadcasted_iota(jnp.int32, (1, beads), 1)
+    for frame in range(frames):
+        live = jnp.where(bead < frame_ref[frame], 1.0, 0.0)
+        here = slice(frame * beads, (frame + 1) * beads)
+        live_ref[:, here] = live
+        sign_ref[:, here] = jnp.where(frame_ref[frames + frame] == 0, live, -live)
 
 
 def edges(onehot_ref, edge_ref, own, halo, cross, slope_ref, total_ref, slope_total_ref, group=4):
@@ -191,11 +202,11 @@
 ):
     halo = read_halo(hf_ref, hs_ref)
     halo_ref[...] = halo
-    halo_rows = mul(wta_ref[0], halo).astype(BF16)
+    halo_rows = mul(wta_ref[...], halo).astype(BF16)
     edges(onehot_ref, edge_ref, own_ref[...], halo_rows, cross_ref[...], slope_ref, total_ref, slope_total_ref)
     gathered = total_ref[...].astype(BF16)
     gathered_ref[...] = gathered
-    state = (state_ref[...].astype(F32) + mul(wtb_ref[0], gathered)).astype(BF16)
+    state = (state_ref[...].astype(F32) + mul(wtb_ref[...], gathered)).astype(BF16)
     next_ref[...] = state
     write_halo(first_ref, second_ref, mul(state, select_ref[...]))
 
@@ -207,19 +218,19 @@
     halo_ref, gathered_ref, cot_low_ref,
     slope_ref, slope_total_ref, total_ref,
 ):
-    last = wta_ref.shape[0] - 1
+    last = wb_ref.shape[0] - 1
     beads = edge_ref.shape[3]
     frames = edge_ref.shape[0]
     halo = read_halo(hf_ref, hs_ref)
     halo_ref[...] = halo
     state = state_ref[...]
-    own = mul(wta_ref[last], state).astype(BF16)
-    cross = mul(wtc_ref[last], state)
-    halo_rows = mul(wta_ref[last], halo).astype(BF16)
+    own = mul(wta_ref[...], state).astype(BF16)
+    cross = mul(wtc_ref[...], state)
+    halo_rows = mul(wta_ref[...], halo).astype(BF16)
     edges(onehot_ref, edge_ref, own, halo_rows, cross, slope_ref, total_ref, slope_total_ref)
     gathered = total_ref[...].astype(BF16)
     gathered_ref[...] = gathered
-    final = (state.astype(F32) + mul(wtb_ref[last], gathered)).astype(BF16).astype(F32)
+    final = (state.astype(F32) + mul(wtb_ref[...], gathered)).astype(BF16).astype(F32)
     sigmoid = jax.nn.sigmoid(final)
     activated = final * sigmoid
     readout = jnp.concatenate([readout_ref[...]] * frames, axis=1)
@@ -252,7 +263,8 @@
     for chunk in range(slots):
         slot = jnp.bitwise_xor(me, chunk)
         for number, grad in enumerate(grads):
-            slots_ref[slot, base + number * rows : base + (number + 1) * rows, :] = grad[chunk * rows : (chunk + 1) * rows]
+            start = base + number * rows
+            slots_ref[slot, start : start + rows, :] = grad[chunk * rows : (chunk + 1) * rows]
 
 
 def upper_grads_kernel(
@@ -263,19 +275,18 @@
     grad_a = mul_nt(state, cot_own_ref[...].astype(BF16)) + mul_nt(halo_ref[...], cot_halo_ref[...])
     grad_c = mul_nt(state, cot_cross_ref[...])
     grad_b = mul_nt(gathered_ref[...], cot_low_ref[...])
+    row = lax.broadcasted_iota(jnp.int32, (SUB, slots_ref.shape[2]), 0)
+    head = jnp.where(row == 0, grad_readout_ref[...], 0.0)
+    for slot in range(slots_ref.shape[0]):
+        slots_ref[slot, :SUB, :] = head
     put_slots(slots_ref, me, [grad_a, grad_c, grad_b], SUB)
-    row = lax.broadcasted_iota(jnp.int32, (SUB, slots_ref.shape[2]), 0)
-    only = jnp.where(row == 0, grad_readout_ref[...], 0.0)
-    for slot in range(slots_ref.shape[0]):
-        slots_ref[slot, :SUB, :] = only
 
 
 def lower_kernel(
     me_ref, bf_ref, bs_ref, select_ref, cot_own_ref, cot_cross_ref, cot_ref, wa_ref, wc_ref, wb_ref,
-    onehot_ref, slope_ref, slope_total_ref, state_ref, halo_ref, gathered_ref,
+    onehot_ref, slope_ref, slope_total_ref, state_ref, halo_ref, gathered_ref, _after,
     slots_ref,
 ):
-    me = me_ref[0]
     frames = onehot_ref.shape[0]
     beads = cot_ref.shape[1] // frames
     back = read_halo(bf_ref, bs_ref)
@@ -295,24 +306,24 @@
         grad_a = here if grad_a is None else grad_a + here
         cot_halo = part[:, beads:] if cot_halo is None else cot_halo + part[:, beads:]
     grad_a = grad_a + mul_nt(halo_ref[...], cot_halo.astype(BF16))
-    put_slots(slots_ref, me, [grad_a, grad_c, grad_b])
+    put_slots(slots_ref, me_ref[0], [grad_a, grad_c, grad_b])
 
 
 def finish_kernel(me_ref, *refs):
-    near, far = refs[:4], refs[4]
-    wa_ref, wc_ref, wb_ref, readout_ref = refs[5:]
+    *near, far, wa_ref, wc_ref, wb_ref, readout_ref = refs
     me = me_ref[0]
+    count = len(near)
     rows = (far.shape[1] - SUB) // 6
-    for slot in range(8):
-        source = near[slot] if slot < 4 else far.at[slot - 4]
+    total = jnp.zeros(readout_ref.shape, F32)
+    for slot in range(2 * count):
+        source = near[slot] if slot < count else far.at[slot - count]
         chunk = jnp.bitwise_xor(me, slot)
         place = pl.ds(pl.multiple_of(chunk * rows, rows), rows)
         for layer, base in ((1, SUB), (0, SUB + 3 * rows)):
             for number, ref in enumerate((wa_ref, wc_ref, wb_ref)):
                 ref[layer, place, :] = source[base + number * rows : base + (number + 1) * rows, :].astype(F32)
-        if slot == 0:
-            head = source[:SUB, :].astype(F32)
-            readout_ref[...] = head[0] + head[1]
+        total = jnp.where(chunk == 0, source[:SUB, :].astype(F32)[0], total)
+    readout_ref[...] = total
 
 
 def kernel_call(body, outs, args, scratch=(), flops=0, smem=0, far=0, limit=24):
@@ -349,13 +360,32 @@
 
 
 def summed(*terms):
-    total = terms[0].astype(F32)
-    for term in terms[1:]:
-        total = total + term.astype(F32)
-    whole = total[..., 0:1, :] + total[..., 1:2, :]
-    upper = lax.reduce_precision(whole, 8, 7)
-    row = lax.broadcasted_iota(jnp.int32, total.shape, total.ndim - 2)
-    return jnp.where(row == 0, upper, jnp.where(row == 1, whole - upper, total)).astype(BF16)
+    terms = [term.astype(F32) for term in terms]
+    while len(terms) > 1:
+        terms = [terms[n] + terms[n + 1] if n + 1 < len(terms) else terms[n] for n in range(0, len(terms), 2)]
+    return terms[0].astype(BF16)
+
+
+def powers(bounds):
+    return jnp.clip(jnp.ceil(jnp.log2(jnp.maximum(bounds, 1e-37))), -120.0, 120.0)
+
+
+def scaled(part):
+    count, rows, width = part.shape
+    head, body = part[:, :1], part[:, SUB:].reshape(count, 6, -1, width)
+    power = powers(jnp.concatenate([jnp.abs(head), jnp.max(jnp.abs(body), axis=2)], axis=1))
+    factor = jnp.exp2(-power)
+    body = (body * factor[:, 1:, None]).reshape(count, -1, width)
+    rest = jnp.zeros((count, SUB - 8, width), F32)
+    return jnp.concatenate([head * factor[:, :1], power, rest, body], axis=1).astype(F16)
+
+
+def restored(sent):
+    rows, width = sent.shape
+    sent = sent.astype(F32)
+    factor = jnp.exp2(sent[1:8])
+    body = sent[SUB:].reshape(6, -1, width) * factor[1:, None]
+    return jnp.concatenate([sent[:1] * factor[:1], jnp.zeros((SUB - 1, width), F32), body.reshape(-1, width)], axis=0)
 
 
 def plane(value, x, y):
@@ -373,12 +403,16 @@
     return mine
 
 
-def reduce_slots(slots):
-    part = slots[:4] + partner(slots[4:], "rep", 1)
-    mine = summed(part[0], plane(part[1], 0, 1), plane(part[2], 1, 0), plane(part[3], 1, 1))
-    mine = along_dom(mine)
-    close = [mine, plane(mine, 0, 1), plane(mine, 1, 0), plane(mine, 1, 1)]
-    return close, partner(jnp.stack(close), "rep", 1)
+def core_sum(slots):
+    return slots[:4] + partner(slots[4:], "rep", 1)
+
+
+def reduce_parts(parts):
+    part = jnp.concatenate(parts, axis=1)
+    sent = scaled(part[1:])
+    terms = [restored(plane(sent[0], 0, 1)), restored(plane(sent[1], 1, 0)), restored(plane(sent[2], 1, 1))]
+    mine = along_dom(summed(part[0], *terms))
+    return [mine, plane(mine, 0, 1), plane(mine, 1, 0), plane(mine, 1, 1)]
 
 
 def local(features, radial, neighbours, halo_lists, slab_counts, frame_labels, w_a, w_c, w_b, readout):
@@ -393,45 +427,48 @@
     where = jnp.stack([me, lax.rem(lax.axis_index(RING), 2).astype(jnp.int32)])
 
     half = (channels // 2, halo_lanes)
-    state, select, first, second = kernel_call(
+    state, select, first, second, neigh, weight = kernel_call(
         select_kernel,
-        (near((channels, lanes)), near((lanes, halo_lanes)), near(half), near(half)),
-        (where, features, halo_lists),
+        (
+            near((channels, lanes)),
+            near((lanes, halo_lanes)),
+            near(half),
+            near(half),
+            near(neighbours.shape, jnp.int32),
+            near(radial.shape),
+        ),
+        (where, features, halo_lists, neighbours, radial),
         scratch=[
             pltpu.VMEM(features.shape, BF16),
             pltpu.VMEM(halo_lists.shape, jnp.int32),
-            pltpu.SemaphoreType.DMA((2,)),
+            pltpu.SemaphoreType.DMA((4,)),
         ],
         smem=1,
-        far=2,
+        far=4,
     )
     second, first = swapped(second, 1), swapped(first, 0)
     weights = [near((layers, channels, hidden)), near((layers, channels, hidden)), near((layers, hidden, channels))]
-    turned = [near((layers, hidden, channels)), near((layers, hidden, channels)), near((layers, channels, hidden))]
+    turned = near((hidden, channels))
     onehot_type = near((frames, rows, degree * beads))
-    onehot, edge, wa, wc, wb, wta, wtc, wtb, own, cross, live, sign, wide = kernel_call(
+    onehot, edge, wa, wc, wb, readout_near, wta, wtb, own, cross = kernel_call(
         functools.partial(prepare_kernel, halo),
         (
             onehot_type,
             near((frames, degree, SUB, beads)),
             *weights,
-            *turned,
+            near(readout.shape, F32),
+            turned,
+            turned,
             near((hidden, lanes)),
             near((hidden, lanes), F32),
-            near((1, lanes), F32),
-            near((1, lanes), F32),
-            near((channels, beads), F32),
         ),
-        (where, slab_counts, frame_labels, neighbours, radial, w_a, w_c, w_b, readout, state),
+        (where, w_a, w_c, w_b, readout, state, neigh, weight),
         scratch=[
             pltpu.VMEM(neighbours.shape, jnp.int32),
-            pltpu.VMEM(radial.shape, BF16),
-            pltpu.VMEM(readout.shape, F32),
-            pltpu.VMEM(neighbours.shape, jnp.int32),
-            pltpu.SemaphoreType.DMA((6,)),
+            pltpu.SemaphoreType.DMA((4,)),
         ],
-        smem=3,
-        far=6,
+        smem=1,
+        far=4,
         flops=2 * 10**9,
     )
     totals = (hidden, lanes)
@@ -450,6 +487,13 @@
         (first, second, onehot, edge, wta, wtb, own, cross, state, select),
         scratch=[pltpu.VMEM(totals, F32)],
         flops=4 * 10**9,
+    )
+    wta, wtc, wtb, wide, live, sign = kernel_call(
+        later_kernel,
+        (turned, turned, turned, near((channels, beads), F32), near((1, lanes), F32), near((1, lanes), F32)),
+        (jnp.concatenate([slab_counts[:, 0], frame_labels]), first, wa, wc, wb, readout_near),
+        smem=1,
+        flops=10**8,
     )
     second, first = swapped(second, 1), swapped(first, 0)
     energy, grad_readout, cot, first, second, cot_own, cot_halo, cot_cross, halo1, gathered1, cot_low1 = kernel_call(
@@ -480,17 +524,19 @@
         smem=1,
         flops=10**9,
     )
+    upper_part = core_sum(upper_slots)
     lower_slots = kernel_call(
         lower_kernel,
         near((8, 3 * chunk, channels), F32),
         (
             where, first, second, select, cot_own, cot_cross, cot, wa, wc, wb,
-            onehot, slope0, slope_total0, state, halo0, gathered0,
+            onehot, slope0, slope_total0, state, halo0, gathered0, upper_slots,
         ),
         smem=1,
         flops=4 * 10**9,
     )
-    close, far = reduce_slots(jnp.concatenate([upper_slots, lower_slots], axis=1))
+    close = reduce_parts([upper_part, core_sum(lower_slots)])
+    far = partner(jnp.stack(close), "rep", 1)
     grad = jax.ShapeDtypeStruct((layers, channels, hidden), F32)
     grad_wa, grad_wc, grad_wb, grad_readout = kernel_call(
         finish_kernel,

time: 78.9 us -> 72.7 us (0.921)
  waiting for transfers between devices: 32.8 us -> 23.3 us
  starting transfers between devices: 22.1 us -> 26.2 us
  local copies, waits for them, and re-layouts: 1.44 us -> 0.31 us
    ppermute x6, waiting for transfers between devices: 13.7 us -> 9.36 us  [plane(): lax.ppermute(value, EVERY, [(s, s ^ flip) for s in range(rep * dom * tp)])]
    ppermute x6, waiting for transfers between devices: 8.84 us -> 4.75 us  [swapped(): return lax.ppermute(value, RING, pairs)]
    ppermute x6, starting transfers between devices: 10.4 us -> 14 us  [swapped(): return lax.ppermute(value, RING, pairs)]
    unnamed x3 -> x4, local copies, waits for them, and re-layouts: 1.4 us -> 0.01 us
    ppermute x5 -> x6, waiting for transfers between devices: 10.3 us -> 9.22 us  [partner(): lax.ppermute(value, axis, [(s, s ^ bits) for s in range(lax.axis_size(axi...]
    ppermute x5 -> x6, starting transfers between devices: 4.59 us -> 5.15 us  [partner(): lax.ppermute(value, axis, [(s, s ^ bits) for s in range(lax.axis_size(axi...]
    pallas_call x7 -> x8, Pallas kernels: 20.7 us -> 20.7 us  [kernel_call(): pl.pallas_call(body, out_shape=outs, in_specs=[pl.BlockSpec(memory_space=...]
  transfers between devices with their start and end apart: 17 -> 18, of which waited for: 14 -> 14; matrix products, arithmetic and copies ran while one was open for 1% -> 1% of each run, Pallas kernels for 6% -> 6%
where the time goes in v2:
time: 72.7 us; the launch traced here: 72.6 us
  starting transfers between devices  26.2 us (36%)
  waiting for transfers between devices  23.3 us (32%)
  Pallas kernels  20.7 us (28%)
  other arithmetic  1.01 us (1%)
  between operations  0.96 us (1%)
    pallas_call x8, Pallas kernels, kernel_call(): pl.pallas_call(body, out_shape=outs, in_specs=[pl.BlockSpec(memory_space=...  20.7 us
    ppermute x6, starting transfers between devices, swapped(): return lax.ppermute(value, RING, pairs)  14 us
    ppermute x6, waiting for transfers between devices, plane(): lax.ppermute(value, EVERY, [(s, s ^ flip) for s in range(rep * dom * tp)])  9.36 us
    ppermute x6, waiting for transfers between devices, partner(): lax.ppermute(value, axis, [(s, s ^ bits) for s in range(lax.axis_size(axi...  9.22 us
    ppermute x6, starting transfers between devices, plane(): lax.ppermute(value, EVERY, [(s, s ^ flip) for s in range(rep * dom * tp)])  7.11 us
    ppermute x6, starting transfers between devices, partner(): lax.ppermute(value, axis, [(s, s ^ bits) for s in range(lax.axis_size(axi...  5.15 us
    ppermute x6, waiting for transfers between devices, swapped(): return lax.ppermute(value, RING, pairs)  4.75 us
  transfers between devices with their start and end apart: 18, of which 14 were waited for; matrix products, arithmetic and copies ran while one was open for 1% of the time, Pallas kernels for 6%

profile of v2, /device:TPU:0, one launch (start us, length us, event | category | flops | bytes accessed | tf_op | source)
XLA Modules:
  0.0 72.6 jit_solution(1005088321750463532)
XLA Ops:
  0.7 1.8 %shard_map.137 = (bf16[256,256]{1,0:T(8,128)(2,1)S(1)}, bf16[256,128]{1,0:T(8,128)(2,1)S(1)}, bf16[128,128]{1,0:T(8,128)(2,1)S(1)}, bf16[128,128]{1,0:T(8,128)(2...) custom-call(s32[2]{0:T(128)S(1)} %pad_add_fusion.where_ref.me_ref, bf16[2,128,256]{2,1,0:T(8,128)(2,1)} %feat_hbm.1, ...), custom_call_target="tpu_custom_call" | custom-call | tf_op jit(solution)/shard_map/pallas_call | solution.py:332
  2.5 3.0 %collective-permute-start = (bf16[128,128]{1,0:T(8,128)(2,1)S(1)}, bf16[128,128]{1,0:T(8,128)(2,1)S(1)}, u32[]{:S(2)}, u32[]{:S(2)}) collective-permute-start(bf16[128,128]{1,0:T(8,128)(2,1)S(1)} %get-tuple-element.49), channel_id=1, source_target_pairs={{0,1},{1,0},{2,3},{3,2},{4,5},{5,4},{6,7},{7,6},{8,9},{9,8},{10,11... | collective-permute-start | bytes 98312 | tf_op jit(solution)/shard_map/ppermute | solution.py:355
  5.6 3.5 %collective-permute-start.1 = (bf16[128,128]{1,0:T(8,128)(2,1)S(1)}, bf16[128,128]{1,0:T(8,128)(2,1)S(1)}, u32[]{:S(2)}, u32[]{:S(2)}) collective-permute-start(bf16[128,128]{1,0:T(8,128)(2,1)S(1)} %get-tuple-element.50), channel_id=1, source_target_pairs={{0,7},{1,2},{2,1},{3,4},{4,3},{5,6},{6,5},{7,0},{8,15},{9,10},{10,... | collective-permute-start | bytes 98312 | tf_op jit(solution)/shard_map/ppermute | solution.py:355
  9.1 2.7 %shard_map.138 = (bf16[2,256,4096]{2,1,0:T(8,128)(2,1)S(1)}, bf16[2,32,16,128]{3,2,1,0:T(8,128)(2,1)S(1)}, bf16[2,256,256]{2,1,0:T(8,128)(2,1)S(1)}, bf16[2,256,...) custom-call(s32[2]{0:T(128)S(1)} %pad_add_fusion.where_ref.me_ref, ...), custom_call_target="tpu_custom_call" | custom-call | flops 2000000000 | tf_op jit(solution)/shard_map/pallas_call | solution.py:332
  12.2 4.0 %shard_map.139 = (bf16[256,256]{1,0:T(8,128)(2,1)S(1)}, bf16[128,128]{1,0:T(8,128)(2,1)S(1)}, bf16[128,128]{1,0:T(8,128)(2,1)S(1)}, bf16[256,128]{1,0:T(8,128)(2...) custom-call(bf16[128,128]{1,0:T(8,128)(2,1)S(1)} %collective-permute-done.hf_ref, ...), custom_call_target="tpu_custom_call" | custom-call | flops 4000000000 | tf_op jit(solution)/shard_map/pallas_call | solution.py:332
  16.3 3.6 %collective-permute-start.3 = (bf16[128,128]{1,0:T(8,128)(2,1)S(1)}, bf16[128,128]{1,0:T(8,128)(2,1)S(1)}, u32[]{:S(2)}, u32[]{:S(2)}) collective-permute-start(bf16[128,128]{1,0:T(8,128)(2,1)S(1)} %get-tuple-element.63), channel_id=1, source_target_pairs={{0,7},{1,2},{2,1},{3,4},{4,3},{5,6},{6,5},{7,0},{8,15},{9,10},{10,... | collective-permute-start | bytes 98312 | tf_op jit(solution)/shard_map/ppermute | solution.py:355
  20.7 2.2 %collective-permute-done.3.hs_ref = bf16[128,128]{1,0:T(8,128)(2,1)S(1)} collective-permute-done((bf16[128,128]{1,0:T(8,128)(2,1)S(1)}, bf16[128,128]{1,0:T(8,128)(2,1)S(1)}, u32[]{:S(2)}, u32[]{:S(2)}) %collective-permute-start.3) | collective-permute-done | bytes 32800 | tf_op jit(solution)/shard_map/ppermute | solution.py:355
  23.0 5.8 %shard_map.141 = (f32[2,128]{1,0:T(2,128)}, f32[16,256]{1,0:T(8,128)S(1)}, f32[256,256]{1,0:T(8,128)S(1)}, bf16[128,128]{1,0:T(8,128)(2,1)S(1)}, bf16[128,128]{1...) custom-call(bf16[128,128]{1,0:T(8,128)(2,1)S(1)} %collective-permute, ...), custom_call_target="tpu_custom_call" | custom-call | flops 6000000000 | tf_op jit(solution)/shard_map/pallas_call | solution.py:332
  28.9 3.5 %collective-permute-start.6 = (bf16[128,128]{1,0:T(8,128)(2,1)S(1)}, bf16[128,128]{1,0:T(8,128)(2,1)S(1)}, u32[]{:S(2)}, u32[]{:S(2)}) collective-permute-start(bf16[128,128]{1,0:T(8,128)(2,1)S(1)} %get-tuple-element.82), channel_id=1, source_target_pairs={{0,7},{1,2},{2,1},{3,4},{4,3},{5,6},{6,5},{7,0},{8,15},{9,10},{10,... | collective-permute-start | bytes 98312 | tf_op jit(solution)/shard_map/ppermute | solution.py:355
  33.3 2.2 %collective-permute-done.6.bs_ref = bf16[128,128]{1,0:T(8,128)(2,1)S(1)} collective-permute-done((bf16[128,128]{1,0:T(8,128)(2,1)S(1)}, bf16[128,128]{1,0:T(8,128)(2,1)S(1)}, u32[]{:S(2)}, u32[]{:S(2)}) %collective-permute-start.6) | collective-permute-done | bytes 32800 | tf_op jit(solution)/shard_map/ppermute | solution.py:355
  35.5 3.0 %shard_map.143 = f32[8,96,256]{2,1,0:T(8,128)S(1)} custom-call(s32[2]{0:T(128)S(1)} %pad_add_fusion.where_ref.me_ref, bf16[128,128]{1,0:T(8,128)(2,1)S(1)} %collective-permute-done.5.bf_ref, bf16[128,128]{1,0:T(8,128)(2,1)S(1)} %collective-permute-done.6.bs_ref, bf16[256,128]{1,0:T(8,128)(2,1)S(1)} %get-tuple-element.60.select_ref, ...), custom_call_target="tpu_custom_call" | custom-call | flops 4000000000 | tf_op jit(solution)/shard_map/pallas_call | solution.py:332
  41.8 1.5 %collective-permute-start.9 = (f16[208,256]{1,0:T(8,128)(2,1)S(1)}, f16[208,256]{1,0:T(8,128)(2,1)S(1)}, u32[]{:S(2)}, u32[]{:S(2)}) collective-permute-start(f16[208,256]{1,0:T(8,128)(2,1)S(1)} %get-tuple-element.94), channel_id=1, source_target_pairs={{0,16},{1,17},{2,18},{3,19},{4,20},{5,21},{6,22},{7,23},{8,24},{9,... | collective-permute-start | bytes 319496 | tf_op jit(solution)/shard_map/ppermute | solution.py:394
  43.3 1.9 %collective-permute-start.10 = (f16[208,256]{1,0:T(8,128)(2,1)S(1)}, f16[208,256]{1,0:T(8,128)(2,1)S(1)}, u32[]{:S(2)}, u32[]{:S(2)}) collective-permute-start(f16[208,256]{1,0:T(8,128)(2,1)S(1)} %get-tuple-element.93), channel_id=1, source_target_pairs={{0,17},{1,16},{2,19},{3,18},{4,21},{5,20},{6,23},{7,22},{8,25},{9,... | collective-permute-start | bytes 319496 | tf_op jit(solution)/shard_map/ppermute | solution.py:394
  45.2 1.4 %collective-permute-done.8 = f16[208,256]{1,0:T(8,128)(2,1)S(1)} collective-permute-done((f16[208,256]{1,0:T(8,128)(2,1)S(1)}, f16[208,256]{1,0:T(8,128)(2,1)S(1)}, u32[]{:S(2)}, u32[]{:S(2)}) %collective-permute-start.8) | collective-permute-done | bytes 106528 | tf_op jit(solution)/shard_map/ppermute | solution.py:394
  46.9 3.4 %collective-permute-done.10 = f16[208,256]{1,0:T(8,128)(2,1)S(1)} collective-permute-done((f16[208,256]{1,0:T(8,128)(2,1)S(1)}, f16[208,256]{1,0:T(8,128)(2,1)S(1)}, u32[]{:S(2)}, u32[]{:S(2)}) %collective-permute-start.10) | collective-permute-done | bytes 106528 | tf_op jit(solution)/shard_map/ppermute | solution.py:394
  50.5 2.8 %collective-permute-start.13 = (bf16[208,256]{1,0:T(8,128)(2,1)S(1)}, bf16[208,256]{1,0:T(8,128)(2,1)S(1)}, u32[]{:S(2)}, u32[]{:S(2)}) collective-permute-start(bf16[208,256]{1,0:T(8,128)(2,1)S(1)} %fusion.4), channel_id=1, source_target_pairs={{0,6},{2,4},{4,2},{6,0},{1,7},{3,5},{5,3},{7,1},{8,14},{10,12},{12... | collective-permute-start | bytes 319496 | tf_op jit(solution)/shard_map/ppermute | solution.py:359
  53.3 1.7 %collective-permute-start.11 = (bf16[208,256]{1,0:T(8,128)(2,1)S(1)}, bf16[208,256]{1,0:T(8,128)(2,1)S(1)}, u32[]{:S(2)}, u32[]{:S(2)}) collective-permute-start(bf16[208,256]{1,0:T(8,128)(2,1)S(1)} %fusion.4), channel_id=1, source_target_pairs={{0,2},{2,0},{4,6},{6,4},{1,3},{3,1},{5,7},{7,5},{8,10},{10,8},{12,... | collective-permute-start | bytes 319496 | tf_op jit(solution)/shard_map/ppermute | solution.py:359
  54.9 3.4 %collective-permute-done.13 = bf16[208,256]{1,0:T(8,128)(2,1)S(1)} collective-permute-done((bf16[208,256]{1,0:T(8,128)(2,1)S(1)}, bf16[208,256]{1,0:T(8,128)(2,1)S(1)}, u32[]{:S(2)}, u32[]{:S(2)}) %collective-permute-start.13) | collective-permute-done | bytes 106528 | tf_op jit(solution)/shard_map/ppermute | solution.py:359
  58.3 2.5 %collective-permute-done.12 = bf16[208,256]{1,0:T(8,128)(2,1)S(1)} collective-permute-done((bf16[208,256]{1,0:T(8,128)(2,1)S(1)}, bf16[208,256]{1,0:T(8,128)(2,1)S(1)}, u32[]{:S(2)}, u32[]{:S(2)}) %collective-permute-start.12) | collective-permute-done | bytes 106528 | tf_op jit(solution)/shard_map/ppermute | solution.py:359
  61.8 1.5 %collective-permute-start.15 = (bf16[208,256]{1,0:T(8,128)(2,1)S(1)}, bf16[208,256]{1,0:T(8,128)(2,1)S(1)}, u32[]{:S(2)}, u32[]{:S(2)}) collective-permute-start(bf16[208,256]{1,0:T(8,128)(2,1)S(1)} %add_convert_fusion.refs_0_), channel_id=1, source_target_pairs={{0,16},{1,17},{2,18},{3,19},{4,20},{5,21},{6,22},{7,23},{8,24},{9,... | collective-permute-start | bytes 319496 | tf_op jit(solution)/shard_map/ppermute | solution.py:394
  64.4 1.8 %collective-permute-done.14.refs_1_ = bf16[208,256]{1,0:T(8,128)(2,1)S(1)} collective-permute-done((bf16[208,256]{1,0:T(8,128)(2,1)S(1)}, bf16[208,256]{1,0:T(8,128)(2,1)S(1)}, u32[]{:S(2)}, u32[]{:S(2)}) %collective-permute-start.14) | collective-permute-done | bytes 106528 | tf_op jit(solution)/shard_map/ppermute | solution.py:394
  67.5 1.4 %collective-permute-done.16.refs_3_ = bf16[208,256]{1,0:T(8,128)(2,1)S(1)} collective-permute-done((bf16[208,256]{1,0:T(8,128)(2,1)S(1)}, bf16[208,256]{1,0:T(8,128)(2,1)S(1)}, u32[]{:S(2)}, u32[]{:S(2)}) %collective-permute-start.16) | collective-permute-done | bytes 106528 | tf_op jit(solution)/shard_map/ppermute | solution.py:394
  69.0 1.8 %collective-permute-done.17.refs_4_ = bf16[4,208,256]{2,1,0:T(8,128)(2,1)S(1)} collective-permute-done((bf16[4,208,256]{2,1,0:T(8,128)(2,1)S(1)}, bf16[4,208,256]{2,1,0:T(8,128)(2,1)S(1)}, u32[]{:S(2)}, u32[]{:S(2)}) %collective-permute-start.17) | collective-permute-done | bytes 426016 | tf_op jit(solution)/shard_map/ppermute | solution.py:359
  70.8 1.8 %shard_map.144 = (f32[2,256,256]{2,1,0:T(8,128)}, f32[2,256,256]{2,1,0:T(8,128)}, f32[2,256,256]{2,1,0:T(8,128)}, f32[256]{0:T(256)}) custom-call(s32[2]{0:T(128)S(1)} %pad_add_fusion.where_ref.me_ref, bf16[208,256]{1,0:T(8,128)(2,1)S(1)} %add_convert_fusion.refs_0_, bf16[208,256]{1,0:T(8,128)(2,1)S(1)} %collective-permute-done.14.refs_1_, ...), custom_call_target="tpu_custom_call" | custom-call | tf_op jit(solution)/shard_map/pallas_call | solution.py:332
  (61 shorter events, 9.4 us)
Async XLA Ops:
  2.5 9.3 %collective-permute-start = (bf16[128,128]{1,0:T(8,128)(2,1)S(1)}, bf16[128,128]{1,0:T(8,128)(2,1)S(1)}, u32[]{:S(2)}, u32[]{:S(2)}) collective-permute-start(bf16[128,128]{1,0:T(8,128)(2,1)S(1)} %get-tuple-element.49), channel_id=1, source_target_pairs={{0,1},{1,0},{2,3},{3,2},{4,5},{5,4},{6,7},{7,6},{8,9},{9,8},{10,11... | collective-permute-start | bytes 98312 | tf_op jit(solution)/shard_map/ppermute | solution.py:355
  5.6 6.6 %collective-permute-start.1 = (bf16[128,128]{1,0:T(8,128)(2,1)S(1)}, bf16[128,128]{1,0:T(8,128)(2,1)S(1)}, u32[]{:S(2)}, u32[]{:S(2)}) collective-permute-start(bf16[128,128]{1,0:T(8,128)(2,1)S(1)} %get-tuple-element.50), channel_id=1, source_target_pairs={{0,7},{1,2},{2,1},{3,4},{4,3},{5,6},{6,5},{7,0},{8,15},{9,10},{10,... | collective-permute-start | bytes 98312 | tf_op jit(solution)/shard_map/ppermute | solution.py:355
  12.2 7.7 %copy-start = (s32[2]{0:T(128)S(1)}, s32[2]{0:T(128)}, u32[]{:S(2)}) copy-start(s32[2]{0:T(128)} %param.15) | copy-start | bytes 28
  12.2 7.7 %copy-start.1 = (s32[2,1]{0,1:T(1,128)S(1)}, s32[2,1]{0,1:T(1,128)}, u32[]{:S(2)}) copy-start(s32[2,1]{0,1:T(1,128)} %param.14) | copy-start | bytes 28
  16.2 4.5 %collective-permute-start.2 = (bf16[128,128]{1,0:T(8,128)(2,1)S(1)}, bf16[128,128]{1,0:T(8,128)(2,1)S(1)}, u32[]{:S(2)}, u32[]{:S(2)}) collective-permute-start(bf16[128,128]{1,0:T(8,128)(2,1)S(1)} %get-tuple-element.62._after), channel_id=1, source_target_pairs={{0,1},{1,0},{2,3},{3,2},{4,5},{5,4},{6,7},{7,6},{8,9},{9,8},{10,11... | collective-permute-start | bytes 98312 | tf_op jit(solution)/shard_map/ppermute | solution.py:355
  16.3 6.7 %collective-permute-start.3 = (bf16[128,128]{1,0:T(8,128)(2,1)S(1)}, bf16[128,128]{1,0:T(8,128)(2,1)S(1)}, u32[]{:S(2)}, u32[]{:S(2)}) collective-permute-start(bf16[128,128]{1,0:T(8,128)(2,1)S(1)} %get-tuple-element.63), channel_id=1, source_target_pairs={{0,7},{1,2},{2,1},{3,4},{4,3},{5,6},{6,5},{7,0},{8,15},{9,10},{10,... | collective-permute-start | bytes 98312 | tf_op jit(solution)/shard_map/ppermute | solution.py:355
  28.7 4.6 %collective-permute-start.5 = (bf16[128,128]{1,0:T(8,128)(2,1)S(1)}, bf16[128,128]{1,0:T(8,128)(2,1)S(1)}, u32[]{:S(2)}, u32[]{:S(2)}) collective-permute-start(bf16[128,128]{1,0:T(8,128)(2,1)S(1)} %get-tuple-element.81), channel_id=1, source_target_pairs={{0,1},{1,0},{2,3},{3,2},{4,5},{5,4},{6,7},{7,6},{8,9},{9,8},{10,11... | collective-permute-start | bytes 98312 | tf_op jit(solution)/shard_map/ppermute | solution.py:355
  28.9 6.6 %collective-permute-start.6 = (bf16[128,128]{1,0:T(8,128)(2,1)S(1)}, bf16[128,128]{1,0:T(8,128)(2,1)S(1)}, u32[]{:S(2)}, u32[]{:S(2)}) collective-permute-start(bf16[128,128]{1,0:T(8,128)(2,1)S(1)} %get-tuple-element.82), channel_id=1, source_target_pairs={{0,7},{1,2},{2,1},{3,4},{4,3},{5,6},{6,5},{7,0},{8,15},{9,10},{10,... | collective-permute-start | bytes 98312 | tf_op jit(solution)/shard_map/ppermute | solution.py:355
  38.6 1.8 %collective-permute-start.7 = (f32[4,96,256]{2,1,0:T(8,128)S(1)}, f32[4,96,256]{2,1,0:T(8,128)S(1)}, u32[]{:S(2)}, u32[]{:S(2)}) collective-permute-start(f32[4,96,256]{2,1,0:T(8,128)S(1)} %slice.115), channel_id=1, source_target_pairs={{0,8},{8,0},{16,24},{24,16},{1,9},{9,1},{17,25},{25,17},{2,10},{10... | collective-permute-start | bytes 1179656 | tf_op jit(solution)/shard_map/ppermute | solution.py:359
  38.7 2.3 %collective-permute-start.4 = (f32[4,112,256]{2,1,0:T(8,128)S(1)}, f32[4,112,256]{2,1,0:T(8,128)S(1)}, u32[]{:S(2)}, u32[]{:S(2)}) collective-permute-start(f32[4,112,256]{2,1,0:T(8,128)S(1)} %slice.113), channel_id=1, source_target_pairs={{0,8},{8,0},{16,24},{24,16},{1,9},{9,1},{17,25},{25,17},{2,10},{10... | collective-permute-start | bytes 1376264 | tf_op jit(solution)/shard_map/ppermute | solution.py:359
  41.6 5.1 %collective-permute-start.8 = (f16[208,256]{1,0:T(8,128)(2,1)S(1)}, f16[208,256]{1,0:T(8,128)(2,1)S(1)}, u32[]{:S(2)}, u32[]{:S(2)}) collective-permute-start(f16[208,256]{1,0:T(8,128)(2,1)S(1)} %get-tuple-element.95), channel_id=1, source_target_pairs={{0,1},{1,0},{2,3},{3,2},{4,5},{5,4},{6,7},{7,6},{8,9},{9,8},{10,11... | collective-permute-start | bytes 319496 | tf_op jit(solution)/shard_map/ppermute | solution.py:394
  41.8 5.0 %collective-permute-start.9 = (f16[208,256]{1,0:T(8,128)(2,1)S(1)}, f16[208,256]{1,0:T(8,128)(2,1)S(1)}, u32[]{:S(2)}, u32[]{:S(2)}) collective-permute-start(f16[208,256]{1,0:T(8,128)(2,1)S(1)} %get-tuple-element.94), channel_id=1, source_target_pairs={{0,16},{1,17},{2,18},{3,19},{4,20},{5,21},{6,22},{7,23},{8,24},{9,... | collective-permute-start | bytes 319496 | tf_op jit(solution)/shard_map/ppermute | solution.py:394
  43.3 6.9 %collective-permute-start.10 = (f16[208,256]{1,0:T(8,128)(2,1)S(1)}, f16[208,256]{1,0:T(8,128)(2,1)S(1)}, u32[]{:S(2)}, u32[]{:S(2)}) collective-permute-start(f16[208,256]{1,0:T(8,128)(2,1)S(1)} %get-tuple-element.93), channel_id=1, source_target_pairs={{0,17},{1,16},{2,19},{3,18},{4,21},{5,20},{6,23},{7,22},{8,25},{9,... | collective-permute-start | bytes 319496 | tf_op jit(solution)/shard_map/ppermute | solution.py:394
  50.5 7.8 %collective-permute-start.13 = (bf16[208,256]{1,0:T(8,128)(2,1)S(1)}, bf16[208,256]{1,0:T(8,128)(2,1)S(1)}, u32[]{:S(2)}, u32[]{:S(2)}) collective-permute-start(bf16[208,256]{1,0:T(8,128)(2,1)S(1)} %fusion.4), channel_id=1, source_target_pairs={{0,6},{2,4},{4,2},{6,0},{1,7},{3,5},{5,3},{7,1},{8,14},{10,12},{12... | collective-permute-start | bytes 319496 | tf_op jit(solution)/shard_map/ppermute | solution.py:359
  53.3 7.5 %collective-permute-start.12 = (bf16[208,256]{1,0:T(8,128)(2,1)S(1)}, bf16[208,256]{1,0:T(8,128)(2,1)S(1)}, u32[]{:S(2)}, u32[]{:S(2)}) collective-permute-start(bf16[208,256]{1,0:T(8,128)(2,1)S(1)} %fusion.4), channel_id=1, source_target_pairs={{0,4},{2,6},{4,0},{6,2},{1,5},{3,7},{5,1},{7,3},{8,12},{10,14},{12... | collective-permute-start | bytes 319496 | tf_op jit(solution)/shard_map/ppermute | solution.py:359
  53.3 7.5 %collective-permute-start.11 = (bf16[208,256]{1,0:T(8,128)(2,1)S(1)}, bf16[208,256]{1,0:T(8,128)(2,1)S(1)}, u32[]{:S(2)}, u32[]{:S(2)}) collective-permute-start(bf16[208,256]{1,0:T(8,128)(2,1)S(1)} %fusion.4), channel_id=1, source_target_pairs={{0,2},{2,0},{4,6},{6,4},{1,3},{3,1},{5,7},{7,5},{8,10},{10,8},{12,... | collective-permute-start | bytes 319496 | tf_op jit(solution)/shard_map/ppermute | solution.py:359
  60.8 5.4 %collective-permute-start.14 = (bf16[208,256]{1,0:T(8,128)(2,1)S(1)}, bf16[208,256]{1,0:T(8,128)(2,1)S(1)}, u32[]{:S(2)}, u32[]{:S(2)}) collective-permute-start(bf16[208,256]{1,0:T(8,128)(2,1)S(1)} %add_convert_fusion.refs_0_), channel_id=1, source_target_pairs={{0,1},{1,0},{2,3},{3,2},{4,5},{5,4},{6,7},{7,6},{8,9},{9,8},{10,11... | collective-permute-start | bytes 319496 | tf_op jit(solution)/shard_map/ppermute | solution.py:394
  61.8 5.7 %collective-permute-start.15 = (bf16[208,256]{1,0:T(8,128)(2,1)S(1)}, bf16[208,256]{1,0:T(8,128)(2,1)S(1)}, u32[]{:S(2)}, u32[]{:S(2)}) collective-permute-start(bf16[208,256]{1,0:T(8,128)(2,1)S(1)} %add_convert_fusion.refs_0_), channel_id=1, source_target_pairs={{0,16},{1,17},{2,18},{3,19},{4,20},{5,21},{6,22},{7,23},{8,24},{9,... | collective-permute-start | bytes 319496 | tf_op jit(solution)/shard_map/ppermute | solution.py:394
  63.3 5.6 %collective-permute-start.16 = (bf16[208,256]{1,0:T(8,128)(2,1)S(1)}, bf16[208,256]{1,0:T(8,128)(2,1)S(1)}, u32[]{:S(2)}, u32[]{:S(2)}) collective-permute-start(bf16[208,256]{1,0:T(8,128)(2,1)S(1)} %add_convert_fusion.refs_0_), channel_id=1, source_target_pairs={{0,17},{1,16},{2,19},{3,18},{4,21},{5,20},{6,23},{7,22},{8,25},{9,... | collective-permute-start | bytes 319496 | tf_op jit(solution)/shard_map/ppermute | solution.py:394
  69.0 1.8 %collective-permute-start.17 = (bf16[4,208,256]{2,1,0:T(8,128)(2,1)S(1)}, bf16[4,208,256]{2,1,0:T(8,128)(2,1)S(1)}, u32[]{:S(2)}, u32[]{:S(2)}) collective-permute-start(bf16[4,208,256]{2,1,0:T(8,128)(2,1)S(1)} %pad_maximum_fusion.1), channel_id=1, source_target_pairs={{0,8},{8,0},{16,24},{24,16},{1,9},{9,1},{17,25},{25,17},{2,10},{10... | collective-permute-start | bytes 1277960 | tf_op jit(solution)/shard_map/ppermute | solution.py:359

commit v3 on v2

--- a/solution.py
+++ b/solution.py
@@ -11,6 +11,7 @@
 BF16, F16, F32 = jnp.bfloat16, jnp.float16, jnp.float32
 MEBI = 1024 * 1024
 SUB = 16
+TAIL = 8
 RING = ("dom", "tp")
 EVERY = ("rep", "dom", "tp")
 
@@ -130,10 +131,14 @@
 
 
 def later_kernel(
-    frame_ref, _after, wa_ref, wc_ref, wb_ref, readout_ref, wta_ref, wtc_ref, wtb_ref, wide_ref, live_ref, sign_ref
-):
-    for source, target in ((wa_ref, wta_ref), (wc_ref, wtc_ref), (wb_ref, wtb_ref)):
-        target[...] = source[source.shape[0] - 1].astype(F32).T.astype(BF16)
+    frame_ref, state_ref, wa_ref, wc_ref, wb_ref, readout_ref, wta_ref, wtb_ref, own_ref, cross_ref, wide_ref, live_ref, sign_ref
+):
+    last = wa_ref.shape[0] - 1
+    turned_a, turned_c, turned_b = (ref[last].astype(F32).T.astype(BF16) for ref in (wa_ref, wc_ref, wb_ref))
+    wta_ref[...] = turned_a
+    wtb_ref[...] = turned_b
+    own_ref[...] = mul(turned_a, state_ref[...]).astype(BF16)
+    cross_ref[...] = mul(turned_c, state_ref[...])
     wide = readout_ref[...].reshape(1, -1)
     beads = wide_ref.shape[1]
     wide_ref[...] = jnp.broadcast_to(wide, (beads, wide.shape[1])).T
@@ -162,15 +167,16 @@
             at = slice(index * group * beads, (index + 1) * group * beads)
             half = (mul(table, onehot_ref[frame, :, at]) + wide_cross).astype(BF16)
             turn = jnp.tanh(half)
-            act = half + half * turn
-            slope = (1 + turn) + half * (1 - turn * turn)
+            rise = 1 + turn
+            rest = 1 + half * (1 - turn)
             act_sum, slope_sum = None, None
             kept = []
             for part in range(group):
                 here = slice(part * beads, (part + 1) * beads)
                 weight = edge_ref[frame, index * group + part]
-                a = (act[:, here].reshape(blocks, SUB, beads) * weight[None]).reshape(hidden, beads)
-                s = (slope[:, here].reshape(blocks, SUB, beads) * (weight * jnp.asarray(0.5, BF16))[None]).reshape(hidden, beads)
+                weighted = (rise[:, here].reshape(blocks, SUB, beads) * weight[None]).reshape(hidden, beads)
+                a = half[:, here] * weighted
+                s = rest[:, here] * weighted
                 kept.append(s)
                 act_sum = a if act_sum is None else act_sum + a
                 slope_sum = s if slope_sum is None else slope_sum + s
@@ -196,7 +202,7 @@
 
 
 def first_kernel(
-    hf_ref, hs_ref, onehot_ref, edge_ref, wta_ref, wtb_ref, own_ref, cross_ref, state_ref, select_ref,
+    hs_ref, hf_ref, onehot_ref, edge_ref, wta_ref, wtb_ref, own_ref, cross_ref, state_ref, select_ref,
     next_ref, first_ref, second_ref, halo_ref, gathered_ref, slope_ref, slope_total_ref,
     total_ref,
 ):
@@ -213,7 +219,7 @@
 
 def middle_kernel(
     scale,
-    hf_ref, hs_ref, onehot_ref, edge_ref, wta_ref, wtc_ref, wtb_ref, wb_ref, state_ref, live_ref, sign_ref, readout_ref,
+    hs_ref, hf_ref, onehot_ref, edge_ref, wta_ref, wtb_ref, wb_ref, own_ref, cross_ref, state_ref, live_ref, sign_ref, readout_ref,
     energy_ref, grad_readout_ref, cot_ref, first_ref, second_ref, cot_own_ref, cot_halo_ref, cot_cross_ref,
     halo_ref, gathered_ref, cot_low_ref,
     slope_ref, slope_total_ref, total_ref,
@@ -224,10 +230,8 @@
     halo = read_halo(hf_ref, hs_ref)
     halo_ref[...] = halo
     state = state_ref[...]
-    own = mul(wta_ref[...], state).astype(BF16)
-    cross = mul(wtc_ref[...], state)
     halo_rows = mul(wta_ref[...], halo).astype(BF16)
-    edges(onehot_ref, edge_ref, own, halo_rows, cross, slope_ref, total_ref, slope_total_ref)
+    edges(onehot_ref, edge_ref, own_ref[...], halo_rows, cross_ref[...], slope_ref, total_ref, slope_total_ref)
     gathered = total_ref[...].astype(BF16)
     gathered_ref[...] = gathered
     final = (state.astype(F32) + mul(wtb_ref[...], gathered)).astype(BF16).astype(F32)
@@ -245,7 +249,7 @@
     cot_ref[...] = cot
     cot_low = cot.astype(BF16)
     cot_low_ref[...] = cot_low
-    cot_gathered = mul(wb_ref[last], cot_low)
+    cot_gathered = mul(wb_ref[last], cot_low) * 0.5
     cot_cross_ref[...] = (cot_gathered * slope_total_ref[...]).astype(BF16)
     cot_gathered = cot_gathered.astype(BF16)
     cot_halo = None
@@ -257,45 +261,48 @@
     cot_halo_ref[...] = cot_halo.astype(BF16)
 
 
-def put_slots(slots_ref, me, grads, base=0):
+def put_slots(slots_ref, me, grads):
     slots = slots_ref.shape[0]
     rows = grads[0].shape[0] // slots
     for chunk in range(slots):
         slot = jnp.bitwise_xor(me, chunk)
         for number, grad in enumerate(grads):
-            start = base + number * rows
+            start = number * rows
             slots_ref[slot, start : start + rows, :] = grad[chunk * rows : (chunk + 1) * rows]
 
 
 def upper_grads_kernel(
-    me_ref, state_ref, halo_ref, gathered_ref, cot_low_ref, cot_own_ref, cot_halo_ref, cot_cross_ref, grad_readout_ref, slots_ref
+    me_ref, state_ref, halo_ref, gathered_ref, cot_low_ref, cot_own_ref, cot_halo_ref, cot_cross_ref, grad_readout_ref,
+    cot_ref, wc_ref,
+    slots_ref, base_ref,
 ):
     me = me_ref[0]
     state = state_ref[...]
     grad_a = mul_nt(state, cot_own_ref[...].astype(BF16)) + mul_nt(halo_ref[...], cot_halo_ref[...])
     grad_c = mul_nt(state, cot_cross_ref[...])
     grad_b = mul_nt(gathered_ref[...], cot_low_ref[...])
-    row = lax.broadcasted_iota(jnp.int32, (SUB, slots_ref.shape[2]), 0)
-    head = jnp.where(row == 0, grad_readout_ref[...], 0.0)
+    row = lax.broadcasted_iota(jnp.int32, (TAIL, slots_ref.shape[2]), 0)
+    tail = jnp.where(row == 0, grad_readout_ref[:TAIL], 0.0)
     for slot in range(slots_ref.shape[0]):
-        slots_ref[slot, :SUB, :] = head
-    put_slots(slots_ref, me, [grad_a, grad_c, grad_b], SUB)
+        slots_ref[slot, slots_ref.shape[1] - TAIL :, :] = tail
+    put_slots(slots_ref, me, [grad_a, grad_c, grad_b])
+    base_ref[...] = cot_ref[...] + mul(wc_ref[1], cot_cross_ref[...])
 
 
 def lower_kernel(
-    me_ref, bf_ref, bs_ref, select_ref, cot_own_ref, cot_cross_ref, cot_ref, wa_ref, wc_ref, wb_ref,
-    onehot_ref, slope_ref, slope_total_ref, state_ref, halo_ref, gathered_ref, _after,
+    me_ref, bs_ref, bf_ref, select_ref, cot_own_ref, cot_ref, wa_ref, wb_ref,
+    onehot_ref, slope_ref, slope_total_ref, state_ref, halo_ref, gathered_ref,
     slots_ref,
 ):
     frames = onehot_ref.shape[0]
     beads = cot_ref.shape[1] // frames
     back = read_halo(bf_ref, bs_ref)
     cot_own = (cot_own_ref[...] + mul_nt(back, select_ref[...])).astype(BF16)
-    cot = cot_ref[...] + mul(wa_ref[1], cot_own) + mul(wc_ref[1], cot_cross_ref[...])
+    cot = cot_ref[...] + mul(wa_ref[1], cot_own)
     cot_low = cot.astype(BF16)
     state = state_ref[...]
     grad_b = mul_nt(gathered_ref[...], cot_low)
-    cot_gathered = mul(wb_ref[0], cot_low)
+    cot_gathered = mul(wb_ref[0], cot_low) * 0.5
     grad_c = mul_nt(state, (cot_gathered * slope_total_ref[...]).astype(BF16))
     cot_gathered = cot_gathered.astype(BF16)
     cot_halo, grad_a = None, None
@@ -313,16 +320,16 @@
     *near, far, wa_ref, wc_ref, wb_ref, readout_ref = refs
     me = me_ref[0]
     count = len(near)
-    rows = (far.shape[1] - SUB) // 6
+    rows = (far.shape[1] - TAIL) // 6
     total = jnp.zeros(readout_ref.shape, F32)
     for slot in range(2 * count):
-        source = near[slot] if slot < count else far.at[slot - count]
+        source = near[count - 1 - slot] if slot < count else far.at[2 * count - 1 - slot]
         chunk = jnp.bitwise_xor(me, slot)
         place = pl.ds(pl.multiple_of(chunk * rows, rows), rows)
-        for layer, base in ((1, SUB), (0, SUB + 3 * rows)):
+        for layer, base in ((0, 0), (1, 3 * rows)):
             for number, ref in enumerate((wa_ref, wc_ref, wb_ref)):
                 ref[layer, place, :] = source[base + number * rows : base + (number + 1) * rows, :].astype(F32)
-        total = jnp.where(chunk == 0, source[:SUB, :].astype(F32)[0], total)
+        total = jnp.where(chunk == 0, source[6 * rows :, :].astype(F32)[0], total)
     readout_ref[...] = total
 
 
@@ -372,20 +379,20 @@
 
 def scaled(part):
     count, rows, width = part.shape
-    head, body = part[:, :1], part[:, SUB:].reshape(count, 6, -1, width)
-    power = powers(jnp.concatenate([jnp.abs(head), jnp.max(jnp.abs(body), axis=2)], axis=1))
+    body, readout = part[:, :-TAIL].reshape(count, 6, -1, width), part[:, rows - TAIL : rows - TAIL + 1]
+    power = powers(jnp.concatenate([jnp.abs(readout), jnp.max(jnp.abs(body), axis=2)], axis=1))
     factor = jnp.exp2(-power)
     body = (body * factor[:, 1:, None]).reshape(count, -1, width)
-    rest = jnp.zeros((count, SUB - 8, width), F32)
-    return jnp.concatenate([head * factor[:, :1], power, rest, body], axis=1).astype(F16)
+    return jnp.concatenate([body, readout * factor[:, :1], power], axis=1).astype(F16)
 
 
 def restored(sent):
     rows, width = sent.shape
     sent = sent.astype(F32)
-    factor = jnp.exp2(sent[1:8])
-    body = sent[SUB:].reshape(6, -1, width) * factor[1:, None]
-    return jnp.concatenate([sent[:1] * factor[:1], jnp.zeros((SUB - 1, width), F32), body.reshape(-1, width)], axis=0)
+    factor = jnp.exp2(sent[rows - TAIL + 1 :])
+    body = sent[:-TAIL].reshape(6, -1, width) * factor[1:, None]
+    readout = sent[rows - TAIL : rows - TAIL + 1] * factor[:1]
+    return jnp.concatenate([body.reshape(-1, width), readout, jnp.zeros((TAIL - 1, width), F32)], axis=0)
 
 
 def plane(value, x, y):
@@ -397,7 +404,7 @@
 def along_dom(mine):
     count, bit = lax.axis_size("dom"), 1
     while bit < count:
-        flips = [bit] if 2 * bit >= count else [bit, 2 * bit, 3 * bit]
+        flips = [bit] if 2 * bit >= count else [3 * bit, 2 * bit, bit]
         mine = summed(mine, *[partner(mine, "dom", flip) for flip in flips])
         bit *= 4
     return mine
@@ -412,7 +419,7 @@
     sent = scaled(part[1:])
     terms = [restored(plane(sent[0], 0, 1)), restored(plane(sent[1], 1, 0)), restored(plane(sent[2], 1, 1))]
     mine = along_dom(summed(part[0], *terms))
-    return [mine, plane(mine, 0, 1), plane(mine, 1, 0), plane(mine, 1, 1)]
+    return [plane(mine, 1, 1), plane(mine, 1, 0), plane(mine, 0, 1), mine]
 
 
 def local(features, radial, neighbours, halo_lists, slab_counts, frame_labels, w_a, w_c, w_b, readout):
@@ -484,14 +491,17 @@
             near(edge_slopes),
             near(totals, F32),
         ),
-        (first, second, onehot, edge, wta, wtb, own, cross, state, select),
+        (second, first, onehot, edge, wta, wtb, own, cross, state, select),
         scratch=[pltpu.VMEM(totals, F32)],
         flops=4 * 10**9,
     )
-    wta, wtc, wtb, wide, live, sign = kernel_call(
+    wta, wtb, own, cross, wide, live, sign = kernel_call(
         later_kernel,
-        (turned, turned, turned, near((channels, beads), F32), near((1, lanes), F32), near((1, lanes), F32)),
-        (jnp.concatenate([slab_counts[:, 0], frame_labels]), first, wa, wc, wb, readout_near),
+        (
+            turned, turned, near((hidden, lanes)), near((hidden, lanes), F32), near((channels, beads), F32),
+            near((1, lanes), F32), near((1, lanes), F32),
+        ),
+        (jnp.concatenate([slab_counts[:, 0], frame_labels]), state1, wa, wc, wb, readout_near),
         smem=1,
         flops=10**8,
     )
@@ -511,16 +521,16 @@
             near(totals),
             near((channels, lanes)),
         ),
-        (first, second, onehot, edge, wta, wtc, wtb, wb, state1, live, sign, wide),
+        (second, first, onehot, edge, wta, wtb, wb, own, cross, state1, live, sign, wide),
         scratch=[pltpu.VMEM(edge_slopes, BF16), pltpu.VMEM(totals, F32), pltpu.VMEM(totals, F32)],
         flops=6 * 10**9,
     )
     second, first = swapped(second, 1), swapped(first, 0)
     chunk = hidden // 8
-    upper_slots = kernel_call(
+    upper_slots, cot = kernel_call(
         upper_grads_kernel,
-        near((8, SUB + 3 * chunk, channels), F32),
-        (where, state1, halo1, gathered1, cot_low1, cot_own, cot_halo, cot_cross, grad_readout),
+        (near((8, 3 * chunk + TAIL, channels), F32), near((channels, lanes), F32)),
+        (where, state1, halo1, gathered1, cot_low1, cot_own, cot_halo, cot_cross, grad_readout, cot, wc),
         smem=1,
         flops=10**9,
     )
@@ -529,13 +539,13 @@
         lower_kernel,
         near((8, 3 * chunk, channels), F32),
         (
-            where, first, second, select, cot_own, cot_cross, cot, wa, wc, wb,
-            onehot, slope0, slope_total0, state, halo0, gathered0, upper_slots,
+            where, second, first, select, cot_own, cot, wa, wb,
+            onehot, slope0, slope_total0, state, halo0, gathered0,
         ),
         smem=1,
         flops=4 * 10**9,
     )
-    close = reduce_parts([upper_part, core_sum(lower_slots)])
+    close = reduce_parts([core_sum(lower_slots), upper_part])
     far = partner(jnp.stack(close), "rep", 1)
     grad = jax.ShapeDtypeStruct((layers, channels, hidden), F32)
     grad_wa, grad_wc, grad_wb, grad_readout = kernel_call(

time: 72.7 us -> 72.2 us (level)
  waiting for transfers between devices: 23.3 us -> 26.9 us
  starting transfers between devices: 26.2 us -> 23 us
    ppermute x6, waiting for transfers between devices: 4.75 us -> 8.95 us  [swapped(): return lax.ppermute(value, RING, pairs)]
    ppermute x6, starting transfers between devices: 14 us -> 11.3 us  [swapped(): return lax.ppermute(value, RING, pairs)]
    ppermute x6, waiting for transfers between devices: 9.36 us -> 8.33 us  [plane(): lax.ppermute(value, EVERY, [(s, s ^ flip) for s in range(rep * dom * tp)])]
    pallas_call x8, Pallas kernels: 20.7 us -> 20 us  [kernel_call(): pl.pallas_call(body, out_shape=outs, in_specs=[pl.BlockSpec(memory_space=...]
  transfers between devices with their start and end apart: 18 -> 18, of which waited for: 14 -> 15; matrix products, arithmetic and copies ran while one was open for 1% -> 0% of each run, Pallas kernels for 6% -> 9%
where the time goes in v3:
time: 72.2 us; the launch traced here: 72 us
  waiting for transfers between devices  26.9 us (37%)
  starting transfers between devices  23 us (32%)
  Pallas kernels  20 us (28%)
  other arithmetic  0.96 us (1%)
  between operations  0.95 us (1%)
    pallas_call x8, Pallas kernels, kernel_call(): pl.pallas_call(body, out_shape=outs, in_specs=[pl.BlockSpec(memory_space=...  20 us
    ppermute x6, starting transfers between devices, swapped(): return lax.ppermute(value, RING, pairs)  11.3 us
    ppermute x6, waiting for transfers between devices, partner(): lax.ppermute(value, axis, [(s, s ^ bits) for s in range(lax.axis_size(axi...  9.62 us
    ppermute x6, waiting for transfers between devices, swapped(): return lax.ppermute(value, RING, pairs)  8.95 us
    ppermute x6, waiting for transfers between devices, plane(): lax.ppermute(value, EVERY, [(s, s ^ flip) for s in range(rep * dom * tp)])  8.33 us
    ppermute x6, starting transfers between devices, plane(): lax.ppermute(value, EVERY, [(s, s ^ flip) for s in range(rep * dom * tp)])  7.11 us
    ppermute x6, starting transfers between devices, partner(): lax.ppermute(value, axis, [(s, s ^ bits) for s in range(lax.axis_size(axi...  4.67 us
  transfers between devices with their start and end apart: 18, of which 15 were waited for; matrix products, arithmetic and copies ran while one was open for 0% of the time, Pallas kernels for 9%

profile of v3, /device:TPU:0, one launch (start us, length us, event | category | flops | bytes accessed | tf_op | source)
XLA Modules:
  0.0 72.0 jit_solution(1175766545755506113)
XLA Ops:
  0.7 1.8 %shard_map.137 = (bf16[256,256]{1,0:T(8,128)(2,1)S(1)}, bf16[256,128]{1,0:T(8,128)(2,1)S(1)}, bf16[128,128]{1,0:T(8,128)(2,1)S(1)}, bf16[128,128]{1,0:T(8,128)(2...) custom-call(s32[2]{0:T(128)S(1)} %pad_add_fusion.where_ref.me_ref, bf16[2,128,256]{2,1,0:T(8,128)(2,1)} %feat_hbm.1, ...), custom_call_target="tpu_custom_call" | custom-call | tf_op jit(solution)/shard_map/pallas_call | solution.py:339
  2.5 6.1 %collective-permute-start = (bf16[128,128]{1,0:T(8,128)(2,1)S(1)}, bf16[128,128]{1,0:T(8,128)(2,1)S(1)}, u32[]{:S(2)}, u32[]{:S(2)}) collective-permute-start(bf16[128,128]{1,0:T(8,128)(2,1)S(1)} %get-tuple-element.52), channel_id=1, source_target_pairs={{0,7},{1,2},{2,1},{3,4},{4,3},{5,6},{6,5},{7,0},{8,15},{9,10},{10,... | collective-permute-start | bytes 98312 | tf_op jit(solution)/shard_map/ppermute | solution.py:362
  8.6 2.7 %shard_map.138 = (bf16[2,256,4096]{2,1,0:T(8,128)(2,1)S(1)}, bf16[2,32,16,128]{3,2,1,0:T(8,128)(2,1)S(1)}, bf16[2,256,256]{2,1,0:T(8,128)(2,1)S(1)}, bf16[2,256,...) custom-call(s32[2]{0:T(128)S(1)} %pad_add_fusion.where_ref.me_ref, ...), custom_call_target="tpu_custom_call" | custom-call | flops 2000000000 | tf_op jit(solution)/shard_map/pallas_call | solution.py:339
  11.3 1.2 %collective-permute-done.1.hf_ref = bf16[128,128]{1,0:T(8,128)(2,1)S(1)} collective-permute-done((bf16[128,128]{1,0:T(8,128)(2,1)S(1)}, bf16[128,128]{1,0:T(8,128)(2,1)S(1)}, u32[]{:S(2)}, u32[]{:S(2)}) %collective-permute-start.1) | collective-permute-done | bytes 32800 | tf_op jit(solution)/shard_map/ppermute | solution.py:362
  12.5 3.7 %shard_map.139 = (bf16[256,256]{1,0:T(8,128)(2,1)S(1)}, bf16[128,128]{1,0:T(8,128)(2,1)S(1)}, bf16[128,128]{1,0:T(8,128)(2,1)S(1)}, bf16[256,128]{1,0:T(8,128)(2...) custom-call(bf16[128,128]{1,0:T(8,128)(2,1)S(1)} %collective-permute-done.hs_ref, ...), custom_call_target="tpu_custom_call" | custom-call | flops 4000000000 | tf_op jit(solution)/shard_map/pallas_call | solution.py:339
  16.3 2.8 %collective-permute-start.2 = (bf16[128,128]{1,0:T(8,128)(2,1)S(1)}, bf16[128,128]{1,0:T(8,128)(2,1)S(1)}, u32[]{:S(2)}, u32[]{:S(2)}) collective-permute-start(bf16[128,128]{1,0:T(8,128)(2,1)S(1)} %get-tuple-element.64), channel_id=1, source_target_pairs={{0,7},{1,2},{2,1},{3,4},{4,3},{5,6},{6,5},{7,0},{8,15},{9,10},{10,... | collective-permute-start | bytes 98312 | tf_op jit(solution)/shard_map/ppermute | solution.py:362
  20.0 3.0 %collective-permute-done.2.hs_ref = bf16[128,128]{1,0:T(8,128)(2,1)S(1)} collective-permute-done((bf16[128,128]{1,0:T(8,128)(2,1)S(1)}, bf16[128,128]{1,0:T(8,128)(2,1)S(1)}, u32[]{:S(2)}, u32[]{:S(2)}) %collective-permute-start.2) | collective-permute-done | bytes 32800 | tf_op jit(solution)/shard_map/ppermute | solution.py:362
  23.3 5.4 %shard_map.141 = (f32[2,128]{1,0:T(2,128)}, f32[16,256]{1,0:T(8,128)S(1)}, f32[256,256]{1,0:T(8,128)S(1)}, bf16[128,128]{1,0:T(8,128)(2,1)S(1)}, bf16[128,128]{1...) custom-call(bf16[128,128]{1,0:T(8,128)(2,1)S(1)} %collective-permute, ...), custom_call_target="tpu_custom_call" | custom-call | flops 6000000000 | tf_op jit(solution)/shard_map/pallas_call | solution.py:339
  29.7 2.4 %collective-permute-start.4 = (bf16[128,128]{1,0:T(8,128)(2,1)S(1)}, bf16[128,128]{1,0:T(8,128)(2,1)S(1)}, u32[]{:S(2)}, u32[]{:S(2)}) collective-permute-start(bf16[128,128]{1,0:T(8,128)(2,1)S(1)} %get-tuple-element.78), channel_id=1, source_target_pairs={{0,7},{1,2},{2,1},{3,4},{4,3},{5,6},{6,5},{7,0},{8,15},{9,10},{10,... | collective-permute-start | bytes 98312 | tf_op jit(solution)/shard_map/ppermute | solution.py:362
  32.2 4.3 %collective-permute-done.4.bs_ref = bf16[128,128]{1,0:T(8,128)(2,1)S(1)} collective-permute-done((bf16[128,128]{1,0:T(8,128)(2,1)S(1)}, bf16[128,128]{1,0:T(8,128)(2,1)S(1)}, u32[]{:S(2)}, u32[]{:S(2)}) %collective-permute-start.4) | collective-permute-done | bytes 32800 | tf_op jit(solution)/shard_map/ppermute | solution.py:362
  36.6 2.8 %shard_map.143 = f32[8,96,256]{2,1,0:T(8,128)S(1)} custom-call(s32[2]{0:T(128)S(1)} %pad_add_fusion.where_ref.me_ref, bf16[128,128]{1,0:T(8,128)(2,1)S(1)} %collective-permute-done.4.bs_ref, bf16[128,128]{1,0:T(8,128)(2,1)S(1)} %collective-permute-done.5.bf_ref, bf16[256,128]{1,0:T(8,128)(2,1)S(1)} %get-tuple-element.63.select_ref, ...), custom_call_target="tpu_custom_call" | custom-call | flops 4000000000 | tf_op jit(solution)/shard_map/pallas_call | solution.py:339
  39.6 1.6 %collective-permute-done.6 = f32[4,96,256]{2,1,0:T(8,128)S(1)} collective-permute-done((f32[4,96,256]{2,1,0:T(8,128)S(1)}, f32[4,96,256]{2,1,0:T(8,128)S(1)}, u32[]{:S(2)}, u32[]{:S(2)}) %collective-permute-start.6) | collective-permute-done | bytes 393248 | tf_op jit(solution)/shard_map/ppermute | solution.py:366
  42.3 1.1 %collective-permute-start.9 = (f16[200,256]{1,0:T(8,128)(2,1)S(1)}, f16[200,256]{1,0:T(8,128)(2,1)S(1)}, u32[]{:S(2)}, u32[]{:S(2)}) collective-permute-start(f16[200,256]{1,0:T(8,128)(2,1)S(1)} %get-tuple-element.100), channel_id=1, source_target_pairs={{0,16},{1,17},{2,18},{3,19},{4,20},{5,21},{6,22},{7,23},{8,24},{9,... | collective-permute-start | bytes 307208 | tf_op jit(solution)/shard_map/ppermute | solution.py:401
  43.4 2.0 %collective-permute-start.8 = (f16[200,256]{1,0:T(8,128)(2,1)S(1)}, f16[200,256]{1,0:T(8,128)(2,1)S(1)}, u32[]{:S(2)}, u32[]{:S(2)}) collective-permute-start(f16[200,256]{1,0:T(8,128)(2,1)S(1)} %get-tuple-element.101), channel_id=1, source_target_pairs={{0,1},{1,0},{2,3},{3,2},{4,5},{5,4},{6,7},{7,6},{8,9},{9,8},{10,11... | collective-permute-start | bytes 307208 | tf_op jit(solution)/shard_map/ppermute | solution.py:401
  45.4 3.1 %collective-permute-done.10 = f16[200,256]{1,0:T(8,128)(2,1)S(1)} collective-permute-done((f16[200,256]{1,0:T(8,128)(2,1)S(1)}, f16[200,256]{1,0:T(8,128)(2,1)S(1)}, u32[]{:S(2)}, u32[]{:S(2)}) %collective-permute-start.10) | collective-permute-done | bytes 102432 | tf_op jit(solution)/shard_map/ppermute | solution.py:401
  50.1 1.6 %collective-permute-start.11 = (bf16[200,256]{1,0:T(8,128)(2,1)S(1)}, bf16[200,256]{1,0:T(8,128)(2,1)S(1)}, u32[]{:S(2)}, u32[]{:S(2)}) collective-permute-start(bf16[200,256]{1,0:T(8,128)(2,1)S(1)} %fusion.4), channel_id=1, source_target_pairs={{0,6},{2,4},{4,2},{6,0},{1,7},{3,5},{5,3},{7,1},{8,14},{10,12},{12... | collective-permute-start | bytes 307208 | tf_op jit(solution)/shard_map/ppermute | solution.py:366
  51.7 2.8 %collective-permute-start.13 = (bf16[200,256]{1,0:T(8,128)(2,1)S(1)}, bf16[200,256]{1,0:T(8,128)(2,1)S(1)}, u32[]{:S(2)}, u32[]{:S(2)}) collective-permute-start(bf16[200,256]{1,0:T(8,128)(2,1)S(1)} %fusion.4), channel_id=1, source_target_pairs={{0,2},{2,0},{4,6},{6,4},{1,3},{3,1},{5,7},{7,5},{8,10},{10,8},{12,... | collective-permute-start | bytes 307208 | tf_op jit(solution)/shard_map/ppermute | solution.py:366
  54.5 3.3 %collective-permute-done.11 = bf16[200,256]{1,0:T(8,128)(2,1)S(1)} collective-permute-done((bf16[200,256]{1,0:T(8,128)(2,1)S(1)}, bf16[200,256]{1,0:T(8,128)(2,1)S(1)}, u32[]{:S(2)}, u32[]{:S(2)}) %collective-permute-start.11) | collective-permute-done | bytes 102432 | tf_op jit(solution)/shard_map/ppermute | solution.py:366
  57.8 3.0 %collective-permute-done.12 = bf16[200,256]{1,0:T(8,128)(2,1)S(1)} collective-permute-done((bf16[200,256]{1,0:T(8,128)(2,1)S(1)}, bf16[200,256]{1,0:T(8,128)(2,1)S(1)}, u32[]{:S(2)}, u32[]{:S(2)}) %collective-permute-start.12) | collective-permute-done | bytes 102432 | tf_op jit(solution)/shard_map/ppermute | solution.py:366
  60.8 1.3 %collective-permute-start.14 = (bf16[200,256]{1,0:T(8,128)(2,1)S(1)}, bf16[200,256]{1,0:T(8,128)(2,1)S(1)}, u32[]{:S(2)}, u32[]{:S(2)}) collective-permute-start(bf16[200,256]{1,0:T(8,128)(2,1)S(1)} %add_convert_fusion.refs_3_), channel_id=1, source_target_pairs={{0,17},{1,16},{2,19},{3,18},{4,21},{5,20},{6,23},{7,22},{8,25},{9,... | collective-permute-start | bytes 307208 | tf_op jit(solution)/shard_map/ppermute | solution.py:401
  62.6 1.7 %collective-permute-start.16 = (bf16[200,256]{1,0:T(8,128)(2,1)S(1)}, bf16[200,256]{1,0:T(8,128)(2,1)S(1)}, u32[]{:S(2)}, u32[]{:S(2)}) collective-permute-start(bf16[200,256]{1,0:T(8,128)(2,1)S(1)} %add_convert_fusion.refs_3_), channel_id=1, source_target_pairs={{0,1},{1,0},{2,3},{3,2},{4,5},{5,4},{6,7},{7,6},{8,9},{9,8},{10,11... | collective-permute-start | bytes 307208 | tf_op jit(solution)/shard_map/ppermute | solution.py:401
  64.4 3.0 %collective-permute-done.14.refs_0_ = bf16[200,256]{1,0:T(8,128)(2,1)S(1)} collective-permute-done((bf16[200,256]{1,0:T(8,128)(2,1)S(1)}, bf16[200,256]{1,0:T(8,128)(2,1)S(1)}, u32[]{:S(2)}, u32[]{:S(2)}) %collective-permute-start.14) | collective-permute-done | bytes 102432 | tf_op jit(solution)/shard_map/ppermute | solution.py:401
  68.5 1.7 %collective-permute-done.17.refs_4_ = bf16[4,200,256]{2,1,0:T(8,128)(2,1)S(1)} collective-permute-done((bf16[4,200,256]{2,1,0:T(8,128)(2,1)S(1)}, bf16[4,200,256]{2,1,0:T(8,128)(2,1)S(1)}, u32[]{:S(2)}, u32[]{:S(2)}) %collective-permute-start.17) | collective-permute-done | bytes 409632 | tf_op jit(solution)/shard_map/ppermute | solution.py:366
  70.3 1.8 %shard_map.144 = (f32[2,256,256]{2,1,0:T(8,128)}, f32[2,256,256]{2,1,0:T(8,128)}, f32[2,256,256]{2,1,0:T(8,128)}, f32[256]{0:T(256)}) custom-call(s32[2]{0:T(128)S(1)} %pad_add_fusion.where_ref.me_ref, bf16[200,256]{1,0:T(8,128)(2,1)S(1)} %collective-permute-done.14.refs_0_, bf16[200,256]{1,0:T(8,128)(2,1)S(1)} %collective-permute-done.15.refs_1_, ...), custom_call_target="tpu_custom_call" | custom-call | tf_op jit(solution)/shard_map/pallas_call | solution.py:339
  (59 shorter events, 6.8 us)
Async XLA Ops:
  2.5 8.8 %collective-permute-start = (bf16[128,128]{1,0:T(8,128)(2,1)S(1)}, bf16[128,128]{1,0:T(8,128)(2,1)S(1)}, u32[]{:S(2)}, u32[]{:S(2)}) collective-permute-start(bf16[128,128]{1,0:T(8,128)(2,1)S(1)} %get-tuple-element.52), channel_id=1, source_target_pairs={{0,7},{1,2},{2,1},{3,4},{4,3},{5,6},{6,5},{7,0},{8,15},{9,10},{10,... | collective-permute-start | bytes 98312 | tf_op jit(solution)/shard_map/ppermute | solution.py:362
  8.6 3.9 %collective-permute-start.1 = (bf16[128,128]{1,0:T(8,128)(2,1)S(1)}, bf16[128,128]{1,0:T(8,128)(2,1)S(1)}, u32[]{:S(2)}, u32[]{:S(2)}) collective-permute-start(bf16[128,128]{1,0:T(8,128)(2,1)S(1)} %get-tuple-element.53), channel_id=1, source_target_pairs={{0,1},{1,0},{2,3},{3,2},{4,5},{5,4},{6,7},{7,6},{8,9},{9,8},{10,11... | collective-permute-start | bytes 98312 | tf_op jit(solution)/shard_map/ppermute | solution.py:362
  12.5 6.5 %copy-start = (s32[2]{0:T(128)S(1)}, s32[2]{0:T(128)}, u32[]{:S(2)}) copy-start(s32[2]{0:T(128)} %param.15) | copy-start | bytes 28
  12.5 6.5 %copy-start.1 = (s32[2,1]{0,1:T(1,128)S(1)}, s32[2,1]{0,1:T(1,128)}, u32[]{:S(2)}) copy-start(s32[2,1]{0,1:T(1,128)} %param.14) | copy-start | bytes 28
  16.3 6.7 %collective-permute-start.2 = (bf16[128,128]{1,0:T(8,128)(2,1)S(1)}, bf16[128,128]{1,0:T(8,128)(2,1)S(1)}, u32[]{:S(2)}, u32[]{:S(2)}) collective-permute-start(bf16[128,128]{1,0:T(8,128)(2,1)S(1)} %get-tuple-element.64), channel_id=1, source_target_pairs={{0,7},{1,2},{2,1},{3,4},{4,3},{5,6},{6,5},{7,0},{8,15},{9,10},{10,... | collective-permute-start | bytes 98312 | tf_op jit(solution)/shard_map/ppermute | solution.py:362
  19.0 4.3 %collective-permute-start.3 = (bf16[128,128]{1,0:T(8,128)(2,1)S(1)}, bf16[128,128]{1,0:T(8,128)(2,1)S(1)}, u32[]{:S(2)}, u32[]{:S(2)}) collective-permute-start(bf16[128,128]{1,0:T(8,128)(2,1)S(1)} %get-tuple-element.65), channel_id=1, source_target_pairs={{0,1},{1,0},{2,3},{3,2},{4,5},{5,4},{6,7},{7,6},{8,9},{9,8},{10,11... | collective-permute-start | bytes 98312 | tf_op jit(solution)/shard_map/ppermute | solution.py:362
  29.7 9.8 %collective-permute-start.7 = (f32[4,104,256]{2,1,0:T(8,128)S(1)}, f32[4,104,256]{2,1,0:T(8,128)S(1)}, u32[]{:S(2)}, u32[]{:S(2)}) collective-permute-start(f32[4,104,256]{2,1,0:T(8,128)S(1)} %slice.88), channel_id=1, source_target_pairs={{0,8},{8,0},{16,24},{24,16},{1,9},{9,1},{17,25},{25,17},{2,10},{10... | collective-permute-start | bytes 1277960 | tf_op jit(solution)/shard_map/ppermute | solution.py:366
  29.7 6.7 %collective-permute-start.4 = (bf16[128,128]{1,0:T(8,128)(2,1)S(1)}, bf16[128,128]{1,0:T(8,128)(2,1)S(1)}, u32[]{:S(2)}, u32[]{:S(2)}) collective-permute-start(bf16[128,128]{1,0:T(8,128)(2,1)S(1)} %get-tuple-element.78), channel_id=1, source_target_pairs={{0,7},{1,2},{2,1},{3,4},{4,3},{5,6},{6,5},{7,0},{8,15},{9,10},{10,... | collective-permute-start | bytes 98312 | tf_op jit(solution)/shard_map/ppermute | solution.py:362
  32.2 4.4 %collective-permute-start.5 = (bf16[128,128]{1,0:T(8,128)(2,1)S(1)}, bf16[128,128]{1,0:T(8,128)(2,1)S(1)}, u32[]{:S(2)}, u32[]{:S(2)}) collective-permute-start(bf16[128,128]{1,0:T(8,128)(2,1)S(1)} %get-tuple-element.79), channel_id=1, source_target_pairs={{0,1},{1,0},{2,3},{3,2},{4,5},{5,4},{6,7},{7,6},{8,9},{9,8},{10,11... | collective-permute-start | bytes 98312 | tf_op jit(solution)/shard_map/ppermute | solution.py:362
  39.4 1.8 %collective-permute-start.6 = (f32[4,96,256]{2,1,0:T(8,128)S(1)}, f32[4,96,256]{2,1,0:T(8,128)S(1)}, u32[]{:S(2)}, u32[]{:S(2)}) collective-permute-start(f32[4,96,256]{2,1,0:T(8,128)S(1)} %slice.113), channel_id=1, source_target_pairs={{0,8},{8,0},{16,24},{24,16},{1,9},{9,1},{17,25},{25,17},{2,10},{10... | collective-permute-start | bytes 1179656 | tf_op jit(solution)/shard_map/ppermute | solution.py:366
  41.7 6.7 %collective-permute-start.10 = (f16[200,256]{1,0:T(8,128)(2,1)S(1)}, f16[200,256]{1,0:T(8,128)(2,1)S(1)}, u32[]{:S(2)}, u32[]{:S(2)}) collective-permute-start(f16[200,256]{1,0:T(8,128)(2,1)S(1)} %get-tuple-element.99), channel_id=1, source_target_pairs={{0,17},{1,16},{2,19},{3,18},{4,21},{5,20},{6,23},{7,22},{8,25},{9,... | collective-permute-start | bytes 307208 | tf_op jit(solution)/shard_map/ppermute | solution.py:401
  42.3 6.4 %collective-permute-start.9 = (f16[200,256]{1,0:T(8,128)(2,1)S(1)}, f16[200,256]{1,0:T(8,128)(2,1)S(1)}, u32[]{:S(2)}, u32[]{:S(2)}) collective-permute-start(f16[200,256]{1,0:T(8,128)(2,1)S(1)} %get-tuple-element.100), channel_id=1, source_target_pairs={{0,16},{1,17},{2,18},{3,19},{4,20},{5,21},{6,22},{7,23},{8,24},{9,... | collective-permute-start | bytes 307208 | tf_op jit(solution)/shard_map/ppermute | solution.py:401
  43.4 6.4 %collective-permute-start.8 = (f16[200,256]{1,0:T(8,128)(2,1)S(1)}, f16[200,256]{1,0:T(8,128)(2,1)S(1)}, u32[]{:S(2)}, u32[]{:S(2)}) collective-permute-start(f16[200,256]{1,0:T(8,128)(2,1)S(1)} %get-tuple-element.101), channel_id=1, source_target_pairs={{0,1},{1,0},{2,3},{3,2},{4,5},{5,4},{6,7},{7,6},{8,9},{9,8},{10,11... | collective-permute-start | bytes 307208 | tf_op jit(solution)/shard_map/ppermute | solution.py:401
  50.1 7.7 %collective-permute-start.11 = (bf16[200,256]{1,0:T(8,128)(2,1)S(1)}, bf16[200,256]{1,0:T(8,128)(2,1)S(1)}, u32[]{:S(2)}, u32[]{:S(2)}) collective-permute-start(bf16[200,256]{1,0:T(8,128)(2,1)S(1)} %fusion.4), channel_id=1, source_target_pairs={{0,6},{2,4},{4,2},{6,0},{1,7},{3,5},{5,3},{7,1},{8,14},{10,12},{12... | collective-permute-start | bytes 307208 | tf_op jit(solution)/shard_map/ppermute | solution.py:366
  51.7 9.1 %collective-permute-start.12 = (bf16[200,256]{1,0:T(8,128)(2,1)S(1)}, bf16[200,256]{1,0:T(8,128)(2,1)S(1)}, u32[]{:S(2)}, u32[]{:S(2)}) collective-permute-start(bf16[200,256]{1,0:T(8,128)(2,1)S(1)} %fusion.4), channel_id=1, source_target_pairs={{0,4},{2,6},{4,0},{6,2},{1,5},{3,7},{5,1},{7,3},{8,12},{10,14},{12... | collective-permute-start | bytes 307208 | tf_op jit(solution)/shard_map/ppermute | solution.py:366
  51.7 9.1 %collective-permute-start.13 = (bf16[200,256]{1,0:T(8,128)(2,1)S(1)}, bf16[200,256]{1,0:T(8,128)(2,1)S(1)}, u32[]{:S(2)}, u32[]{:S(2)}) collective-permute-start(bf16[200,256]{1,0:T(8,128)(2,1)S(1)} %fusion.4), channel_id=1, source_target_pairs={{0,2},{2,0},{4,6},{6,4},{1,3},{3,1},{5,7},{7,5},{8,10},{10,8},{12,... | collective-permute-start | bytes 307208 | tf_op jit(solution)/shard_map/ppermute | solution.py:366
  60.8 6.6 %collective-permute-start.14 = (bf16[200,256]{1,0:T(8,128)(2,1)S(1)}, bf16[200,256]{1,0:T(8,128)(2,1)S(1)}, u32[]{:S(2)}, u32[]{:S(2)}) collective-permute-start(bf16[200,256]{1,0:T(8,128)(2,1)S(1)} %add_convert_fusion.refs_3_), channel_id=1, source_target_pairs={{0,17},{1,16},{2,19},{3,18},{4,21},{5,20},{6,23},{7,22},{8,25},{9,... | collective-permute-start | bytes 307208 | tf_op jit(solution)/shard_map/ppermute | solution.py:401
  62.1 5.5 %collective-permute-start.15 = (bf16[200,256]{1,0:T(8,128)(2,1)S(1)}, bf16[200,256]{1,0:T(8,128)(2,1)S(1)}, u32[]{:S(2)}, u32[]{:S(2)}) collective-permute-start(bf16[200,256]{1,0:T(8,128)(2,1)S(1)} %add_convert_fusion.refs_3_), channel_id=1, source_target_pairs={{0,16},{1,17},{2,18},{3,19},{4,20},{5,21},{6,22},{7,23},{8,24},{9,... | collective-permute-start | bytes 307208 | tf_op jit(solution)/shard_map/ppermute | solution.py:401
  62.6 5.7 %collective-permute-start.16 = (bf16[200,256]{1,0:T(8,128)(2,1)S(1)}, bf16[200,256]{1,0:T(8,128)(2,1)S(1)}, u32[]{:S(2)}, u32[]{:S(2)}) collective-permute-start(bf16[200,256]{1,0:T(8,128)(2,1)S(1)} %add_convert_fusion.refs_3_), channel_id=1, source_target_pairs={{0,1},{1,0},{2,3},{3,2},{4,5},{5,4},{6,7},{7,6},{8,9},{9,8},{10,11... | collective-permute-start | bytes 307208 | tf_op jit(solution)/shard_map/ppermute | solution.py:401
  68.4 1.8 %collective-permute-start.17 = (bf16[4,200,256]{2,1,0:T(8,128)(2,1)S(1)}, bf16[4,200,256]{2,1,0:T(8,128)(2,1)S(1)}, u32[]{:S(2)}, u32[]{:S(2)}) collective-permute-start(bf16[4,200,256]{2,1,0:T(8,128)(2,1)S(1)} %pad_maximum_fusion.1), channel_id=1, source_target_pairs={{0,8},{8,0},{16,24},{24,16},{1,9},{9,1},{17,25},{25,17},{2,10},{10... | collective-permute-start | bytes 1228808 | tf_op jit(solution)/shard_map/ppermute | solution.py:366

commit v4 on v3

--- a/solution.py
+++ b/solution.py
@@ -290,7 +290,7 @@
 
 
 def lower_kernel(
-    me_ref, bs_ref, bf_ref, select_ref, cot_own_ref, cot_ref, wa_ref, wb_ref,
+    me_ref, bf_ref, bs_ref, select_ref, cot_own_ref, cot_ref, wa_ref, wb_ref,
     onehot_ref, slope_ref, slope_total_ref, state_ref, halo_ref, gathered_ref,
     slots_ref,
 ):
@@ -317,13 +317,13 @@
 
 
 def finish_kernel(me_ref, *refs):
-    *near, far, wa_ref, wc_ref, wb_ref, readout_ref = refs
+    *sources, wa_ref, wc_ref, wb_ref, readout_ref = refs
     me = me_ref[0]
-    count = len(near)
-    rows = (far.shape[1] - TAIL) // 6
+    count = len(sources) // 2
+    rows = (sources[0].shape[0] - TAIL) // 6
     total = jnp.zeros(readout_ref.shape, F32)
     for slot in range(2 * count):
-        source = near[count - 1 - slot] if slot < count else far.at[2 * count - 1 - slot]
+        source = sources[slot ^ (count - 1)]
         chunk = jnp.bitwise_xor(me, slot)
         place = pl.ds(pl.multiple_of(chunk * rows, rows), rows)
         for layer, base in ((0, 0), (1, 3 * rows)):
@@ -532,26 +532,26 @@
         (near((8, 3 * chunk + TAIL, channels), F32), near((channels, lanes), F32)),
         (where, state1, halo1, gathered1, cot_low1, cot_own, cot_halo, cot_cross, grad_readout, cot, wc),
         smem=1,
-        flops=10**9,
+        flops=10**8,
     )
     upper_part = core_sum(upper_slots)
     lower_slots = kernel_call(
         lower_kernel,
         near((8, 3 * chunk, channels), F32),
         (
-            where, second, first, select, cot_own, cot, wa, wb,
+            where, first, second, select, cot_own, cot, wa, wb,
             onehot, slope0, slope_total0, state, halo0, gathered0,
         ),
         smem=1,
         flops=4 * 10**9,
     )
     close = reduce_parts([core_sum(lower_slots), upper_part])
-    far = partner(jnp.stack(close), "rep", 1)
+    far = [partner(value, "rep", 1) for value in close]
     grad = jax.ShapeDtypeStruct((layers, channels, hidden), F32)
     grad_wa, grad_wc, grad_wb, grad_readout = kernel_call(
         finish_kernel,
         (grad, grad, grad, jax.ShapeDtypeStruct((channels,), F32)),
-        (where, *close, far),
+        (where, *close, *far),
         smem=1,
     )
     return grad_wa, grad_wc, grad_wb, grad_readout, energy

time: 72.2 us -> 71.6 us (level)
  waiting for transfers between devices: 26.9 us -> 26 us
    ppermute x6 -> x9, waiting for transfers between devices: 9.62 us -> 9.19 us  [partner(): lax.ppermute(value, axis, [(s, s ^ bits) for s in range(lax.axis_size(axi...]
    ppermute x6 -> x9, starting transfers between devices: 4.67 us -> 4.91 us  [partner(): lax.ppermute(value, axis, [(s, s ^ bits) for s in range(lax.axis_size(axi...]
  transfers between devices with their start and end apart: 18 -> 21, of which waited for: 15 -> 17; matrix products, arithmetic and copies ran while one was open for 0% -> 0% of each run, Pallas kernels for 9% -> 9%
where the time goes in v4:
time: 71.6 us; the launch traced here: 71.4 us
  waiting for transfers between devices  26 us (36%)
  starting transfers between devices  23.4 us (33%)
  Pallas kernels  20 us (28%)
  between operations  0.95 us (1%)
  other arithmetic  0.91 us (1%)
    pallas_call x8, Pallas kernels, kernel_call(): pl.pallas_call(body, out_shape=outs, in_specs=[pl.BlockSpec(memory_space=...  20 us
    ppermute x6, starting transfers between devices, swapped(): return lax.ppermute(value, RING, pairs)  11.4 us
    ppermute x9, waiting for transfers between devices, partner(): lax.ppermute(value, axis, [(s, s ^ bits) for s in range(lax.axis_size(axi...  9.19 us
    ppermute x6, waiting for transfers between devices, swapped(): return lax.ppermute(value, RING, pairs)  8.77 us
    ppermute x6, waiting for transfers between devices, plane(): lax.ppermute(value, EVERY, [(s, s ^ flip) for s in range(rep * dom * tp)])  8.04 us
    ppermute x6, starting transfers between devices, plane(): lax.ppermute(value, EVERY, [(s, s ^ flip) for s in range(rep * dom * tp)])  7.11 us
    ppermute x9, starting transfers between devices, partner(): lax.ppermute(value, axis, [(s, s ^ bits) for s in range(lax.axis_size(axi...  4.91 us
  transfers between devices with their start and end apart: 21, of which 17 were waited for; matrix products, arithmetic and copies ran while one was open for 0% of the time, Pallas kernels for 9%

profile of v4, /device:TPU:0, one launch (start us, length us, event | category | flops | bytes accessed | tf_op | source)
XLA Modules:
  0.0 71.4 jit_solution(12560032457077165698)
XLA Ops:
  0.7 1.8 %shard_map.137 = (bf16[256,256]{1,0:T(8,128)(2,1)S(1)}, bf16[256,128]{1,0:T(8,128)(2,1)S(1)}, bf16[128,128]{1,0:T(8,128)(2,1)S(1)}, bf16[128,128]{1,0:T(8,128)(2...) custom-call(s32[2]{0:T(128)S(1)} %pad_add_fusion.where_ref.me_ref, bf16[2,128,256]{2,1,0:T(8,128)(2,1)} %feat_hbm.1, ...), custom_call_target="tpu_custom_call" | custom-call | tf_op jit(solution)/shard_map/pallas_call | solution.py:339
  2.5 6.1 %collective-permute-start = (bf16[128,128]{1,0:T(8,128)(2,1)S(1)}, bf16[128,128]{1,0:T(8,128)(2,1)S(1)}, u32[]{:S(2)}, u32[]{:S(2)}) collective-permute-start(bf16[128,128]{1,0:T(8,128)(2,1)S(1)} %get-tuple-element.52), channel_id=1, source_target_pairs={{0,7},{1,2},{2,1},{3,4},{4,3},{5,6},{6,5},{7,0},{8,15},{9,10},{10,... | collective-permute-start | bytes 98312 | tf_op jit(solution)/shard_map/ppermute | solution.py:362
  8.6 2.7 %shard_map.138 = (bf16[2,256,4096]{2,1,0:T(8,128)(2,1)S(1)}, bf16[2,32,16,128]{3,2,1,0:T(8,128)(2,1)S(1)}, bf16[2,256,256]{2,1,0:T(8,128)(2,1)S(1)}, bf16[2,256,...) custom-call(s32[2]{0:T(128)S(1)} %pad_add_fusion.where_ref.me_ref, ...), custom_call_target="tpu_custom_call" | custom-call | flops 2000000000 | tf_op jit(solution)/shard_map/pallas_call | solution.py:339
  11.3 1.2 %collective-permute-done.1.hf_ref = bf16[128,128]{1,0:T(8,128)(2,1)S(1)} collective-permute-done((bf16[128,128]{1,0:T(8,128)(2,1)S(1)}, bf16[128,128]{1,0:T(8,128)(2,1)S(1)}, u32[]{:S(2)}, u32[]{:S(2)}) %collective-permute-start.1) | collective-permute-done | bytes 32800 | tf_op jit(solution)/shard_map/ppermute | solution.py:362
  12.5 3.7 %shard_map.139 = (bf16[256,256]{1,0:T(8,128)(2,1)S(1)}, bf16[128,128]{1,0:T(8,128)(2,1)S(1)}, bf16[128,128]{1,0:T(8,128)(2,1)S(1)}, bf16[256,128]{1,0:T(8,128)(2...) custom-call(bf16[128,128]{1,0:T(8,128)(2,1)S(1)} %collective-permute-done.hs_ref, ...), custom_call_target="tpu_custom_call" | custom-call | flops 4000000000 | tf_op jit(solution)/shard_map/pallas_call | solution.py:339
  16.3 2.8 %collective-permute-start.2 = (bf16[128,128]{1,0:T(8,128)(2,1)S(1)}, bf16[128,128]{1,0:T(8,128)(2,1)S(1)}, u32[]{:S(2)}, u32[]{:S(2)}) collective-permute-start(bf16[128,128]{1,0:T(8,128)(2,1)S(1)} %get-tuple-element.64), channel_id=1, source_target_pairs={{0,7},{1,2},{2,1},{3,4},{4,3},{5,6},{6,5},{7,0},{8,15},{9,10},{10,... | collective-permute-start | bytes 98312 | tf_op jit(solution)/shard_map/ppermute | solution.py:362
  20.0 3.0 %collective-permute-done.2.hs_ref = bf16[128,128]{1,0:T(8,128)(2,1)S(1)} collective-permute-done((bf16[128,128]{1,0:T(8,128)(2,1)S(1)}, bf16[128,128]{1,0:T(8,128)(2,1)S(1)}, u32[]{:S(2)}, u32[]{:S(2)}) %collective-permute-start.2) | collective-permute-done | bytes 32800 | tf_op jit(solution)/shard_map/ppermute | solution.py:362
  23.3 5.4 %shard_map.141 = (f32[2,128]{1,0:T(2,128)}, f32[16,256]{1,0:T(8,128)S(1)}, f32[256,256]{1,0:T(8,128)S(1)}, bf16[128,128]{1,0:T(8,128)(2,1)S(1)}, bf16[128,128]{1...) custom-call(bf16[128,128]{1,0:T(8,128)(2,1)S(1)} %collective-permute, ...), custom_call_target="tpu_custom_call" | custom-call | flops 6000000000 | tf_op jit(solution)/shard_map/pallas_call | solution.py:339
  29.8 2.4 %collective-permute-start.5 = (bf16[128,128]{1,0:T(8,128)(2,1)S(1)}, bf16[128,128]{1,0:T(8,128)(2,1)S(1)}, u32[]{:S(2)}, u32[]{:S(2)}) collective-permute-start(bf16[128,128]{1,0:T(8,128)(2,1)S(1)} %get-tuple-element.79), channel_id=1, source_target_pairs={{0,7},{1,2},{2,1},{3,4},{4,3},{5,6},{6,5},{7,0},{8,15},{9,10},{10,... | collective-permute-start | bytes 98312 | tf_op jit(solution)/shard_map/ppermute | solution.py:362
  32.3 1.5 %collective-permute-done.4.bf_ref = bf16[128,128]{1,0:T(8,128)(2,1)S(1)} collective-permute-done((bf16[128,128]{1,0:T(8,128)(2,1)S(1)}, bf16[128,128]{1,0:T(8,128)(2,1)S(1)}, u32[]{:S(2)}, u32[]{:S(2)}) %collective-permute-start.4) | collective-permute-done | bytes 32800 | tf_op jit(solution)/shard_map/ppermute | solution.py:362
  33.7 2.8 %collective-permute-done.5.bs_ref = bf16[128,128]{1,0:T(8,128)(2,1)S(1)} collective-permute-done((bf16[128,128]{1,0:T(8,128)(2,1)S(1)}, bf16[128,128]{1,0:T(8,128)(2,1)S(1)}, u32[]{:S(2)}, u32[]{:S(2)}) %collective-permute-start.5) | collective-permute-done | bytes 32800 | tf_op jit(solution)/shard_map/ppermute | solution.py:362
  36.5 2.8 %shard_map.143 = f32[8,96,256]{2,1,0:T(8,128)S(1)} custom-call(s32[2]{0:T(128)S(1)} %pad_add_fusion.where_ref.me_ref, bf16[128,128]{1,0:T(8,128)(2,1)S(1)} %collective-permute-done.4.bf_ref, bf16[128,128]{1,0:T(8,128)(2,1)S(1)} %collective-permute-done.5.bs_ref, bf16[256,128]{1,0:T(8,128)(2,1)S(1)} %get-tuple-element.63.select_ref, ...), custom_call_target="tpu_custom_call" | custom-call | flops 4000000000 | tf_op jit(solution)/shard_map/pallas_call | solution.py:339
  39.5 1.6 %collective-permute-done.6 = f32[4,96,256]{2,1,0:T(8,128)S(1)} collective-permute-done((f32[4,96,256]{2,1,0:T(8,128)S(1)}, f32[4,96,256]{2,1,0:T(8,128)S(1)}, u32[]{:S(2)}, u32[]{:S(2)}) %collective-permute-start.6) | collective-permute-done | bytes 393248 | tf_op jit(solution)/shard_map/ppermute | solution.py:366
  41.6 1.1 %collective-permute-start.10 = (f16[200,256]{1,0:T(8,128)(2,1)S(1)}, f16[200,256]{1,0:T(8,128)(2,1)S(1)}, u32[]{:S(2)}, u32[]{:S(2)}) collective-permute-start(f16[200,256]{1,0:T(8,128)(2,1)S(1)} %get-tuple-element.99), channel_id=1, source_target_pairs={{0,17},{1,16},{2,19},{3,18},{4,21},{5,20},{6,23},{7,22},{8,25},{9,... | collective-permute-start | bytes 307208 | tf_op jit(solution)/shard_map/ppermute | solution.py:401
  43.4 1.9 %collective-permute-start.8 = (f16[200,256]{1,0:T(8,128)(2,1)S(1)}, f16[200,256]{1,0:T(8,128)(2,1)S(1)}, u32[]{:S(2)}, u32[]{:S(2)}) collective-permute-start(f16[200,256]{1,0:T(8,128)(2,1)S(1)} %get-tuple-element.101), channel_id=1, source_target_pairs={{0,1},{1,0},{2,3},{3,2},{4,5},{5,4},{6,7},{7,6},{8,9},{9,8},{10,11... | collective-permute-start | bytes 307208 | tf_op jit(solution)/shard_map/ppermute | solution.py:401
  45.3 3.1 %collective-permute-done.10 = f16[200,256]{1,0:T(8,128)(2,1)S(1)} collective-permute-done((f16[200,256]{1,0:T(8,128)(2,1)S(1)}, f16[200,256]{1,0:T(8,128)(2,1)S(1)}, u32[]{:S(2)}, u32[]{:S(2)}) %collective-permute-start.10) | collective-permute-done | bytes 102432 | tf_op jit(solution)/shard_map/ppermute | solution.py:401
  50.0 1.6 %collective-permute-start.11 = (bf16[200,256]{1,0:T(8,128)(2,1)S(1)}, bf16[200,256]{1,0:T(8,128)(2,1)S(1)}, u32[]{:S(2)}, u32[]{:S(2)}) collective-permute-start(bf16[200,256]{1,0:T(8,128)(2,1)S(1)} %fusion.4), channel_id=1, source_target_pairs={{0,6},{2,4},{4,2},{6,0},{1,7},{3,5},{5,3},{7,1},{8,14},{10,12},{12... | collective-permute-start | bytes 307208 | tf_op jit(solution)/shard_map/ppermute | solution.py:366
  51.6 2.8 %collective-permute-start.13 = (bf16[200,256]{1,0:T(8,128)(2,1)S(1)}, bf16[200,256]{1,0:T(8,128)(2,1)S(1)}, u32[]{:S(2)}, u32[]{:S(2)}) collective-permute-start(bf16[200,256]{1,0:T(8,128)(2,1)S(1)} %fusion.4), channel_id=1, source_target_pairs={{0,2},{2,0},{4,6},{6,4},{1,3},{3,1},{5,7},{7,5},{8,10},{10,8},{12,... | collective-permute-start | bytes 307208 | tf_op jit(solution)/shard_map/ppermute | solution.py:366
  54.4 3.3 %collective-permute-done.11 = bf16[200,256]{1,0:T(8,128)(2,1)S(1)} collective-permute-done((bf16[200,256]{1,0:T(8,128)(2,1)S(1)}, bf16[200,256]{1,0:T(8,128)(2,1)S(1)}, u32[]{:S(2)}, u32[]{:S(2)}) %collective-permute-start.11) | collective-permute-done | bytes 102432 | tf_op jit(solution)/shard_map/ppermute | solution.py:366
  57.7 3.0 %collective-permute-done.12 = bf16[200,256]{1,0:T(8,128)(2,1)S(1)} collective-permute-done((bf16[200,256]{1,0:T(8,128)(2,1)S(1)}, bf16[200,256]{1,0:T(8,128)(2,1)S(1)}, u32[]{:S(2)}, u32[]{:S(2)}) %collective-permute-start.12) | collective-permute-done | bytes 102432 | tf_op jit(solution)/shard_map/ppermute | solution.py:366
  60.7 1.3 %collective-permute-start.14 = (bf16[200,256]{1,0:T(8,128)(2,1)S(1)}, bf16[200,256]{1,0:T(8,128)(2,1)S(1)}, u32[]{:S(2)}, u32[]{:S(2)}) collective-permute-start(bf16[200,256]{1,0:T(8,128)(2,1)S(1)} %add_convert_fusion.refs_3_), channel_id=1, source_target_pairs={{0,17},{1,16},{2,19},{3,18},{4,21},{5,20},{6,23},{7,22},{8,25},{9,... | collective-permute-start | bytes 307208 | tf_op jit(solution)/shard_map/ppermute | solution.py:401
  62.5 1.7 %collective-permute-start.16 = (bf16[200,256]{1,0:T(8,128)(2,1)S(1)}, bf16[200,256]{1,0:T(8,128)(2,1)S(1)}, u32[]{:S(2)}, u32[]{:S(2)}) collective-permute-start(bf16[200,256]{1,0:T(8,128)(2,1)S(1)} %add_convert_fusion.refs_3_), channel_id=1, source_target_pairs={{0,1},{1,0},{2,3},{3,2},{4,5},{5,4},{6,7},{7,6},{8,9},{9,8},{10,11... | collective-permute-start | bytes 307208 | tf_op jit(solution)/shard_map/ppermute | solution.py:401
  64.3 3.0 %collective-permute-done.14.refs_0_ = bf16[200,256]{1,0:T(8,128)(2,1)S(1)} collective-permute-done((bf16[200,256]{1,0:T(8,128)(2,1)S(1)}, bf16[200,256]{1,0:T(8,128)(2,1)S(1)}, u32[]{:S(2)}, u32[]{:S(2)}) %collective-permute-start.14) | collective-permute-done | bytes 102432 | tf_op jit(solution)/shard_map/ppermute | solution.py:401
  69.6 1.8 %shard_map.144 = (f32[2,256,256]{2,1,0:T(8,128)}, f32[2,256,256]{2,1,0:T(8,128)}, f32[2,256,256]{2,1,0:T(8,128)}, f32[256]{0:T(256)}) custom-call(s32[2]{0:T(128)S(1)} %pad_add_fusion.where_ref.me_ref, bf16[200,256]{1,0:T(8,128)(2,1)S(1)} %collective-permute-done.14.refs_0_, bf16[200,256]{1,0:T(8,128)(2,1)S(1)} %collective-permute-done.15.refs_1_, ...), custom_call_target="tpu_custom_call" | custom-call | tf_op jit(solution)/shard_map/pallas_call | solution.py:339
  (64 shorter events, 8.0 us)
Async XLA Ops:
  2.5 8.8 %collective-permute-start = (bf16[128,128]{1,0:T(8,128)(2,1)S(1)}, bf16[128,128]{1,0:T(8,128)(2,1)S(1)}, u32[]{:S(2)}, u32[]{:S(2)}) collective-permute-start(bf16[128,128]{1,0:T(8,128)(2,1)S(1)} %get-tuple-element.52), channel_id=1, source_target_pairs={{0,7},{1,2},{2,1},{3,4},{4,3},{5,6},{6,5},{7,0},{8,15},{9,10},{10,... | collective-permute-start | bytes 98312 | tf_op jit(solution)/shard_map/ppermute | solution.py:362
  8.6 3.9 %collective-permute-start.1 = (bf16[128,128]{1,0:T(8,128)(2,1)S(1)}, bf16[128,128]{1,0:T(8,128)(2,1)S(1)}, u32[]{:S(2)}, u32[]{:S(2)}) collective-permute-start(bf16[128,128]{1,0:T(8,128)(2,1)S(1)} %get-tuple-element.53), channel_id=1, source_target_pairs={{0,1},{1,0},{2,3},{3,2},{4,5},{5,4},{6,7},{7,6},{8,9},{9,8},{10,11... | collective-permute-start | bytes 98312 | tf_op jit(solution)/shard_map/ppermute | solution.py:362
  12.5 6.5 %copy-start = (s32[2]{0:T(128)S(1)}, s32[2]{0:T(128)}, u32[]{:S(2)}) copy-start(s32[2]{0:T(128)} %param.15) | copy-start | bytes 28
  12.5 6.5 %copy-start.1 = (s32[2,1]{0,1:T(1,128)S(1)}, s32[2,1]{0,1:T(1,128)}, u32[]{:S(2)}) copy-start(s32[2,1]{0,1:T(1,128)} %param.14) | copy-start | bytes 28
  16.3 6.7 %collective-permute-start.2 = (bf16[128,128]{1,0:T(8,128)(2,1)S(1)}, bf16[128,128]{1,0:T(8,128)(2,1)S(1)}, u32[]{:S(2)}, u32[]{:S(2)}) collective-permute-start(bf16[128,128]{1,0:T(8,128)(2,1)S(1)} %get-tuple-element.64), channel_id=1, source_target_pairs={{0,7},{1,2},{2,1},{3,4},{4,3},{5,6},{6,5},{7,0},{8,15},{9,10},{10,... | collective-permute-start | bytes 98312 | tf_op jit(solution)/shard_map/ppermute | solution.py:362
  19.0 4.3 %collective-permute-start.3 = (bf16[128,128]{1,0:T(8,128)(2,1)S(1)}, bf16[128,128]{1,0:T(8,128)(2,1)S(1)}, u32[]{:S(2)}, u32[]{:S(2)}) collective-permute-start(bf16[128,128]{1,0:T(8,128)(2,1)S(1)} %get-tuple-element.65), channel_id=1, source_target_pairs={{0,1},{1,0},{2,3},{3,2},{4,5},{5,4},{6,7},{7,6},{8,9},{9,8},{10,11... | collective-permute-start | bytes 98312 | tf_op jit(solution)/shard_map/ppermute | solution.py:362
  29.7 9.8 %collective-permute-start.7 = (f32[4,104,256]{2,1,0:T(8,128)S(1)}, f32[4,104,256]{2,1,0:T(8,128)S(1)}, u32[]{:S(2)}, u32[]{:S(2)}) collective-permute-start(f32[4,104,256]{2,1,0:T(8,128)S(1)} %slice.88), channel_id=1, source_target_pairs={{0,8},{8,0},{16,24},{24,16},{1,9},{9,1},{17,25},{25,17},{2,10},{10... | collective-permute-start | bytes 1277960 | tf_op jit(solution)/shard_map/ppermute | solution.py:366
  29.7 4.0 %collective-permute-start.4 = (bf16[128,128]{1,0:T(8,128)(2,1)S(1)}, bf16[128,128]{1,0:T(8,128)(2,1)S(1)}, u32[]{:S(2)}, u32[]{:S(2)}) collective-permute-start(bf16[128,128]{1,0:T(8,128)(2,1)S(1)} %get-tuple-element.78), channel_id=1, source_target_pairs={{0,1},{1,0},{2,3},{3,2},{4,5},{5,4},{6,7},{7,6},{8,9},{9,8},{10,11... | collective-permute-start | bytes 98312 | tf_op jit(solution)/shard_map/ppermute | solution.py:362
  29.8 6.7 %collective-permute-start.5 = (bf16[128,128]{1,0:T(8,128)(2,1)S(1)}, bf16[128,128]{1,0:T(8,128)(2,1)S(1)}, u32[]{:S(2)}, u32[]{:S(2)}) collective-permute-start(bf16[128,128]{1,0:T(8,128)(2,1)S(1)} %get-tuple-element.79), channel_id=1, source_target_pairs={{0,7},{1,2},{2,1},{3,4},{4,3},{5,6},{6,5},{7,0},{8,15},{9,10},{10,... | collective-permute-start | bytes 98312 | tf_op jit(solution)/shard_map/ppermute | solution.py:362
  39.3 1.8 %collective-permute-start.6 = (f32[4,96,256]{2,1,0:T(8,128)S(1)}, f32[4,96,256]{2,1,0:T(8,128)S(1)}, u32[]{:S(2)}, u32[]{:S(2)}) collective-permute-start(f32[4,96,256]{2,1,0:T(8,128)S(1)} %slice.113), channel_id=1, source_target_pairs={{0,8},{8,0},{16,24},{24,16},{1,9},{9,1},{17,25},{25,17},{2,10},{10... | collective-permute-start | bytes 1179656 | tf_op jit(solution)/shard_map/ppermute | solution.py:366
  41.6 6.7 %collective-permute-start.10 = (f16[200,256]{1,0:T(8,128)(2,1)S(1)}, f16[200,256]{1,0:T(8,128)(2,1)S(1)}, u32[]{:S(2)}, u32[]{:S(2)}) collective-permute-start(f16[200,256]{1,0:T(8,128)(2,1)S(1)} %get-tuple-element.99), channel_id=1, source_target_pairs={{0,17},{1,16},{2,19},{3,18},{4,21},{5,20},{6,23},{7,22},{8,25},{9,... | collective-permute-start | bytes 307208 | tf_op jit(solution)/shard_map/ppermute | solution.py:401
  42.8 5.7 %collective-permute-start.9 = (f16[200,256]{1,0:T(8,128)(2,1)S(1)}, f16[200,256]{1,0:T(8,128)(2,1)S(1)}, u32[]{:S(2)}, u32[]{:S(2)}) collective-permute-start(f16[200,256]{1,0:T(8,128)(2,1)S(1)} %get-tuple-element.100), channel_id=1, source_target_pairs={{0,16},{1,17},{2,18},{3,19},{4,20},{5,21},{6,22},{7,23},{8,24},{9,... | collective-permute-start | bytes 307208 | tf_op jit(solution)/shard_map/ppermute | solution.py:401
  43.4 6.3 %collective-permute-start.8 = (f16[200,256]{1,0:T(8,128)(2,1)S(1)}, f16[200,256]{1,0:T(8,128)(2,1)S(1)}, u32[]{:S(2)}, u32[]{:S(2)}) collective-permute-start(f16[200,256]{1,0:T(8,128)(2,1)S(1)} %get-tuple-element.101), channel_id=1, source_target_pairs={{0,1},{1,0},{2,3},{3,2},{4,5},{5,4},{6,7},{7,6},{8,9},{9,8},{10,11... | collective-permute-start | bytes 307208 | tf_op jit(solution)/shard_map/ppermute | solution.py:401
  50.0 7.7 %collective-permute-start.11 = (bf16[200,256]{1,0:T(8,128)(2,1)S(1)}, bf16[200,256]{1,0:T(8,128)(2,1)S(1)}, u32[]{:S(2)}, u32[]{:S(2)}) collective-permute-start(bf16[200,256]{1,0:T(8,128)(2,1)S(1)} %fusion.4), channel_id=1, source_target_pairs={{0,6},{2,4},{4,2},{6,0},{1,7},{3,5},{5,3},{7,1},{8,14},{10,12},{12... | collective-permute-start | bytes 307208 | tf_op jit(solution)/shard_map/ppermute | solution.py:366
  51.6 9.1 %collective-permute-start.12 = (bf16[200,256]{1,0:T(8,128)(2,1)S(1)}, bf16[200,256]{1,0:T(8,128)(2,1)S(1)}, u32[]{:S(2)}, u32[]{:S(2)}) collective-permute-start(bf16[200,256]{1,0:T(8,128)(2,1)S(1)} %fusion.4), channel_id=1, source_target_pairs={{0,4},{2,6},{4,0},{6,2},{1,5},{3,7},{5,1},{7,3},{8,12},{10,14},{12... | collective-permute-start | bytes 307208 | tf_op jit(solution)/shard_map/ppermute | solution.py:366
  51.6 9.1 %collective-permute-start.13 = (bf16[200,256]{1,0:T(8,128)(2,1)S(1)}, bf16[200,256]{1,0:T(8,128)(2,1)S(1)}, u32[]{:S(2)}, u32[]{:S(2)}) collective-permute-start(bf16[200,256]{1,0:T(8,128)(2,1)S(1)} %fusion.4), channel_id=1, source_target_pairs={{0,2},{2,0},{4,6},{6,4},{1,3},{3,1},{5,7},{7,5},{8,10},{10,8},{12,... | collective-permute-start | bytes 307208 | tf_op jit(solution)/shard_map/ppermute | solution.py:366
  60.7 6.6 %collective-permute-start.14 = (bf16[200,256]{1,0:T(8,128)(2,1)S(1)}, bf16[200,256]{1,0:T(8,128)(2,1)S(1)}, u32[]{:S(2)}, u32[]{:S(2)}) collective-permute-start(bf16[200,256]{1,0:T(8,128)(2,1)S(1)} %add_convert_fusion.refs_3_), channel_id=1, source_target_pairs={{0,17},{1,16},{2,19},{3,18},{4,21},{5,20},{6,23},{7,22},{8,25},{9,... | collective-permute-start | bytes 307208 | tf_op jit(solution)/shard_map/ppermute | solution.py:401
  62.0 5.5 %collective-permute-start.15 = (bf16[200,256]{1,0:T(8,128)(2,1)S(1)}, bf16[200,256]{1,0:T(8,128)(2,1)S(1)}, u32[]{:S(2)}, u32[]{:S(2)}) collective-permute-start(bf16[200,256]{1,0:T(8,128)(2,1)S(1)} %add_convert_fusion.refs_3_), channel_id=1, source_target_pairs={{0,16},{1,17},{2,18},{3,19},{4,20},{5,21},{6,22},{7,23},{8,24},{9,... | collective-permute-start | bytes 307208 | tf_op jit(solution)/shard_map/ppermute | solution.py:401
  62.5 5.8 %collective-permute-start.16 = (bf16[200,256]{1,0:T(8,128)(2,1)S(1)}, bf16[200,256]{1,0:T(8,128)(2,1)S(1)}, u32[]{:S(2)}, u32[]{:S(2)}) collective-permute-start(bf16[200,256]{1,0:T(8,128)(2,1)S(1)} %add_convert_fusion.refs_3_), channel_id=1, source_target_pairs={{0,1},{1,0},{2,3},{3,2},{4,5},{5,4},{6,7},{7,6},{8,9},{9,8},{10,11... | collective-permute-start | bytes 307208 | tf_op jit(solution)/shard_map/ppermute | solution.py:401
  64.3 4.0 %collective-permute-start.20 = (bf16[200,256]{1,0:T(8,128)(2,1)S(1)}, bf16[200,256]{1,0:T(8,128)(2,1)S(1)}, u32[]{:S(2)}, u32[]{:S(2)}) collective-permute-start(bf16[200,256]{1,0:T(8,128)(2,1)S(1)} %add_convert_fusion.refs_3_), channel_id=1, source_target_pairs={{0,8},{8,0},{16,24},{24,16},{1,9},{9,1},{17,25},{25,17},{2,10},{10... | collective-permute-start | bytes 307208 | tf_op jit(solution)/shard_map/ppermute | solution.py:366
  67.3 1.3 %collective-permute-start.17 = (bf16[200,256]{1,0:T(8,128)(2,1)S(1)}, bf16[200,256]{1,0:T(8,128)(2,1)S(1)}, u32[]{:S(2)}, u32[]{:S(2)}) collective-permute-start(bf16[200,256]{1,0:T(8,128)(2,1)S(1)} %collective-permute-done.14.refs_0_), channel_id=1, source_target_pairs={{0,8},{8,0},{16,24},{24,16},{1,9},{9,1},{17,25},{25,17},{2,10},{10... | collective-permute-start | bytes 307208 | tf_op jit(solution)/shard_map/ppermute | solution.py:366
  67.5 1.3 %collective-permute-start.18 = (bf16[200,256]{1,0:T(8,128)(2,1)S(1)}, bf16[200,256]{1,0:T(8,128)(2,1)S(1)}, u32[]{:S(2)}, u32[]{:S(2)}) collective-permute-start(bf16[200,256]{1,0:T(8,128)(2,1)S(1)} %collective-permute-done.15.refs_1_), channel_id=1, source_target_pairs={{0,8},{8,0},{16,24},{24,16},{1,9},{9,1},{17,25},{25,17},{2,10},{10... | collective-permute-start | bytes 307208 | tf_op jit(solution)/shard_map/ppermute | solution.py:366
  68.3 1.3 %collective-permute-start.19 = (bf16[200,256]{1,0:T(8,128)(2,1)S(1)}, bf16[200,256]{1,0:T(8,128)(2,1)S(1)}, u32[]{:S(2)}, u32[]{:S(2)}) collective-permute-start(bf16[200,256]{1,0:T(8,128)(2,1)S(1)} %collective-permute-done.16.refs_2_), channel_id=1, source_target_pairs={{0,8},{8,0},{16,24},{24,16},{1,9},{9,1},{17,25},{25,17},{2,10},{10... | collective-permute-start | bytes 307208 | tf_op jit(solution)/shard_map/ppermute | solution.py:366

commit v5 on v4

--- a/solution.py
+++ b/solution.py
@@ -534,7 +534,6 @@
         smem=1,
         flops=10**8,
     )
-    upper_part = core_sum(upper_slots)
     lower_slots = kernel_call(
         lower_kernel,
         near((8, 3 * chunk, channels), F32),
@@ -545,7 +544,7 @@
         smem=1,
         flops=4 * 10**9,
     )
-    close = reduce_parts([core_sum(lower_slots), upper_part])
+    close = reduce_parts([jnp.concatenate([lower_slots[:4], upper_slots[:4]], axis=1) + partner(jnp.concatenate([lower_slots[4:], upper_slots[4:]], axis=1), "rep", 1)])
     far = [partner(value, "rep", 1) for value in close]
     grad = jax.ShapeDtypeStruct((layers, channels, hidden), F32)
     grad_wa, grad_wc, grad_wb, grad_readout = kernel_call(

time: 71.6 us -> 71.2 us (level)
    ppermute x6, waiting for transfers between devices: 8.77 us -> 7.81 us  [swapped(): return lax.ppermute(value, RING, pairs)]
    ppermute x9 -> x8, waiting for transfers between devices: 9.19 us -> 9.89 us  [partner(): lax.ppermute(value, axis, [(s, s ^ bits) for s in range(lax.axis_size(axi...]
    ppermute x9 -> x8, starting transfers between devices: 4.91 us -> 4.91 us  [partner(): lax.ppermute(value, axis, [(s, s ^ bits) for s in range(lax.axis_size(axi...]
  transfers between devices with their start and end apart: 21 -> 20, of which waited for: 17 -> 17; matrix products, arithmetic and copies ran while one was open for 0% -> 0% of each run, Pallas kernels for 9% -> 6%
where the time goes in v5:
time: 71.2 us; the launch traced here: 71.1 us
  waiting for transfers between devices  25.7 us (36%)
  starting transfers between devices  23.2 us (33%)
  Pallas kernels  20 us (28%)
  other arithmetic  0.97 us (1%)
  between operations  0.93 us (1%)
    pallas_call x8, Pallas kernels, kernel_call(): pl.pallas_call(body, out_shape=outs, in_specs=[pl.BlockSpec(memory_space=...  20 us
    ppermute x6, starting transfers between devices, swapped(): return lax.ppermute(value, RING, pairs)  11.2 us
    ppermute x8, waiting for transfers between devices, partner(): lax.ppermute(value, axis, [(s, s ^ bits) for s in range(lax.axis_size(axi...  9.89 us
    ppermute x6, waiting for transfers between devices, plane(): lax.ppermute(value, EVERY, [(s, s ^ flip) for s in range(rep * dom * tp)])  8.02 us
    ppermute x6, waiting for transfers between devices, swapped(): return lax.ppermute(value, RING, pairs)  7.81 us
    ppermute x6, starting transfers between devices, plane(): lax.ppermute(value, EVERY, [(s, s ^ flip) for s in range(rep * dom * tp)])  7.11 us
    ppermute x8, starting transfers between devices, partner(): lax.ppermute(value, axis, [(s, s ^ bits) for s in range(lax.axis_size(axi...  4.91 us
  transfers between devices with their start and end apart: 20, of which 17 were waited for; matrix products, arithmetic and copies ran while one was open for 0% of the time, Pallas kernels for 6%

profile of v5, /device:TPU:0, one launch (start us, length us, event | category | flops | bytes accessed | tf_op | source)
XLA Modules:
  0.0 71.1 jit_solution(2044510835486203136)
XLA Ops:
  0.7 1.8 %shard_map.137 = (bf16[256,256]{1,0:T(8,128)(2,1)S(1)}, bf16[256,128]{1,0:T(8,128)(2,1)S(1)}, bf16[128,128]{1,0:T(8,128)(2,1)S(1)}, bf16[128,128]{1,0:T(8,128)(2...) custom-call(s32[2]{0:T(128)S(1)} %pad_add_fusion.where_ref.me_ref, bf16[2,128,256]{2,1,0:T(8,128)(2,1)} %feat_hbm.1, ...), custom_call_target="tpu_custom_call" | custom-call | tf_op jit(solution)/shard_map/pallas_call | solution.py:339
  2.5 6.1 %collective-permute-start = (bf16[128,128]{1,0:T(8,128)(2,1)S(1)}, bf16[128,128]{1,0:T(8,128)(2,1)S(1)}, u32[]{:S(2)}, u32[]{:S(2)}) collective-permute-start(bf16[128,128]{1,0:T(8,128)(2,1)S(1)} %get-tuple-element.52), channel_id=1, source_target_pairs={{0,7},{1,2},{2,1},{3,4},{4,3},{5,6},{6,5},{7,0},{8,15},{9,10},{10,... | collective-permute-start | bytes 98312 | tf_op jit(solution)/shard_map/ppermute | solution.py:362
  8.6 2.7 %shard_map.138 = (bf16[2,256,4096]{2,1,0:T(8,128)(2,1)S(1)}, bf16[2,32,16,128]{3,2,1,0:T(8,128)(2,1)S(1)}, bf16[2,256,256]{2,1,0:T(8,128)(2,1)S(1)}, bf16[2,256,...) custom-call(s32[2]{0:T(128)S(1)} %pad_add_fusion.where_ref.me_ref, ...), custom_call_target="tpu_custom_call" | custom-call | flops 2000000000 | tf_op jit(solution)/shard_map/pallas_call | solution.py:339
  11.3 1.2 %collective-permute-done.1.hf_ref = bf16[128,128]{1,0:T(8,128)(2,1)S(1)} collective-permute-done((bf16[128,128]{1,0:T(8,128)(2,1)S(1)}, bf16[128,128]{1,0:T(8,128)(2,1)S(1)}, u32[]{:S(2)}, u32[]{:S(2)}) %collective-permute-start.1) | collective-permute-done | bytes 32800 | tf_op jit(solution)/shard_map/ppermute | solution.py:362
  12.5 3.7 %shard_map.139 = (bf16[256,256]{1,0:T(8,128)(2,1)S(1)}, bf16[128,128]{1,0:T(8,128)(2,1)S(1)}, bf16[128,128]{1,0:T(8,128)(2,1)S(1)}, bf16[256,128]{1,0:T(8,128)(2...) custom-call(bf16[128,128]{1,0:T(8,128)(2,1)S(1)} %collective-permute-done.hs_ref, ...), custom_call_target="tpu_custom_call" | custom-call | flops 4000000000 | tf_op jit(solution)/shard_map/pallas_call | solution.py:339
  16.3 2.8 %collective-permute-start.2 = (bf16[128,128]{1,0:T(8,128)(2,1)S(1)}, bf16[128,128]{1,0:T(8,128)(2,1)S(1)}, u32[]{:S(2)}, u32[]{:S(2)}) collective-permute-start(bf16[128,128]{1,0:T(8,128)(2,1)S(1)} %get-tuple-element.64), channel_id=1, source_target_pairs={{0,7},{1,2},{2,1},{3,4},{4,3},{5,6},{6,5},{7,0},{8,15},{9,10},{10,... | collective-permute-start | bytes 98312 | tf_op jit(solution)/shard_map/ppermute | solution.py:362
  20.0 3.1 %collective-permute-done.2.hs_ref = bf16[128,128]{1,0:T(8,128)(2,1)S(1)} collective-permute-done((bf16[128,128]{1,0:T(8,128)(2,1)S(1)}, bf16[128,128]{1,0:T(8,128)(2,1)S(1)}, u32[]{:S(2)}, u32[]{:S(2)}) %collective-permute-start.2) | collective-permute-done | bytes 32800 | tf_op jit(solution)/shard_map/ppermute | solution.py:362
  23.3 5.4 %shard_map.141 = (f32[2,128]{1,0:T(2,128)}, f32[16,256]{1,0:T(8,128)S(1)}, f32[256,256]{1,0:T(8,128)S(1)}, bf16[128,128]{1,0:T(8,128)(2,1)S(1)}, bf16[128,128]{1...) custom-call(bf16[128,128]{1,0:T(8,128)(2,1)S(1)} %collective-permute, ...), custom_call_target="tpu_custom_call" | custom-call | flops 6000000000 | tf_op jit(solution)/shard_map/pallas_call | solution.py:339
  28.7 2.4 %collective-permute-start.5 = (bf16[128,128]{1,0:T(8,128)(2,1)S(1)}, bf16[128,128]{1,0:T(8,128)(2,1)S(1)}, u32[]{:S(2)}, u32[]{:S(2)}) collective-permute-start(bf16[128,128]{1,0:T(8,128)(2,1)S(1)} %get-tuple-element.79), channel_id=1, source_target_pairs={{0,7},{1,2},{2,1},{3,4},{4,3},{5,6},{6,5},{7,0},{8,15},{9,10},{10,... | collective-permute-start | bytes 98312 | tf_op jit(solution)/shard_map/ppermute | solution.py:362
  32.6 2.7 %collective-permute-done.5.bs_ref = bf16[128,128]{1,0:T(8,128)(2,1)S(1)} collective-permute-done((bf16[128,128]{1,0:T(8,128)(2,1)S(1)}, bf16[128,128]{1,0:T(8,128)(2,1)S(1)}, u32[]{:S(2)}, u32[]{:S(2)}) %collective-permute-start.5) | collective-permute-done | bytes 32800 | tf_op jit(solution)/shard_map/ppermute | solution.py:362
  35.3 2.8 %shard_map.143 = f32[8,96,256]{2,1,0:T(8,128)S(1)} custom-call(s32[2]{0:T(128)S(1)} %pad_add_fusion.where_ref.me_ref, bf16[128,128]{1,0:T(8,128)(2,1)S(1)} %collective-permute-done.4.bf_ref, bf16[128,128]{1,0:T(8,128)(2,1)S(1)} %collective-permute-done.5.bs_ref, bf16[256,128]{1,0:T(8,128)(2,1)S(1)} %get-tuple-element.63.select_ref, ...), custom_call_target="tpu_custom_call" | custom-call | flops 4000000000 | tf_op jit(solution)/shard_map/pallas_call | solution.py:339
  38.3 2.3 %collective-permute-done.6 = f32[4,200,256]{2,1,0:T(8,128)S(1)} collective-permute-done((f32[4,200,256]{2,1,0:T(8,128)S(1)}, f32[4,200,256]{2,1,0:T(8,128)S(1)}, u32[]{:S(2)}, u32[]{:S(2)}) %collective-permute-start.6) | collective-permute-done | bytes 819232 | tf_op jit(solution)/shard_map/ppermute | solution.py:366
  41.2 1.2 %collective-permute-start.9 = (f16[200,256]{1,0:T(8,128)(2,1)S(1)}, f16[200,256]{1,0:T(8,128)(2,1)S(1)}, u32[]{:S(2)}, u32[]{:S(2)}) collective-permute-start(f16[200,256]{1,0:T(8,128)(2,1)S(1)} %get-tuple-element.103), channel_id=1, source_target_pairs={{0,17},{1,16},{2,19},{3,18},{4,21},{5,20},{6,23},{7,22},{8,25},{9,... | collective-permute-start | bytes 307208 | tf_op jit(solution)/shard_map/ppermute | solution.py:401
  43.1 1.8 %collective-permute-start.7 = (f16[200,256]{1,0:T(8,128)(2,1)S(1)}, f16[200,256]{1,0:T(8,128)(2,1)S(1)}, u32[]{:S(2)}, u32[]{:S(2)}) collective-permute-start(f16[200,256]{1,0:T(8,128)(2,1)S(1)} %get-tuple-element.105), channel_id=1, source_target_pairs={{0,1},{1,0},{2,3},{3,2},{4,5},{5,4},{6,7},{7,6},{8,9},{9,8},{10,11... | collective-permute-start | bytes 307208 | tf_op jit(solution)/shard_map/ppermute | solution.py:401
  44.9 3.1 %collective-permute-done.9 = f16[200,256]{1,0:T(8,128)(2,1)S(1)} collective-permute-done((f16[200,256]{1,0:T(8,128)(2,1)S(1)}, f16[200,256]{1,0:T(8,128)(2,1)S(1)}, u32[]{:S(2)}, u32[]{:S(2)}) %collective-permute-start.9) | collective-permute-done | bytes 102432 | tf_op jit(solution)/shard_map/ppermute | solution.py:401
  48.2 1.1 %collective-permute-done.7 = f16[200,256]{1,0:T(8,128)(2,1)S(1)} collective-permute-done((f16[200,256]{1,0:T(8,128)(2,1)S(1)}, f16[200,256]{1,0:T(8,128)(2,1)S(1)}, u32[]{:S(2)}, u32[]{:S(2)}) %collective-permute-start.7) | collective-permute-done | bytes 102432 | tf_op jit(solution)/shard_map/ppermute | solution.py:401
  49.6 1.6 %collective-permute-start.10 = (bf16[200,256]{1,0:T(8,128)(2,1)S(1)}, bf16[200,256]{1,0:T(8,128)(2,1)S(1)}, u32[]{:S(2)}, u32[]{:S(2)}) collective-permute-start(bf16[200,256]{1,0:T(8,128)(2,1)S(1)} %fusion.3), channel_id=1, source_target_pairs={{0,6},{2,4},{4,2},{6,0},{1,7},{3,5},{5,3},{7,1},{8,14},{10,12},{12... | collective-permute-start | bytes 307208 | tf_op jit(solution)/shard_map/ppermute | solution.py:366
  51.2 2.8 %collective-permute-start.12 = (bf16[200,256]{1,0:T(8,128)(2,1)S(1)}, bf16[200,256]{1,0:T(8,128)(2,1)S(1)}, u32[]{:S(2)}, u32[]{:S(2)}) collective-permute-start(bf16[200,256]{1,0:T(8,128)(2,1)S(1)} %fusion.3), channel_id=1, source_target_pairs={{0,2},{2,0},{4,6},{6,4},{1,3},{3,1},{5,7},{7,5},{8,10},{10,8},{12,... | collective-permute-start | bytes 307208 | tf_op jit(solution)/shard_map/ppermute | solution.py:366
  54.0 3.2 %collective-permute-done.10 = bf16[200,256]{1,0:T(8,128)(2,1)S(1)} collective-permute-done((bf16[200,256]{1,0:T(8,128)(2,1)S(1)}, bf16[200,256]{1,0:T(8,128)(2,1)S(1)}, u32[]{:S(2)}, u32[]{:S(2)}) %collective-permute-start.10) | collective-permute-done | bytes 102432 | tf_op jit(solution)/shard_map/ppermute | solution.py:366
  57.2 3.0 %collective-permute-done.11 = bf16[200,256]{1,0:T(8,128)(2,1)S(1)} collective-permute-done((bf16[200,256]{1,0:T(8,128)(2,1)S(1)}, bf16[200,256]{1,0:T(8,128)(2,1)S(1)}, u32[]{:S(2)}, u32[]{:S(2)}) %collective-permute-start.11) | collective-permute-done | bytes 102432 | tf_op jit(solution)/shard_map/ppermute | solution.py:366
  60.4 1.3 %collective-permute-start.13 = (bf16[200,256]{1,0:T(8,128)(2,1)S(1)}, bf16[200,256]{1,0:T(8,128)(2,1)S(1)}, u32[]{:S(2)}, u32[]{:S(2)}) collective-permute-start(bf16[200,256]{1,0:T(8,128)(2,1)S(1)} %add_convert_fusion.refs_3_), channel_id=1, source_target_pairs={{0,17},{1,16},{2,19},{3,18},{4,21},{5,20},{6,23},{7,22},{8,25},{9,... | collective-permute-start | bytes 307208 | tf_op jit(solution)/shard_map/ppermute | solution.py:401
  62.2 1.8 %collective-permute-start.15 = (bf16[200,256]{1,0:T(8,128)(2,1)S(1)}, bf16[200,256]{1,0:T(8,128)(2,1)S(1)}, u32[]{:S(2)}, u32[]{:S(2)}) collective-permute-start(bf16[200,256]{1,0:T(8,128)(2,1)S(1)} %add_convert_fusion.refs_3_), channel_id=1, source_target_pairs={{0,1},{1,0},{2,3},{3,2},{4,5},{5,4},{6,7},{7,6},{8,9},{9,8},{10,11... | collective-permute-start | bytes 307208 | tf_op jit(solution)/shard_map/ppermute | solution.py:401
  63.9 3.1 %collective-permute-done.13.refs_0_ = bf16[200,256]{1,0:T(8,128)(2,1)S(1)} collective-permute-done((bf16[200,256]{1,0:T(8,128)(2,1)S(1)}, bf16[200,256]{1,0:T(8,128)(2,1)S(1)}, u32[]{:S(2)}, u32[]{:S(2)}) %collective-permute-start.13) | collective-permute-done | bytes 102432 | tf_op jit(solution)/shard_map/ppermute | solution.py:401
  69.3 1.8 %shard_map.144 = (f32[2,256,256]{2,1,0:T(8,128)}, f32[2,256,256]{2,1,0:T(8,128)}, f32[2,256,256]{2,1,0:T(8,128)}, f32[256]{0:T(256)}) custom-call(s32[2]{0:T(128)S(1)} %pad_add_fusion.where_ref.me_ref, bf16[200,256]{1,0:T(8,128)(2,1)S(1)} %collective-permute-done.13.refs_0_, bf16[200,256]{1,0:T(8,128)(2,1)S(1)} %collective-permute-done.14.refs_1_, ...), custom_call_target="tpu_custom_call" | custom-call | tf_op jit(solution)/shard_map/pallas_call | solution.py:339
  (62 shorter events, 7.4 us)
Async XLA Ops:
  2.5 8.8 %collective-permute-start = (bf16[128,128]{1,0:T(8,128)(2,1)S(1)}, bf16[128,128]{1,0:T(8,128)(2,1)S(1)}, u32[]{:S(2)}, u32[]{:S(2)}) collective-permute-start(bf16[128,128]{1,0:T(8,128)(2,1)S(1)} %get-tuple-element.52), channel_id=1, source_target_pairs={{0,7},{1,2},{2,1},{3,4},{4,3},{5,6},{6,5},{7,0},{8,15},{9,10},{10,... | collective-permute-start | bytes 98312 | tf_op jit(solution)/shard_map/ppermute | solution.py:362
  8.6 3.9 %collective-permute-start.1 = (bf16[128,128]{1,0:T(8,128)(2,1)S(1)}, bf16[128,128]{1,0:T(8,128)(2,1)S(1)}, u32[]{:S(2)}, u32[]{:S(2)}) collective-permute-start(bf16[128,128]{1,0:T(8,128)(2,1)S(1)} %get-tuple-element.53), channel_id=1, source_target_pairs={{0,1},{1,0},{2,3},{3,2},{4,5},{5,4},{6,7},{7,6},{8,9},{9,8},{10,11... | collective-permute-start | bytes 98312 | tf_op jit(solution)/shard_map/ppermute | solution.py:362
  12.5 6.5 %copy-start = (s32[2]{0:T(128)S(1)}, s32[2]{0:T(128)}, u32[]{:S(2)}) copy-start(s32[2]{0:T(128)} %param.15) | copy-start | bytes 28
  12.5 6.5 %copy-start.1 = (s32[2,1]{0,1:T(1,128)S(1)}, s32[2,1]{0,1:T(1,128)}, u32[]{:S(2)}) copy-start(s32[2,1]{0,1:T(1,128)} %param.14) | copy-start | bytes 28
  16.3 6.8 %collective-permute-start.2 = (bf16[128,128]{1,0:T(8,128)(2,1)S(1)}, bf16[128,128]{1,0:T(8,128)(2,1)S(1)}, u32[]{:S(2)}, u32[]{:S(2)}) collective-permute-start(bf16[128,128]{1,0:T(8,128)(2,1)S(1)} %get-tuple-element.64), channel_id=1, source_target_pairs={{0,7},{1,2},{2,1},{3,4},{4,3},{5,6},{6,5},{7,0},{8,15},{9,10},{10,... | collective-permute-start | bytes 98312 | tf_op jit(solution)/shard_map/ppermute | solution.py:362
  19.0 4.3 %collective-permute-start.3 = (bf16[128,128]{1,0:T(8,128)(2,1)S(1)}, bf16[128,128]{1,0:T(8,128)(2,1)S(1)}, u32[]{:S(2)}, u32[]{:S(2)}) collective-permute-start(bf16[128,128]{1,0:T(8,128)(2,1)S(1)} %get-tuple-element.65), channel_id=1, source_target_pairs={{0,1},{1,0},{2,3},{3,2},{4,5},{5,4},{6,7},{7,6},{8,9},{9,8},{10,11... | collective-permute-start | bytes 98312 | tf_op jit(solution)/shard_map/ppermute | solution.py:362
  28.7 3.9 %collective-permute-start.4 = (bf16[128,128]{1,0:T(8,128)(2,1)S(1)}, bf16[128,128]{1,0:T(8,128)(2,1)S(1)}, u32[]{:S(2)}, u32[]{:S(2)}) collective-permute-start(bf16[128,128]{1,0:T(8,128)(2,1)S(1)} %get-tuple-element.78), channel_id=1, source_target_pairs={{0,1},{1,0},{2,3},{3,2},{4,5},{5,4},{6,7},{7,6},{8,9},{9,8},{10,11... | collective-permute-start | bytes 98312 | tf_op jit(solution)/shard_map/ppermute | solution.py:362
  28.7 6.6 %collective-permute-start.5 = (bf16[128,128]{1,0:T(8,128)(2,1)S(1)}, bf16[128,128]{1,0:T(8,128)(2,1)S(1)}, u32[]{:S(2)}, u32[]{:S(2)}) collective-permute-start(bf16[128,128]{1,0:T(8,128)(2,1)S(1)} %get-tuple-element.79), channel_id=1, source_target_pairs={{0,7},{1,2},{2,1},{3,4},{4,3},{5,6},{6,5},{7,0},{8,15},{9,10},{10,... | collective-permute-start | bytes 98312 | tf_op jit(solution)/shard_map/ppermute | solution.py:362
  38.3 2.4 %collective-permute-start.6 = (f32[4,200,256]{2,1,0:T(8,128)S(1)}, f32[4,200,256]{2,1,0:T(8,128)S(1)}, u32[]{:S(2)}, u32[]{:S(2)}) collective-permute-start(f32[4,200,256]{2,1,0:T(8,128)S(1)} %pad_maximum_fusion), channel_id=1, source_target_pairs={{0,8},{8,0},{16,24},{24,16},{1,9},{9,1},{17,25},{25,17},{2,10},{10... | collective-permute-start | bytes 2457608 | tf_op jit(solution)/shard_map/ppermute | solution.py:366
  41.2 6.7 %collective-permute-start.9 = (f16[200,256]{1,0:T(8,128)(2,1)S(1)}, f16[200,256]{1,0:T(8,128)(2,1)S(1)}, u32[]{:S(2)}, u32[]{:S(2)}) collective-permute-start(f16[200,256]{1,0:T(8,128)(2,1)S(1)} %get-tuple-element.103), channel_id=1, source_target_pairs={{0,17},{1,16},{2,19},{3,18},{4,21},{5,20},{6,23},{7,22},{8,25},{9,... | collective-permute-start | bytes 307208 | tf_op jit(solution)/shard_map/ppermute | solution.py:401
  42.5 5.6 %collective-permute-start.8 = (f16[200,256]{1,0:T(8,128)(2,1)S(1)}, f16[200,256]{1,0:T(8,128)(2,1)S(1)}, u32[]{:S(2)}, u32[]{:S(2)}) collective-permute-start(f16[200,256]{1,0:T(8,128)(2,1)S(1)} %get-tuple-element.104), channel_id=1, source_target_pairs={{0,16},{1,17},{2,18},{3,19},{4,20},{5,21},{6,22},{7,23},{8,24},{9,... | collective-permute-start | bytes 307208 | tf_op jit(solution)/shard_map/ppermute | solution.py:401
  43.1 6.2 %collective-permute-start.7 = (f16[200,256]{1,0:T(8,128)(2,1)S(1)}, f16[200,256]{1,0:T(8,128)(2,1)S(1)}, u32[]{:S(2)}, u32[]{:S(2)}) collective-permute-start(f16[200,256]{1,0:T(8,128)(2,1)S(1)} %get-tuple-element.105), channel_id=1, source_target_pairs={{0,1},{1,0},{2,3},{3,2},{4,5},{5,4},{6,7},{7,6},{8,9},{9,8},{10,11... | collective-permute-start | bytes 307208 | tf_op jit(solution)/shard_map/ppermute | solution.py:401
  49.6 7.7 %collective-permute-start.10 = (bf16[200,256]{1,0:T(8,128)(2,1)S(1)}, bf16[200,256]{1,0:T(8,128)(2,1)S(1)}, u32[]{:S(2)}, u32[]{:S(2)}) collective-permute-start(bf16[200,256]{1,0:T(8,128)(2,1)S(1)} %fusion.3), channel_id=1, source_target_pairs={{0,6},{2,4},{4,2},{6,0},{1,7},{3,5},{5,3},{7,1},{8,14},{10,12},{12... | collective-permute-start | bytes 307208 | tf_op jit(solution)/shard_map/ppermute | solution.py:366
  51.2 9.1 %collective-permute-start.11 = (bf16[200,256]{1,0:T(8,128)(2,1)S(1)}, bf16[200,256]{1,0:T(8,128)(2,1)S(1)}, u32[]{:S(2)}, u32[]{:S(2)}) collective-permute-start(bf16[200,256]{1,0:T(8,128)(2,1)S(1)} %fusion.3), channel_id=1, source_target_pairs={{0,4},{2,6},{4,0},{6,2},{1,5},{3,7},{5,1},{7,3},{8,12},{10,14},{12... | collective-permute-start | bytes 307208 | tf_op jit(solution)/shard_map/ppermute | solution.py:366
  51.2 9.1 %collective-permute-start.12 = (bf16[200,256]{1,0:T(8,128)(2,1)S(1)}, bf16[200,256]{1,0:T(8,128)(2,1)S(1)}, u32[]{:S(2)}, u32[]{:S(2)}) collective-permute-start(bf16[200,256]{1,0:T(8,128)(2,1)S(1)} %fusion.3), channel_id=1, source_target_pairs={{0,2},{2,0},{4,6},{6,4},{1,3},{3,1},{5,7},{7,5},{8,10},{10,8},{12,... | collective-permute-start | bytes 307208 | tf_op jit(solution)/shard_map/ppermute | solution.py:366
  60.4 6.6 %collective-permute-start.13 = (bf16[200,256]{1,0:T(8,128)(2,1)S(1)}, bf16[200,256]{1,0:T(8,128)(2,1)S(1)}, u32[]{:S(2)}, u32[]{:S(2)}) collective-permute-start(bf16[200,256]{1,0:T(8,128)(2,1)S(1)} %add_convert_fusion.refs_3_), channel_id=1, source_target_pairs={{0,17},{1,16},{2,19},{3,18},{4,21},{5,20},{6,23},{7,22},{8,25},{9,... | collective-permute-start | bytes 307208 | tf_op jit(solution)/shard_map/ppermute | solution.py:401
  61.6 5.5 %collective-permute-start.14 = (bf16[200,256]{1,0:T(8,128)(2,1)S(1)}, bf16[200,256]{1,0:T(8,128)(2,1)S(1)}, u32[]{:S(2)}, u32[]{:S(2)}) collective-permute-start(bf16[200,256]{1,0:T(8,128)(2,1)S(1)} %add_convert_fusion.refs_3_), channel_id=1, source_target_pairs={{0,16},{1,17},{2,18},{3,19},{4,20},{5,21},{6,22},{7,23},{8,24},{9,... | collective-permute-start | bytes 307208 | tf_op jit(solution)/shard_map/ppermute | solution.py:401
  62.2 5.8 %collective-permute-start.15 = (bf16[200,256]{1,0:T(8,128)(2,1)S(1)}, bf16[200,256]{1,0:T(8,128)(2,1)S(1)}, u32[]{:S(2)}, u32[]{:S(2)}) collective-permute-start(bf16[200,256]{1,0:T(8,128)(2,1)S(1)} %add_convert_fusion.refs_3_), channel_id=1, source_target_pairs={{0,1},{1,0},{2,3},{3,2},{4,5},{5,4},{6,7},{7,6},{8,9},{9,8},{10,11... | collective-permute-start | bytes 307208 | tf_op jit(solution)/shard_map/ppermute | solution.py:401
  63.9 4.1 %collective-permute-start.19 = (bf16[200,256]{1,0:T(8,128)(2,1)S(1)}, bf16[200,256]{1,0:T(8,128)(2,1)S(1)}, u32[]{:S(2)}, u32[]{:S(2)}) collective-permute-start(bf16[200,256]{1,0:T(8,128)(2,1)S(1)} %add_convert_fusion.refs_3_), channel_id=1, source_target_pairs={{0,8},{8,0},{16,24},{24,16},{1,9},{9,1},{17,25},{25,17},{2,10},{10... | collective-permute-start | bytes 307208 | tf_op jit(solution)/shard_map/ppermute | solution.py:366
  67.0 1.3 %collective-permute-start.16 = (bf16[200,256]{1,0:T(8,128)(2,1)S(1)}, bf16[200,256]{1,0:T(8,128)(2,1)S(1)}, u32[]{:S(2)}, u32[]{:S(2)}) collective-permute-start(bf16[200,256]{1,0:T(8,128)(2,1)S(1)} %collective-permute-done.13.refs_0_), channel_id=1, source_target_pairs={{0,8},{8,0},{16,24},{24,16},{1,9},{9,1},{17,25},{25,17},{2,10},{10... | collective-permute-start | bytes 307208 | tf_op jit(solution)/shard_map/ppermute | solution.py:366
  67.1 1.3 %collective-permute-start.17 = (bf16[200,256]{1,0:T(8,128)(2,1)S(1)}, bf16[200,256]{1,0:T(8,128)(2,1)S(1)}, u32[]{:S(2)}, u32[]{:S(2)}) collective-permute-start(bf16[200,256]{1,0:T(8,128)(2,1)S(1)} %collective-permute-done.14.refs_1_), channel_id=1, source_target_pairs={{0,8},{8,0},{16,24},{24,16},{1,9},{9,1},{17,25},{25,17},{2,10},{10... | collective-permute-start | bytes 307208 | tf_op jit(solution)/shard_map/ppermute | solution.py:366
  68.0 1.3 %collective-permute-start.18 = (bf16[200,256]{1,0:T(8,128)(2,1)S(1)}, bf16[200,256]{1,0:T(8,128)(2,1)S(1)}, u32[]{:S(2)}, u32[]{:S(2)}) collective-permute-start(bf16[200,256]{1,0:T(8,128)(2,1)S(1)} %collective-permute-done.15.refs_2_), channel_id=1, source_target_pairs={{0,8},{8,0},{16,24},{24,16},{1,9},{9,1},{17,25},{25,17},{2,10},{10... | collective-permute-start | bytes 307208 | tf_op jit(solution)/shard_map/ppermute | solution.py:366

commit v6 on v5

--- a/solution.py
+++ b/solution.py
@@ -404,7 +404,7 @@
 def along_dom(mine):
     count, bit = lax.axis_size("dom"), 1
     while bit < count:
-        flips = [bit] if 2 * bit >= count else [3 * bit, 2 * bit, bit]
+        flips = [bit] if 2 * bit >= count else [2 * bit, 3 * bit, bit]
         mine = summed(mine, *[partner(mine, "dom", flip) for flip in flips])
         bit *= 4
     return mine

time: 71.2 us -> 70.8 us (level)
  starting transfers between devices: 23.2 us -> 22.1 us
    ppermute x8, starting transfers between devices: 4.91 us -> 3.77 us  [partner(): lax.ppermute(value, axis, [(s, s ^ bits) for s in range(lax.axis_size(axi...]
where the time goes in v6:
time: 70.8 us; the launch traced here: 70.6 us
  waiting for transfers between devices  26.4 us (37%)
  starting transfers between devices  22.1 us (31%)
  Pallas kernels  20 us (28%)
  other arithmetic  0.97 us (1%)
  between operations  0.94 us (1%)
    pallas_call x8, Pallas kernels, kernel_call(): pl.pallas_call(body, out_shape=outs, in_specs=[pl.BlockSpec(memory_space=...  20 us
    ppermute x6, starting transfers between devices, swapped(): return lax.ppermute(value, RING, pairs)  11.2 us
    ppermute x8, waiting for transfers between devices, partner(): lax.ppermute(value, axis, [(s, s ^ bits) for s in range(lax.axis_size(axi...  10.3 us
    ppermute x6, waiting for transfers between devices, plane(): lax.ppermute(value, EVERY, [(s, s ^ flip) for s in range(rep * dom * tp)])  8.32 us
    ppermute x6, waiting for transfers between devices, swapped(): return lax.ppermute(value, RING, pairs)  7.81 us
    ppermute x6, starting transfers between devices, plane(): lax.ppermute(value, EVERY, [(s, s ^ flip) for s in range(rep * dom * tp)])  7.11 us
    ppermute x8, starting transfers between devices, partner(): lax.ppermute(value, axis, [(s, s ^ bits) for s in range(lax.axis_size(axi...  3.77 us
  transfers between devices with their start and end apart: 20, of which 17 were waited for; matrix products, arithmetic and copies ran while one was open for 0% of the time, Pallas kernels for 6%

profile of v6, /device:TPU:0, one launch (start us, length us, event | category | flops | bytes accessed | tf_op | source)
XLA Modules:
  0.0 70.6 jit_solution(18085214410647159506)
XLA Ops:
  0.7 1.8 %shard_map.137 = (bf16[256,256]{1,0:T(8,128)(2,1)S(1)}, bf16[256,128]{1,0:T(8,128)(2,1)S(1)}, bf16[128,128]{1,0:T(8,128)(2,1)S(1)}, bf16[128,128]{1,0:T(8,128)(2...) custom-call(s32[2]{0:T(128)S(1)} %pad_add_fusion.where_ref.me_ref, bf16[2,128,256]{2,1,0:T(8,128)(2,1)} %feat_hbm.1, ...), custom_call_target="tpu_custom_call" | custom-call | tf_op jit(solution)/shard_map/pallas_call | solution.py:339
  2.5 6.1 %collective-permute-start = (bf16[128,128]{1,0:T(8,128)(2,1)S(1)}, bf16[128,128]{1,0:T(8,128)(2,1)S(1)}, u32[]{:S(2)}, u32[]{:S(2)}) collective-permute-start(bf16[128,128]{1,0:T(8,128)(2,1)S(1)} %get-tuple-element.52), channel_id=1, source_target_pairs={{0,7},{1,2},{2,1},{3,4},{4,3},{5,6},{6,5},{7,0},{8,15},{9,10},{10,... | collective-permute-start | bytes 98312 | tf_op jit(solution)/shard_map/ppermute | solution.py:362
  8.6 2.7 %shard_map.138 = (bf16[2,256,4096]{2,1,0:T(8,128)(2,1)S(1)}, bf16[2,32,16,128]{3,2,1,0:T(8,128)(2,1)S(1)}, bf16[2,256,256]{2,1,0:T(8,128)(2,1)S(1)}, bf16[2,256,...) custom-call(s32[2]{0:T(128)S(1)} %pad_add_fusion.where_ref.me_ref, ...), custom_call_target="tpu_custom_call" | custom-call | flops 2000000000 | tf_op jit(solution)/shard_map/pallas_call | solution.py:339
  11.3 1.2 %collective-permute-done.1.hf_ref = bf16[128,128]{1,0:T(8,128)(2,1)S(1)} collective-permute-done((bf16[128,128]{1,0:T(8,128)(2,1)S(1)}, bf16[128,128]{1,0:T(8,128)(2,1)S(1)}, u32[]{:S(2)}, u32[]{:S(2)}) %collective-permute-start.1) | collective-permute-done | bytes 32800 | tf_op jit(solution)/shard_map/ppermute | solution.py:362
  12.5 3.7 %shard_map.139 = (bf16[256,256]{1,0:T(8,128)(2,1)S(1)}, bf16[128,128]{1,0:T(8,128)(2,1)S(1)}, bf16[128,128]{1,0:T(8,128)(2,1)S(1)}, bf16[256,128]{1,0:T(8,128)(2...) custom-call(bf16[128,128]{1,0:T(8,128)(2,1)S(1)} %collective-permute-done.hs_ref, ...), custom_call_target="tpu_custom_call" | custom-call | flops 4000000000 | tf_op jit(solution)/shard_map/pallas_call | solution.py:339
  16.3 2.8 %collective-permute-start.2 = (bf16[128,128]{1,0:T(8,128)(2,1)S(1)}, bf16[128,128]{1,0:T(8,128)(2,1)S(1)}, u32[]{:S(2)}, u32[]{:S(2)}) collective-permute-start(bf16[128,128]{1,0:T(8,128)(2,1)S(1)} %get-tuple-element.64), channel_id=1, source_target_pairs={{0,7},{1,2},{2,1},{3,4},{4,3},{5,6},{6,5},{7,0},{8,15},{9,10},{10,... | collective-permute-start | bytes 98312 | tf_op jit(solution)/shard_map/ppermute | solution.py:362
  20.0 3.1 %collective-permute-done.2.hs_ref = bf16[128,128]{1,0:T(8,128)(2,1)S(1)} collective-permute-done((bf16[128,128]{1,0:T(8,128)(2,1)S(1)}, bf16[128,128]{1,0:T(8,128)(2,1)S(1)}, u32[]{:S(2)}, u32[]{:S(2)}) %collective-permute-start.2) | collective-permute-done | bytes 32800 | tf_op jit(solution)/shard_map/ppermute | solution.py:362
  23.3 5.4 %shard_map.141 = (f32[2,128]{1,0:T(2,128)}, f32[16,256]{1,0:T(8,128)S(1)}, f32[256,256]{1,0:T(8,128)S(1)}, bf16[128,128]{1,0:T(8,128)(2,1)S(1)}, bf16[128,128]{1...) custom-call(bf16[128,128]{1,0:T(8,128)(2,1)S(1)} %collective-permute, ...), custom_call_target="tpu_custom_call" | custom-call | flops 6000000000 | tf_op jit(solution)/shard_map/pallas_call | solution.py:339
  28.7 2.4 %collective-permute-start.5 = (bf16[128,128]{1,0:T(8,128)(2,1)S(1)}, bf16[128,128]{1,0:T(8,128)(2,1)S(1)}, u32[]{:S(2)}, u32[]{:S(2)}) collective-permute-start(bf16[128,128]{1,0:T(8,128)(2,1)S(1)} %get-tuple-element.79), channel_id=1, source_target_pairs={{0,7},{1,2},{2,1},{3,4},{4,3},{5,6},{6,5},{7,0},{8,15},{9,10},{10,... | collective-permute-start | bytes 98312 | tf_op jit(solution)/shard_map/ppermute | solution.py:362
  31.1 0.9 %shard_map.142 = (f32[8,104,256]{2,1,0:T(8,128)S(1)}, f32[256,256]{1,0:T(8,128)S(1)}) custom-call(s32[2]{0:T(128)S(1)} %pad_add_fusion.where_ref.me_ref, bf16[256,256]{1,0:T(8,128)(2,1)S(1)} %get-tuple-element.66.state_ref, bf16[256,128]{1,0:T(8,128)(2,1)S(1)} %get-tuple-element.81.halo_ref, bf16[256,256]{1,0:T(8,128)(2,1)S(1)} %get-tuple-element.82.gathered_ref, ...), custom_call_target="tpu_custom_call" | custom-call | flops 100000000 | tf_op jit(solution)/shard_map/pallas_call | solution.py:339
  32.6 2.7 %collective-permute-done.5.bs_ref = bf16[128,128]{1,0:T(8,128)(2,1)S(1)} collective-permute-done((bf16[128,128]{1,0:T(8,128)(2,1)S(1)}, bf16[128,128]{1,0:T(8,128)(2,1)S(1)}, u32[]{:S(2)}, u32[]{:S(2)}) %collective-permute-start.5) | collective-permute-done | bytes 32800 | tf_op jit(solution)/shard_map/ppermute | solution.py:362
  35.3 2.8 %shard_map.143 = f32[8,96,256]{2,1,0:T(8,128)S(1)} custom-call(s32[2]{0:T(128)S(1)} %pad_add_fusion.where_ref.me_ref, bf16[128,128]{1,0:T(8,128)(2,1)S(1)} %collective-permute-done.4.bf_ref, bf16[128,128]{1,0:T(8,128)(2,1)S(1)} %collective-permute-done.5.bs_ref, bf16[256,128]{1,0:T(8,128)(2,1)S(1)} %get-tuple-element.63.select_ref, ...), custom_call_target="tpu_custom_call" | custom-call | flops 4000000000 | tf_op jit(solution)/shard_map/pallas_call | solution.py:339
  38.3 2.3 %collective-permute-done.6 = f32[4,200,256]{2,1,0:T(8,128)S(1)} collective-permute-done((f32[4,200,256]{2,1,0:T(8,128)S(1)}, f32[4,200,256]{2,1,0:T(8,128)S(1)}, u32[]{:S(2)}, u32[]{:S(2)}) %collective-permute-start.6) | collective-permute-done | bytes 819232 | tf_op jit(solution)/shard_map/ppermute | solution.py:366
  41.2 1.2 %collective-permute-start.9 = (f16[200,256]{1,0:T(8,128)(2,1)S(1)}, f16[200,256]{1,0:T(8,128)(2,1)S(1)}, u32[]{:S(2)}, u32[]{:S(2)}) collective-permute-start(f16[200,256]{1,0:T(8,128)(2,1)S(1)} %get-tuple-element.103), channel_id=1, source_target_pairs={{0,17},{1,16},{2,19},{3,18},{4,21},{5,20},{6,23},{7,22},{8,25},{9,... | collective-permute-start | bytes 307208 | tf_op jit(solution)/shard_map/ppermute | solution.py:401
  43.1 1.8 %collective-permute-start.7 = (f16[200,256]{1,0:T(8,128)(2,1)S(1)}, f16[200,256]{1,0:T(8,128)(2,1)S(1)}, u32[]{:S(2)}, u32[]{:S(2)}) collective-permute-start(f16[200,256]{1,0:T(8,128)(2,1)S(1)} %get-tuple-element.105), channel_id=1, source_target_pairs={{0,1},{1,0},{2,3},{3,2},{4,5},{5,4},{6,7},{7,6},{8,9},{9,8},{10,11... | collective-permute-start | bytes 307208 | tf_op jit(solution)/shard_map/ppermute | solution.py:401
  44.9 3.1 %collective-permute-done.9 = f16[200,256]{1,0:T(8,128)(2,1)S(1)} collective-permute-done((f16[200,256]{1,0:T(8,128)(2,1)S(1)}, f16[200,256]{1,0:T(8,128)(2,1)S(1)}, u32[]{:S(2)}, u32[]{:S(2)}) %collective-permute-start.9) | collective-permute-done | bytes 102432 | tf_op jit(solution)/shard_map/ppermute | solution.py:401
  48.2 1.1 %collective-permute-done.7 = f16[200,256]{1,0:T(8,128)(2,1)S(1)} collective-permute-done((f16[200,256]{1,0:T(8,128)(2,1)S(1)}, f16[200,256]{1,0:T(8,128)(2,1)S(1)}, u32[]{:S(2)}, u32[]{:S(2)}) %collective-permute-start.7) | collective-permute-done | bytes 102432 | tf_op jit(solution)/shard_map/ppermute | solution.py:401
  49.7 1.6 %collective-permute-start.11 = (bf16[200,256]{1,0:T(8,128)(2,1)S(1)}, bf16[200,256]{1,0:T(8,128)(2,1)S(1)}, u32[]{:S(2)}, u32[]{:S(2)}) collective-permute-start(bf16[200,256]{1,0:T(8,128)(2,1)S(1)} %fusion.3), channel_id=1, source_target_pairs={{0,6},{2,4},{4,2},{6,0},{1,7},{3,5},{5,3},{7,1},{8,14},{10,12},{12... | collective-permute-start | bytes 307208 | tf_op jit(solution)/shard_map/ppermute | solution.py:366
  51.3 1.9 %collective-permute-start.12 = (bf16[200,256]{1,0:T(8,128)(2,1)S(1)}, bf16[200,256]{1,0:T(8,128)(2,1)S(1)}, u32[]{:S(2)}, u32[]{:S(2)}) collective-permute-start(bf16[200,256]{1,0:T(8,128)(2,1)S(1)} %fusion.3), channel_id=1, source_target_pairs={{0,2},{2,0},{4,6},{6,4},{1,3},{3,1},{5,7},{7,5},{8,10},{10,8},{12,... | collective-permute-start | bytes 307208 | tf_op jit(solution)/shard_map/ppermute | solution.py:366
  53.1 5.4 %collective-permute-done.10 = bf16[200,256]{1,0:T(8,128)(2,1)S(1)} collective-permute-done((bf16[200,256]{1,0:T(8,128)(2,1)S(1)}, bf16[200,256]{1,0:T(8,128)(2,1)S(1)}, u32[]{:S(2)}, u32[]{:S(2)}) %collective-permute-start.10) | collective-permute-done | bytes 102432 | tf_op jit(solution)/shard_map/ppermute | solution.py:366
  58.5 1.4 %collective-permute-done.12 = bf16[200,256]{1,0:T(8,128)(2,1)S(1)} collective-permute-done((bf16[200,256]{1,0:T(8,128)(2,1)S(1)}, bf16[200,256]{1,0:T(8,128)(2,1)S(1)}, u32[]{:S(2)}, u32[]{:S(2)}) %collective-permute-start.12) | collective-permute-done | bytes 102432 | tf_op jit(solution)/shard_map/ppermute | solution.py:366
  60.0 2.2 %collective-permute-start.13 = (bf16[200,256]{1,0:T(8,128)(2,1)S(1)}, bf16[200,256]{1,0:T(8,128)(2,1)S(1)}, u32[]{:S(2)}, u32[]{:S(2)}) collective-permute-start(bf16[200,256]{1,0:T(8,128)(2,1)S(1)} %add_convert_fusion.refs_3_), channel_id=1, source_target_pairs={{0,17},{1,16},{2,19},{3,18},{4,21},{5,20},{6,23},{7,22},{8,25},{9,... | collective-permute-start | bytes 307208 | tf_op jit(solution)/shard_map/ppermute | solution.py:401
  63.5 2.9 %collective-permute-done.13.refs_0_ = bf16[200,256]{1,0:T(8,128)(2,1)S(1)} collective-permute-done((bf16[200,256]{1,0:T(8,128)(2,1)S(1)}, bf16[200,256]{1,0:T(8,128)(2,1)S(1)}, u32[]{:S(2)}, u32[]{:S(2)}) %collective-permute-start.13) | collective-permute-done | bytes 102432 | tf_op jit(solution)/shard_map/ppermute | solution.py:401
  68.9 1.8 %shard_map.144 = (f32[2,256,256]{2,1,0:T(8,128)}, f32[2,256,256]{2,1,0:T(8,128)}, f32[2,256,256]{2,1,0:T(8,128)}, f32[256]{0:T(256)}) custom-call(s32[2]{0:T(128)S(1)} %pad_add_fusion.where_ref.me_ref, bf16[200,256]{1,0:T(8,128)(2,1)S(1)} %collective-permute-done.13.refs_0_, bf16[200,256]{1,0:T(8,128)(2,1)S(1)} %collective-permute-done.14.refs_1_, ...), custom_call_target="tpu_custom_call" | custom-call | tf_op jit(solution)/shard_map/pallas_call | solution.py:339
  (62 shorter events, 7.6 us)
Async XLA Ops:
  2.5 8.8 %collective-permute-start = (bf16[128,128]{1,0:T(8,128)(2,1)S(1)}, bf16[128,128]{1,0:T(8,128)(2,1)S(1)}, u32[]{:S(2)}, u32[]{:S(2)}) collective-permute-start(bf16[128,128]{1,0:T(8,128)(2,1)S(1)} %get-tuple-element.52), channel_id=1, source_target_pairs={{0,7},{1,2},{2,1},{3,4},{4,3},{5,6},{6,5},{7,0},{8,15},{9,10},{10,... | collective-permute-start | bytes 98312 | tf_op jit(solution)/shard_map/ppermute | solution.py:362
  8.6 3.9 %collective-permute-start.1 = (bf16[128,128]{1,0:T(8,128)(2,1)S(1)}, bf16[128,128]{1,0:T(8,128)(2,1)S(1)}, u32[]{:S(2)}, u32[]{:S(2)}) collective-permute-start(bf16[128,128]{1,0:T(8,128)(2,1)S(1)} %get-tuple-element.53), channel_id=1, source_target_pairs={{0,1},{1,0},{2,3},{3,2},{4,5},{5,4},{6,7},{7,6},{8,9},{9,8},{10,11... | collective-permute-start | bytes 98312 | tf_op jit(solution)/shard_map/ppermute | solution.py:362
  12.5 6.5 %copy-start = (s32[2]{0:T(128)S(1)}, s32[2]{0:T(128)}, u32[]{:S(2)}) copy-start(s32[2]{0:T(128)} %param.15) | copy-start | bytes 28
  12.5 6.5 %copy-start.1 = (s32[2,1]{0,1:T(1,128)S(1)}, s32[2,1]{0,1:T(1,128)}, u32[]{:S(2)}) copy-start(s32[2,1]{0,1:T(1,128)} %param.14) | copy-start | bytes 28
  16.3 6.8 %collective-permute-start.2 = (bf16[128,128]{1,0:T(8,128)(2,1)S(1)}, bf16[128,128]{1,0:T(8,128)(2,1)S(1)}, u32[]{:S(2)}, u32[]{:S(2)}) collective-permute-start(bf16[128,128]{1,0:T(8,128)(2,1)S(1)} %get-tuple-element.64), channel_id=1, source_target_pairs={{0,7},{1,2},{2,1},{3,4},{4,3},{5,6},{6,5},{7,0},{8,15},{9,10},{10,... | collective-permute-start | bytes 98312 | tf_op jit(solution)/shard_map/ppermute | solution.py:362
  19.0 4.3 %collective-permute-start.3 = (bf16[128,128]{1,0:T(8,128)(2,1)S(1)}, bf16[128,128]{1,0:T(8,128)(2,1)S(1)}, u32[]{:S(2)}, u32[]{:S(2)}) collective-permute-start(bf16[128,128]{1,0:T(8,128)(2,1)S(1)} %get-tuple-element.65), channel_id=1, source_target_pairs={{0,1},{1,0},{2,3},{3,2},{4,5},{5,4},{6,7},{7,6},{8,9},{9,8},{10,11... | collective-permute-start | bytes 98312 | tf_op jit(solution)/shard_map/ppermute | solution.py:362
  28.7 3.9 %collective-permute-start.4 = (bf16[128,128]{1,0:T(8,128)(2,1)S(1)}, bf16[128,128]{1,0:T(8,128)(2,1)S(1)}, u32[]{:S(2)}, u32[]{:S(2)}) collective-permute-start(bf16[128,128]{1,0:T(8,128)(2,1)S(1)} %get-tuple-element.78), channel_id=1, source_target_pairs={{0,1},{1,0},{2,3},{3,2},{4,5},{5,4},{6,7},{7,6},{8,9},{9,8},{10,11... | collective-permute-start | bytes 98312 | tf_op jit(solution)/shard_map/ppermute | solution.py:362
  28.7 6.6 %collective-permute-start.5 = (bf16[128,128]{1,0:T(8,128)(2,1)S(1)}, bf16[128,128]{1,0:T(8,128)(2,1)S(1)}, u32[]{:S(2)}, u32[]{:S(2)}) collective-permute-start(bf16[128,128]{1,0:T(8,128)(2,1)S(1)} %get-tuple-element.79), channel_id=1, source_target_pairs={{0,7},{1,2},{2,1},{3,4},{4,3},{5,6},{6,5},{7,0},{8,15},{9,10},{10,... | collective-permute-start | bytes 98312 | tf_op jit(solution)/shard_map/ppermute | solution.py:362
  38.3 2.4 %collective-permute-start.6 = (f32[4,200,256]{2,1,0:T(8,128)S(1)}, f32[4,200,256]{2,1,0:T(8,128)S(1)}, u32[]{:S(2)}, u32[]{:S(2)}) collective-permute-start(f32[4,200,256]{2,1,0:T(8,128)S(1)} %pad_maximum_fusion), channel_id=1, source_target_pairs={{0,8},{8,0},{16,24},{24,16},{1,9},{9,1},{17,25},{25,17},{2,10},{10... | collective-permute-start | bytes 2457608 | tf_op jit(solution)/shard_map/ppermute | solution.py:366
  41.2 6.7 %collective-permute-start.9 = (f16[200,256]{1,0:T(8,128)(2,1)S(1)}, f16[200,256]{1,0:T(8,128)(2,1)S(1)}, u32[]{:S(2)}, u32[]{:S(2)}) collective-permute-start(f16[200,256]{1,0:T(8,128)(2,1)S(1)} %get-tuple-element.103), channel_id=1, source_target_pairs={{0,17},{1,16},{2,19},{3,18},{4,21},{5,20},{6,23},{7,22},{8,25},{9,... | collective-permute-start | bytes 307208 | tf_op jit(solution)/shard_map/ppermute | solution.py:401
  42.5 5.6 %collective-permute-start.8 = (f16[200,256]{1,0:T(8,128)(2,1)S(1)}, f16[200,256]{1,0:T(8,128)(2,1)S(1)}, u32[]{:S(2)}, u32[]{:S(2)}) collective-permute-start(f16[200,256]{1,0:T(8,128)(2,1)S(1)} %get-tuple-element.104), channel_id=1, source_target_pairs={{0,16},{1,17},{2,18},{3,19},{4,20},{5,21},{6,22},{7,23},{8,24},{9,... | collective-permute-start | bytes 307208 | tf_op jit(solution)/shard_map/ppermute | solution.py:401
  43.1 6.2 %collective-permute-start.7 = (f16[200,256]{1,0:T(8,128)(2,1)S(1)}, f16[200,256]{1,0:T(8,128)(2,1)S(1)}, u32[]{:S(2)}, u32[]{:S(2)}) collective-permute-start(f16[200,256]{1,0:T(8,128)(2,1)S(1)} %get-tuple-element.105), channel_id=1, source_target_pairs={{0,1},{1,0},{2,3},{3,2},{4,5},{5,4},{6,7},{7,6},{8,9},{9,8},{10,11... | collective-permute-start | bytes 307208 | tf_op jit(solution)/shard_map/ppermute | solution.py:401
  49.6 8.9 %collective-permute-start.10 = (bf16[200,256]{1,0:T(8,128)(2,1)S(1)}, bf16[200,256]{1,0:T(8,128)(2,1)S(1)}, u32[]{:S(2)}, u32[]{:S(2)}) collective-permute-start(bf16[200,256]{1,0:T(8,128)(2,1)S(1)} %fusion.3), channel_id=1, source_target_pairs={{0,4},{2,6},{4,0},{6,2},{1,5},{3,7},{5,1},{7,3},{8,12},{10,14},{12... | collective-permute-start | bytes 307208 | tf_op jit(solution)/shard_map/ppermute | solution.py:366
  49.7 8.8 %collective-permute-start.11 = (bf16[200,256]{1,0:T(8,128)(2,1)S(1)}, bf16[200,256]{1,0:T(8,128)(2,1)S(1)}, u32[]{:S(2)}, u32[]{:S(2)}) collective-permute-start(bf16[200,256]{1,0:T(8,128)(2,1)S(1)} %fusion.3), channel_id=1, source_target_pairs={{0,6},{2,4},{4,2},{6,0},{1,7},{3,5},{5,3},{7,1},{8,14},{10,12},{12... | collective-permute-start | bytes 307208 | tf_op jit(solution)/shard_map/ppermute | solution.py:366
  51.3 8.7 %collective-permute-start.12 = (bf16[200,256]{1,0:T(8,128)(2,1)S(1)}, bf16[200,256]{1,0:T(8,128)(2,1)S(1)}, u32[]{:S(2)}, u32[]{:S(2)}) collective-permute-start(bf16[200,256]{1,0:T(8,128)(2,1)S(1)} %fusion.3), channel_id=1, source_target_pairs={{0,2},{2,0},{4,6},{6,4},{1,3},{3,1},{5,7},{7,5},{8,10},{10,8},{12,... | collective-permute-start | bytes 307208 | tf_op jit(solution)/shard_map/ppermute | solution.py:366
  60.0 6.5 %collective-permute-start.13 = (bf16[200,256]{1,0:T(8,128)(2,1)S(1)}, bf16[200,256]{1,0:T(8,128)(2,1)S(1)}, u32[]{:S(2)}, u32[]{:S(2)}) collective-permute-start(bf16[200,256]{1,0:T(8,128)(2,1)S(1)} %add_convert_fusion.refs_3_), channel_id=1, source_target_pairs={{0,17},{1,16},{2,19},{3,18},{4,21},{5,20},{6,23},{7,22},{8,25},{9,... | collective-permute-start | bytes 307208 | tf_op jit(solution)/shard_map/ppermute | solution.py:401
  62.2 5.0 %collective-permute-start.14 = (bf16[200,256]{1,0:T(8,128)(2,1)S(1)}, bf16[200,256]{1,0:T(8,128)(2,1)S(1)}, u32[]{:S(2)}, u32[]{:S(2)}) collective-permute-start(bf16[200,256]{1,0:T(8,128)(2,1)S(1)} %add_convert_fusion.refs_3_), channel_id=1, source_target_pairs={{0,16},{1,17},{2,18},{3,19},{4,20},{5,21},{6,22},{7,23},{8,24},{9,... | collective-permute-start | bytes 307208 | tf_op jit(solution)/shard_map/ppermute | solution.py:401
  62.7 4.8 %collective-permute-start.15 = (bf16[200,256]{1,0:T(8,128)(2,1)S(1)}, bf16[200,256]{1,0:T(8,128)(2,1)S(1)}, u32[]{:S(2)}, u32[]{:S(2)}) collective-permute-start(bf16[200,256]{1,0:T(8,128)(2,1)S(1)} %add_convert_fusion.refs_3_), channel_id=1, source_target_pairs={{0,1},{1,0},{2,3},{3,2},{4,5},{5,4},{6,7},{7,6},{8,9},{9,8},{10,11... | collective-permute-start | bytes 307208 | tf_op jit(solution)/shard_map/ppermute | solution.py:401
  63.5 4.1 %collective-permute-start.19 = (bf16[200,256]{1,0:T(8,128)(2,1)S(1)}, bf16[200,256]{1,0:T(8,128)(2,1)S(1)}, u32[]{:S(2)}, u32[]{:S(2)}) collective-permute-start(bf16[200,256]{1,0:T(8,128)(2,1)S(1)} %add_convert_fusion.refs_3_), channel_id=1, source_target_pairs={{0,8},{8,0},{16,24},{24,16},{1,9},{9,1},{17,25},{25,17},{2,10},{10... | collective-permute-start | bytes 307208 | tf_op jit(solution)/shard_map/ppermute | solution.py:366
  66.5 1.3 %collective-permute-start.16 = (bf16[200,256]{1,0:T(8,128)(2,1)S(1)}, bf16[200,256]{1,0:T(8,128)(2,1)S(1)}, u32[]{:S(2)}, u32[]{:S(2)}) collective-permute-start(bf16[200,256]{1,0:T(8,128)(2,1)S(1)} %collective-permute-done.13.refs_0_), channel_id=1, source_target_pairs={{0,8},{8,0},{16,24},{24,16},{1,9},{9,1},{17,25},{25,17},{2,10},{10... | collective-permute-start | bytes 307208 | tf_op jit(solution)/shard_map/ppermute | solution.py:366
  67.2 1.3 %collective-permute-start.17 = (bf16[200,256]{1,0:T(8,128)(2,1)S(1)}, bf16[200,256]{1,0:T(8,128)(2,1)S(1)}, u32[]{:S(2)}, u32[]{:S(2)}) collective-permute-start(bf16[200,256]{1,0:T(8,128)(2,1)S(1)} %collective-permute-done.14.refs_1_), channel_id=1, source_target_pairs={{0,8},{8,0},{16,24},{24,16},{1,9},{9,1},{17,25},{25,17},{2,10},{10... | collective-permute-start | bytes 307208 | tf_op jit(solution)/shard_map/ppermute | solution.py:366
  67.5 1.3 %collective-permute-start.18 = (bf16[200,256]{1,0:T(8,128)(2,1)S(1)}, bf16[200,256]{1,0:T(8,128)(2,1)S(1)}, u32[]{:S(2)}, u32[]{:S(2)}) collective-permute-start(bf16[200,256]{1,0:T(8,128)(2,1)S(1)} %collective-permute-done.15.refs_2_), channel_id=1, source_target_pairs={{0,8},{8,0},{16,24},{24,16},{1,9},{9,1},{17,25},{25,17},{2,10},{10... | collective-permute-start | bytes 307208 | tf_op jit(solution)/shard_map/ppermute | solution.py:366

commit v7 on v6

--- a/solution.py
+++ b/solution.py
@@ -417,7 +417,7 @@
 def reduce_parts(parts):
     part = jnp.concatenate(parts, axis=1)
     sent = scaled(part[1:])
-    terms = [restored(plane(sent[0], 0, 1)), restored(plane(sent[1], 1, 0)), restored(plane(sent[2], 1, 1))]
+    terms = [restored(plane(sent[1], 1, 0)), restored(plane(sent[2], 1, 1)), restored(plane(sent[0], 0, 1))]
     mine = along_dom(summed(part[0], *terms))
     return [plane(mine, 1, 1), plane(mine, 1, 0), plane(mine, 0, 1), mine]
 

time: 70.8 us -> 70.1 us (level)
    ppermute x8, waiting for transfers between devices: 10.3 us -> 9.34 us  [partner(): lax.ppermute(value, axis, [(s, s ^ bits) for s in range(lax.axis_size(axi...]
  transfers between devices with their start and end apart: 20 -> 20, of which waited for: 17 -> 15; matrix products, arithmetic and copies ran while one was open for 0% -> 0% of each run, Pallas kernels for 6% -> 6%
where the time goes in v7:
time: 70.1 us; the launch traced here: 69.9 us
  waiting for transfers between devices  25.8 us (37%)
  starting transfers between devices  21.9 us (31%)
  Pallas kernels  20 us (29%)
  other arithmetic  0.97 us (1%)
  between operations  0.95 us (1%)
    pallas_call x8, Pallas kernels, kernel_call(): pl.pallas_call(body, out_shape=outs, in_specs=[pl.BlockSpec(memory_space=...  20 us
    ppermute x6, starting transfers between devices, swapped(): return lax.ppermute(value, RING, pairs)  11.2 us
    ppermute x8, waiting for transfers between devices, partner(): lax.ppermute(value, axis, [(s, s ^ bits) for s in range(lax.axis_size(axi...  9.34 us
    ppermute x6, waiting for transfers between devices, plane(): lax.ppermute(value, EVERY, [(s, s ^ flip) for s in range(rep * dom * tp)])  8.69 us
    ppermute x6, waiting for transfers between devices, swapped(): return lax.ppermute(value, RING, pairs)  7.81 us
    ppermute x6, starting transfers between devices, plane(): lax.ppermute(value, EVERY, [(s, s ^ flip) for s in range(rep * dom * tp)])  7.11 us
    ppermute x8, starting transfers between devices, partner(): lax.ppermute(value, axis, [(s, s ^ bits) for s in range(lax.axis_size(axi...  3.63 us
  transfers between devices with their start and end apart: 20, of which 15 were waited for; matrix products, arithmetic and copies ran while one was open for 0% of the time, Pallas kernels for 6%

profile of v7, /device:TPU:0, one launch (start us, length us, event | category | flops | bytes accessed | tf_op | source)
XLA Modules:
  0.0 69.9 jit_solution(18377208818277942805)
XLA Ops:
  0.7 1.8 %shard_map.137 = (bf16[256,256]{1,0:T(8,128)(2,1)S(1)}, bf16[256,128]{1,0:T(8,128)(2,1)S(1)}, bf16[128,128]{1,0:T(8,128)(2,1)S(1)}, bf16[128,128]{1,0:T(8,128)(2...) custom-call(s32[2]{0:T(128)S(1)} %pad_add_fusion.where_ref.me_ref, bf16[2,128,256]{2,1,0:T(8,128)(2,1)} %feat_hbm.1, ...), custom_call_target="tpu_custom_call" | custom-call | tf_op jit(solution)/shard_map/pallas_call | solution.py:339
  2.5 6.1 %collective-permute-start = (bf16[128,128]{1,0:T(8,128)(2,1)S(1)}, bf16[128,128]{1,0:T(8,128)(2,1)S(1)}, u32[]{:S(2)}, u32[]{:S(2)}) collective-permute-start(bf16[128,128]{1,0:T(8,128)(2,1)S(1)} %get-tuple-element.52), channel_id=1, source_target_pairs={{0,7},{1,2},{2,1},{3,4},{4,3},{5,6},{6,5},{7,0},{8,15},{9,10},{10,... | collective-permute-start | bytes 98312 | tf_op jit(solution)/shard_map/ppermute | solution.py:362
  8.6 2.7 %shard_map.138 = (bf16[2,256,4096]{2,1,0:T(8,128)(2,1)S(1)}, bf16[2,32,16,128]{3,2,1,0:T(8,128)(2,1)S(1)}, bf16[2,256,256]{2,1,0:T(8,128)(2,1)S(1)}, bf16[2,256,...) custom-call(s32[2]{0:T(128)S(1)} %pad_add_fusion.where_ref.me_ref, ...), custom_call_target="tpu_custom_call" | custom-call | flops 2000000000 | tf_op jit(solution)/shard_map/pallas_call | solution.py:339
  11.3 1.2 %collective-permute-done.1.hf_ref = bf16[128,128]{1,0:T(8,128)(2,1)S(1)} collective-permute-done((bf16[128,128]{1,0:T(8,128)(2,1)S(1)}, bf16[128,128]{1,0:T(8,128)(2,1)S(1)}, u32[]{:S(2)}, u32[]{:S(2)}) %collective-permute-start.1) | collective-permute-done | bytes 32800 | tf_op jit(solution)/shard_map/ppermute | solution.py:362
  12.5 3.7 %shard_map.139 = (bf16[256,256]{1,0:T(8,128)(2,1)S(1)}, bf16[128,128]{1,0:T(8,128)(2,1)S(1)}, bf16[128,128]{1,0:T(8,128)(2,1)S(1)}, bf16[256,128]{1,0:T(8,128)(2...) custom-call(bf16[128,128]{1,0:T(8,128)(2,1)S(1)} %collective-permute-done.hs_ref, ...), custom_call_target="tpu_custom_call" | custom-call | flops 4000000000 | tf_op jit(solution)/shard_map/pallas_call | solution.py:339
  16.3 2.8 %collective-permute-start.2 = (bf16[128,128]{1,0:T(8,128)(2,1)S(1)}, bf16[128,128]{1,0:T(8,128)(2,1)S(1)}, u32[]{:S(2)}, u32[]{:S(2)}) collective-permute-start(bf16[128,128]{1,0:T(8,128)(2,1)S(1)} %get-tuple-element.64), channel_id=1, source_target_pairs={{0,7},{1,2},{2,1},{3,4},{4,3},{5,6},{6,5},{7,0},{8,15},{9,10},{10,... | collective-permute-start | bytes 98312 | tf_op jit(solution)/shard_map/ppermute | solution.py:362
  19.1 0.8 %shard_map.140 = (bf16[256,256]{1,0:T(8,128)(2,1)S(1)}, bf16[256,256]{1,0:T(8,128)(2,1)S(1)}, bf16[256,256]{1,0:T(8,128)(2,1)S(1)}, f32[256,256]{1,0:T(8,128)S(1...) custom-call(s32[4]{0:T(128)S(1)} %pad_add_fusion.1.frame_ref, ...), custom_call_target="tpu_custom_call" | custom-call | flops 100000000 | tf_op jit(solution)/shard_map/pallas_call | solution.py:339
  20.0 3.1 %collective-permute-done.2.hs_ref = bf16[128,128]{1,0:T(8,128)(2,1)S(1)} collective-permute-done((bf16[128,128]{1,0:T(8,128)(2,1)S(1)}, bf16[128,128]{1,0:T(8,128)(2,1)S(1)}, u32[]{:S(2)}, u32[]{:S(2)}) %collective-permute-start.2) | collective-permute-done | bytes 32800 | tf_op jit(solution)/shard_map/ppermute | solution.py:362
  23.3 5.4 %shard_map.141 = (f32[2,128]{1,0:T(2,128)}, f32[16,256]{1,0:T(8,128)S(1)}, f32[256,256]{1,0:T(8,128)S(1)}, bf16[128,128]{1,0:T(8,128)(2,1)S(1)}, bf16[128,128]{1...) custom-call(bf16[128,128]{1,0:T(8,128)(2,1)S(1)} %collective-permute, ...), custom_call_target="tpu_custom_call" | custom-call | flops 6000000000 | tf_op jit(solution)/shard_map/pallas_call | solution.py:339
  28.7 2.4 %collective-permute-start.5 = (bf16[128,128]{1,0:T(8,128)(2,1)S(1)}, bf16[128,128]{1,0:T(8,128)(2,1)S(1)}, u32[]{:S(2)}, u32[]{:S(2)}) collective-permute-start(bf16[128,128]{1,0:T(8,128)(2,1)S(1)} %get-tuple-element.79), channel_id=1, source_target_pairs={{0,7},{1,2},{2,1},{3,4},{4,3},{5,6},{6,5},{7,0},{8,15},{9,10},{10,... | collective-permute-start | bytes 98312 | tf_op jit(solution)/shard_map/ppermute | solution.py:362
  31.1 0.9 %shard_map.142 = (f32[8,104,256]{2,1,0:T(8,128)S(1)}, f32[256,256]{1,0:T(8,128)S(1)}) custom-call(s32[2]{0:T(128)S(1)} %pad_add_fusion.where_ref.me_ref, bf16[256,256]{1,0:T(8,128)(2,1)S(1)} %get-tuple-element.66.state_ref, bf16[256,128]{1,0:T(8,128)(2,1)S(1)} %get-tuple-element.81.halo_ref, bf16[256,256]{1,0:T(8,128)(2,1)S(1)} %get-tuple-element.82.gathered_ref, ...), custom_call_target="tpu_custom_call" | custom-call | flops 100000000 | tf_op jit(solution)/shard_map/pallas_call | solution.py:339
  32.6 2.7 %collective-permute-done.5.bs_ref = bf16[128,128]{1,0:T(8,128)(2,1)S(1)} collective-permute-done((bf16[128,128]{1,0:T(8,128)(2,1)S(1)}, bf16[128,128]{1,0:T(8,128)(2,1)S(1)}, u32[]{:S(2)}, u32[]{:S(2)}) %collective-permute-start.5) | collective-permute-done | bytes 32800 | tf_op jit(solution)/shard_map/ppermute | solution.py:362
  35.3 2.8 %shard_map.143 = f32[8,96,256]{2,1,0:T(8,128)S(1)} custom-call(s32[2]{0:T(128)S(1)} %pad_add_fusion.where_ref.me_ref, bf16[128,128]{1,0:T(8,128)(2,1)S(1)} %collective-permute-done.4.bf_ref, bf16[128,128]{1,0:T(8,128)(2,1)S(1)} %collective-permute-done.5.bs_ref, bf16[256,128]{1,0:T(8,128)(2,1)S(1)} %get-tuple-element.63.select_ref, ...), custom_call_target="tpu_custom_call" | custom-call | flops 4000000000 | tf_op jit(solution)/shard_map/pallas_call | solution.py:339
  38.3 2.3 %collective-permute-done.6 = f32[4,200,256]{2,1,0:T(8,128)S(1)} collective-permute-done((f32[4,200,256]{2,1,0:T(8,128)S(1)}, f32[4,200,256]{2,1,0:T(8,128)S(1)}, u32[]{:S(2)}, u32[]{:S(2)}) %collective-permute-start.6) | collective-permute-done | bytes 819232 | tf_op jit(solution)/shard_map/ppermute | solution.py:366
  41.6 2.7 %collective-permute-start.8 = (f16[200,256]{1,0:T(8,128)(2,1)S(1)}, f16[200,256]{1,0:T(8,128)(2,1)S(1)}, u32[]{:S(2)}, u32[]{:S(2)}) collective-permute-start(f16[200,256]{1,0:T(8,128)(2,1)S(1)} %get-tuple-element.104), channel_id=1, source_target_pairs={{0,17},{1,16},{2,19},{3,18},{4,21},{5,20},{6,23},{7,22},{8,25},{9,... | collective-permute-start | bytes 307208 | tf_op jit(solution)/shard_map/ppermute | solution.py:401
  44.9 3.5 %collective-permute-done.9 = f16[200,256]{1,0:T(8,128)(2,1)S(1)} collective-permute-done((f16[200,256]{1,0:T(8,128)(2,1)S(1)}, f16[200,256]{1,0:T(8,128)(2,1)S(1)}, u32[]{:S(2)}, u32[]{:S(2)}) %collective-permute-start.9) | collective-permute-done | bytes 102432 | tf_op jit(solution)/shard_map/ppermute | solution.py:401
  48.5 1.1 %collective-permute-done.7 = f16[200,256]{1,0:T(8,128)(2,1)S(1)} collective-permute-done((f16[200,256]{1,0:T(8,128)(2,1)S(1)}, f16[200,256]{1,0:T(8,128)(2,1)S(1)}, u32[]{:S(2)}, u32[]{:S(2)}) %collective-permute-start.7) | collective-permute-done | bytes 102432 | tf_op jit(solution)/shard_map/ppermute | solution.py:401
  50.0 1.3 %collective-permute-start.11 = (bf16[200,256]{1,0:T(8,128)(2,1)S(1)}, bf16[200,256]{1,0:T(8,128)(2,1)S(1)}, u32[]{:S(2)}, u32[]{:S(2)}) collective-permute-start(bf16[200,256]{1,0:T(8,128)(2,1)S(1)} %fusion.3), channel_id=1, source_target_pairs={{0,6},{2,4},{4,2},{6,0},{1,7},{3,5},{5,3},{7,1},{8,14},{10,12},{12... | collective-permute-start | bytes 307208 | tf_op jit(solution)/shard_map/ppermute | solution.py:366
  51.4 2.2 %collective-permute-start.12 = (bf16[200,256]{1,0:T(8,128)(2,1)S(1)}, bf16[200,256]{1,0:T(8,128)(2,1)S(1)}, u32[]{:S(2)}, u32[]{:S(2)}) collective-permute-start(bf16[200,256]{1,0:T(8,128)(2,1)S(1)} %fusion.3), channel_id=1, source_target_pairs={{0,2},{2,0},{4,6},{6,4},{1,3},{3,1},{5,7},{7,5},{8,10},{10,8},{12,... | collective-permute-start | bytes 307208 | tf_op jit(solution)/shard_map/ppermute | solution.py:366
  53.5 4.9 %collective-permute-done.10 = bf16[200,256]{1,0:T(8,128)(2,1)S(1)} collective-permute-done((bf16[200,256]{1,0:T(8,128)(2,1)S(1)}, bf16[200,256]{1,0:T(8,128)(2,1)S(1)}, u32[]{:S(2)}, u32[]{:S(2)}) %collective-permute-start.10) | collective-permute-done | bytes 102432 | tf_op jit(solution)/shard_map/ppermute | solution.py:366
  59.3 2.1 %collective-permute-start.13 = (bf16[200,256]{1,0:T(8,128)(2,1)S(1)}, bf16[200,256]{1,0:T(8,128)(2,1)S(1)}, u32[]{:S(2)}, u32[]{:S(2)}) collective-permute-start(bf16[200,256]{1,0:T(8,128)(2,1)S(1)} %add_convert_fusion.refs_3_), channel_id=1, source_target_pairs={{0,17},{1,16},{2,19},{3,18},{4,21},{5,20},{6,23},{7,22},{8,25},{9,... | collective-permute-start | bytes 307208 | tf_op jit(solution)/shard_map/ppermute | solution.py:401
  62.8 2.2 %collective-permute-done.13.refs_0_ = bf16[200,256]{1,0:T(8,128)(2,1)S(1)} collective-permute-done((bf16[200,256]{1,0:T(8,128)(2,1)S(1)}, bf16[200,256]{1,0:T(8,128)(2,1)S(1)}, u32[]{:S(2)}, u32[]{:S(2)}) %collective-permute-start.13) | collective-permute-done | bytes 102432 | tf_op jit(solution)/shard_map/ppermute | solution.py:401
  65.0 1.0 %collective-permute-done.14.refs_1_ = bf16[200,256]{1,0:T(8,128)(2,1)S(1)} collective-permute-done((bf16[200,256]{1,0:T(8,128)(2,1)S(1)}, bf16[200,256]{1,0:T(8,128)(2,1)S(1)}, u32[]{:S(2)}, u32[]{:S(2)}) %collective-permute-start.14) | collective-permute-done | bytes 102432 | tf_op jit(solution)/shard_map/ppermute | solution.py:401
  68.2 1.8 %shard_map.144 = (f32[2,256,256]{2,1,0:T(8,128)}, f32[2,256,256]{2,1,0:T(8,128)}, f32[2,256,256]{2,1,0:T(8,128)}, f32[256]{0:T(256)}) custom-call(s32[2]{0:T(128)S(1)} %pad_add_fusion.where_ref.me_ref, bf16[200,256]{1,0:T(8,128)(2,1)S(1)} %collective-permute-done.13.refs_0_, bf16[200,256]{1,0:T(8,128)(2,1)S(1)} %collective-permute-done.14.refs_1_, ...), custom_call_target="tpu_custom_call" | custom-call | tf_op jit(solution)/shard_map/pallas_call | solution.py:339
  (62 shorter events, 7.4 us)
Async XLA Ops:
  2.5 8.8 %collective-permute-start = (bf16[128,128]{1,0:T(8,128)(2,1)S(1)}, bf16[128,128]{1,0:T(8,128)(2,1)S(1)}, u32[]{:S(2)}, u32[]{:S(2)}) collective-permute-start(bf16[128,128]{1,0:T(8,128)(2,1)S(1)} %get-tuple-element.52), channel_id=1, source_target_pairs={{0,7},{1,2},{2,1},{3,4},{4,3},{5,6},{6,5},{7,0},{8,15},{9,10},{10,... | collective-permute-start | bytes 98312 | tf_op jit(solution)/shard_map/ppermute | solution.py:362
  8.6 3.9 %collective-permute-start.1 = (bf16[128,128]{1,0:T(8,128)(2,1)S(1)}, bf16[128,128]{1,0:T(8,128)(2,1)S(1)}, u32[]{:S(2)}, u32[]{:S(2)}) collective-permute-start(bf16[128,128]{1,0:T(8,128)(2,1)S(1)} %get-tuple-element.53), channel_id=1, source_target_pairs={{0,1},{1,0},{2,3},{3,2},{4,5},{5,4},{6,7},{7,6},{8,9},{9,8},{10,11... | collective-permute-start | bytes 98312 | tf_op jit(solution)/shard_map/ppermute | solution.py:362
  12.5 6.5 %copy-start = (s32[2]{0:T(128)S(1)}, s32[2]{0:T(128)}, u32[]{:S(2)}) copy-start(s32[2]{0:T(128)} %param.15) | copy-start | bytes 28
  12.5 6.5 %copy-start.1 = (s32[2,1]{0,1:T(1,128)S(1)}, s32[2,1]{0,1:T(1,128)}, u32[]{:S(2)}) copy-start(s32[2,1]{0,1:T(1,128)} %param.14) | copy-start | bytes 28
  16.3 6.8 %collective-permute-start.2 = (bf16[128,128]{1,0:T(8,128)(2,1)S(1)}, bf16[128,128]{1,0:T(8,128)(2,1)S(1)}, u32[]{:S(2)}, u32[]{:S(2)}) collective-permute-start(bf16[128,128]{1,0:T(8,128)(2,1)S(1)} %get-tuple-element.64), channel_id=1, source_target_pairs={{0,7},{1,2},{2,1},{3,4},{4,3},{5,6},{6,5},{7,0},{8,15},{9,10},{10,... | collective-permute-start | bytes 98312 | tf_op jit(solution)/shard_map/ppermute | solution.py:362
  19.0 4.3 %collective-permute-start.3 = (bf16[128,128]{1,0:T(8,128)(2,1)S(1)}, bf16[128,128]{1,0:T(8,128)(2,1)S(1)}, u32[]{:S(2)}, u32[]{:S(2)}) collective-permute-start(bf16[128,128]{1,0:T(8,128)(2,1)S(1)} %get-tuple-element.65), channel_id=1, source_target_pairs={{0,1},{1,0},{2,3},{3,2},{4,5},{5,4},{6,7},{7,6},{8,9},{9,8},{10,11... | collective-permute-start | bytes 98312 | tf_op jit(solution)/shard_map/ppermute | solution.py:362
  28.7 3.9 %collective-permute-start.4 = (bf16[128,128]{1,0:T(8,128)(2,1)S(1)}, bf16[128,128]{1,0:T(8,128)(2,1)S(1)}, u32[]{:S(2)}, u32[]{:S(2)}) collective-permute-start(bf16[128,128]{1,0:T(8,128)(2,1)S(1)} %get-tuple-element.78), channel_id=1, source_target_pairs={{0,1},{1,0},{2,3},{3,2},{4,5},{5,4},{6,7},{7,6},{8,9},{9,8},{10,11... | collective-permute-start | bytes 98312 | tf_op jit(solution)/shard_map/ppermute | solution.py:362
  28.7 6.6 %collective-permute-start.5 = (bf16[128,128]{1,0:T(8,128)(2,1)S(1)}, bf16[128,128]{1,0:T(8,128)(2,1)S(1)}, u32[]{:S(2)}, u32[]{:S(2)}) collective-permute-start(bf16[128,128]{1,0:T(8,128)(2,1)S(1)} %get-tuple-element.79), channel_id=1, source_target_pairs={{0,7},{1,2},{2,1},{3,4},{4,3},{5,6},{6,5},{7,0},{8,15},{9,10},{10,... | collective-permute-start | bytes 98312 | tf_op jit(solution)/shard_map/ppermute | solution.py:362
  38.3 2.4 %collective-permute-start.6 = (f32[4,200,256]{2,1,0:T(8,128)S(1)}, f32[4,200,256]{2,1,0:T(8,128)S(1)}, u32[]{:S(2)}, u32[]{:S(2)}) collective-permute-start(f32[4,200,256]{2,1,0:T(8,128)S(1)} %pad_maximum_fusion), channel_id=1, source_target_pairs={{0,8},{8,0},{16,24},{24,16},{1,9},{9,1},{17,25},{25,17},{2,10},{10... | collective-permute-start | bytes 2457608 | tf_op jit(solution)/shard_map/ppermute | solution.py:366
  41.2 7.2 %collective-permute-start.9 = (f16[200,256]{1,0:T(8,128)(2,1)S(1)}, f16[200,256]{1,0:T(8,128)(2,1)S(1)}, u32[]{:S(2)}, u32[]{:S(2)}) collective-permute-start(f16[200,256]{1,0:T(8,128)(2,1)S(1)} %get-tuple-element.103), channel_id=1, source_target_pairs={{0,1},{1,0},{2,3},{3,2},{4,5},{5,4},{6,7},{7,6},{8,9},{9,8},{10,11... | collective-permute-start | bytes 307208 | tf_op jit(solution)/shard_map/ppermute | solution.py:401
  41.6 6.9 %collective-permute-start.8 = (f16[200,256]{1,0:T(8,128)(2,1)S(1)}, f16[200,256]{1,0:T(8,128)(2,1)S(1)}, u32[]{:S(2)}, u32[]{:S(2)}) collective-permute-start(f16[200,256]{1,0:T(8,128)(2,1)S(1)} %get-tuple-element.104), channel_id=1, source_target_pairs={{0,17},{1,16},{2,19},{3,18},{4,21},{5,20},{6,23},{7,22},{8,25},{9,... | collective-permute-start | bytes 307208 | tf_op jit(solution)/shard_map/ppermute | solution.py:401
  44.3 5.4 %collective-permute-start.7 = (f16[200,256]{1,0:T(8,128)(2,1)S(1)}, f16[200,256]{1,0:T(8,128)(2,1)S(1)}, u32[]{:S(2)}, u32[]{:S(2)}) collective-permute-start(f16[200,256]{1,0:T(8,128)(2,1)S(1)} %get-tuple-element.105), channel_id=1, source_target_pairs={{0,16},{1,17},{2,18},{3,19},{4,20},{5,21},{6,22},{7,23},{8,24},{9,... | collective-permute-start | bytes 307208 | tf_op jit(solution)/shard_map/ppermute | solution.py:401
  50.0 8.4 %collective-permute-start.10 = (bf16[200,256]{1,0:T(8,128)(2,1)S(1)}, bf16[200,256]{1,0:T(8,128)(2,1)S(1)}, u32[]{:S(2)}, u32[]{:S(2)}) collective-permute-start(bf16[200,256]{1,0:T(8,128)(2,1)S(1)} %fusion.3), channel_id=1, source_target_pairs={{0,4},{2,6},{4,0},{6,2},{1,5},{3,7},{5,1},{7,3},{8,12},{10,14},{12... | collective-permute-start | bytes 307208 | tf_op jit(solution)/shard_map/ppermute | solution.py:366
  50.0 8.4 %collective-permute-start.11 = (bf16[200,256]{1,0:T(8,128)(2,1)S(1)}, bf16[200,256]{1,0:T(8,128)(2,1)S(1)}, u32[]{:S(2)}, u32[]{:S(2)}) collective-permute-start(bf16[200,256]{1,0:T(8,128)(2,1)S(1)} %fusion.3), channel_id=1, source_target_pairs={{0,6},{2,4},{4,2},{6,0},{1,7},{3,5},{5,3},{7,1},{8,14},{10,12},{12... | collective-permute-start | bytes 307208 | tf_op jit(solution)/shard_map/ppermute | solution.py:366
  51.4 7.9 %collective-permute-start.12 = (bf16[200,256]{1,0:T(8,128)(2,1)S(1)}, bf16[200,256]{1,0:T(8,128)(2,1)S(1)}, u32[]{:S(2)}, u32[]{:S(2)}) collective-permute-start(bf16[200,256]{1,0:T(8,128)(2,1)S(1)} %fusion.3), channel_id=1, source_target_pairs={{0,2},{2,0},{4,6},{6,4},{1,3},{3,1},{5,7},{7,5},{8,10},{10,8},{12,... | collective-permute-start | bytes 307208 | tf_op jit(solution)/shard_map/ppermute | solution.py:366
  59.3 5.7 %collective-permute-start.13 = (bf16[200,256]{1,0:T(8,128)(2,1)S(1)}, bf16[200,256]{1,0:T(8,128)(2,1)S(1)}, u32[]{:S(2)}, u32[]{:S(2)}) collective-permute-start(bf16[200,256]{1,0:T(8,128)(2,1)S(1)} %add_convert_fusion.refs_3_), channel_id=1, source_target_pairs={{0,17},{1,16},{2,19},{3,18},{4,21},{5,20},{6,23},{7,22},{8,25},{9,... | collective-permute-start | bytes 307208 | tf_op jit(solution)/shard_map/ppermute | solution.py:401
  61.4 4.7 %collective-permute-start.14 = (bf16[200,256]{1,0:T(8,128)(2,1)S(1)}, bf16[200,256]{1,0:T(8,128)(2,1)S(1)}, u32[]{:S(2)}, u32[]{:S(2)}) collective-permute-start(bf16[200,256]{1,0:T(8,128)(2,1)S(1)} %add_convert_fusion.refs_3_), channel_id=1, source_target_pairs={{0,16},{1,17},{2,18},{3,19},{4,20},{5,21},{6,22},{7,23},{8,24},{9,... | collective-permute-start | bytes 307208 | tf_op jit(solution)/shard_map/ppermute | solution.py:401
  62.2 4.7 %collective-permute-start.15 = (bf16[200,256]{1,0:T(8,128)(2,1)S(1)}, bf16[200,256]{1,0:T(8,128)(2,1)S(1)}, u32[]{:S(2)}, u32[]{:S(2)}) collective-permute-start(bf16[200,256]{1,0:T(8,128)(2,1)S(1)} %add_convert_fusion.refs_3_), channel_id=1, source_target_pairs={{0,1},{1,0},{2,3},{3,2},{4,5},{5,4},{6,7},{7,6},{8,9},{9,8},{10,11... | collective-permute-start | bytes 307208 | tf_op jit(solution)/shard_map/ppermute | solution.py:401
  62.8 4.0 %collective-permute-start.19 = (bf16[200,256]{1,0:T(8,128)(2,1)S(1)}, bf16[200,256]{1,0:T(8,128)(2,1)S(1)}, u32[]{:S(2)}, u32[]{:S(2)}) collective-permute-start(bf16[200,256]{1,0:T(8,128)(2,1)S(1)} %add_convert_fusion.refs_3_), channel_id=1, source_target_pairs={{0,8},{8,0},{16,24},{24,16},{1,9},{9,1},{17,25},{25,17},{2,10},{10... | collective-permute-start | bytes 307208 | tf_op jit(solution)/shard_map/ppermute | solution.py:366
  65.0 1.8 %collective-permute-start.16 = (bf16[200,256]{1,0:T(8,128)(2,1)S(1)}, bf16[200,256]{1,0:T(8,128)(2,1)S(1)}, u32[]{:S(2)}, u32[]{:S(2)}) collective-permute-start(bf16[200,256]{1,0:T(8,128)(2,1)S(1)} %collective-permute-done.13.refs_0_), channel_id=1, source_target_pairs={{0,8},{8,0},{16,24},{24,16},{1,9},{9,1},{17,25},{25,17},{2,10},{10... | collective-permute-start | bytes 307208 | tf_op jit(solution)/shard_map/ppermute | solution.py:366
  66.1 1.3 %collective-permute-start.17 = (bf16[200,256]{1,0:T(8,128)(2,1)S(1)}, bf16[200,256]{1,0:T(8,128)(2,1)S(1)}, u32[]{:S(2)}, u32[]{:S(2)}) collective-permute-start(bf16[200,256]{1,0:T(8,128)(2,1)S(1)} %collective-permute-done.14.refs_1_), channel_id=1, source_target_pairs={{0,8},{8,0},{16,24},{24,16},{1,9},{9,1},{17,25},{25,17},{2,10},{10... | collective-permute-start | bytes 307208 | tf_op jit(solution)/shard_map/ppermute | solution.py:366
  66.8 1.3 %collective-permute-start.18 = (bf16[200,256]{1,0:T(8,128)(2,1)S(1)}, bf16[200,256]{1,0:T(8,128)(2,1)S(1)}, u32[]{:S(2)}, u32[]{:S(2)}) collective-permute-start(bf16[200,256]{1,0:T(8,128)(2,1)S(1)} %collective-permute-done.15.refs_2_), channel_id=1, source_target_pairs={{0,8},{8,0},{16,24},{24,16},{1,9},{9,1},{17,25},{25,17},{2,10},{10... | collective-permute-start | bytes 307208 | tf_op jit(solution)/shard_map/ppermute | solution.py:366
